TPU v7x, 32 devices: a whole 2x2x4 slice. The times are simulated.
32 devices in a mesh: gx: 4 (over x, core), gy: 4 (over z), gz: 2 (over y).
Axes of the slice: x: 2, y: 2, z: 4, core: 2. Of those that a mesh axis runs over, the one named last changes fastest.
Arguments:
- densities: bfloat16 [128, 32, 8, 448], P('gx', 'gy', 'gz'), may hold values from -6 to 6
- upward_weight: bfloat16 [448, 56], replicated, may hold values from -0.25 to 0.25
- transfer_weight: bfloat16 [316, 56, 56], replicated, may hold values from -0.0625 to 0.0625
- downward_weight: bfloat16 [56, 448], replicated, may hold values from -0.75 to 0.75
Outputs:
- leaf_locals: float32 [128, 32, 8, 448], P('gx', 'gy', 'gz')
All inputs are finite; a program needn't handle non-finite values.
Results may differ from a plain program's by a relative error of at most 0.0045.
Values may be sent and summed in bfloat16 or wider, within the bound.
No kernel may reach another device: no remote copies, remote signals or barrier semaphores. Data moves between devices by JAX's collectives and lax.ppermute only.
A program may use at most 128 MiB of HBM per device.

v0:
```python
import jax
import jax.numpy as jnp
from jax import lax
from jax.sharding import PartitionSpec as P


def with_halo(block, sides, width):
    for axis, dim in sides:
        count = lax.axis_size(axis)
        forward = [(i, i + 1) for i in range(count - 1)]
        backward = [(target, source) for source, target in forward]
        low = lax.ppermute(
            lax.slice_in_dim(block, block.shape[dim] - width, None, axis=dim), axis, forward
        )
        high = lax.ppermute(lax.slice_in_dim(block, 0, width, axis=dim), axis, backward)
        block = jnp.concatenate([low, block, high], axis=dim)
    return block


def kernel_table(transfer_weight):
    coeffs = transfer_weight.shape[1]
    empty = jnp.zeros((coeffs, coeffs), transfer_weight.dtype)
    blocks = []
    place = 0
    for first in range(-3, 4):
        for second in range(-3, 4):
            for third in range(-3, 4):
                if max(abs(first), abs(second), abs(third)) >= 2:
                    blocks.append(transfer_weight[place])
                    place = place + 1
                else:
                    blocks.append(empty)
    grid = jnp.stack(blocks).reshape(7, 7, 7, coeffs, coeffs)
    rows = []
    for source in range(8):
        columns = []
        for target in range(8):
            starts = [
                (source >> 2 - coord & 1) - (target >> 2 - coord & 1) + 1 for coord in range(3)
            ]
            piece = grid[
                starts[0] : starts[0] + 5 : 2,
                starts[1] : starts[1] + 5 : 2,
                starts[2] : starts[2] + 5 : 2,
            ]
            columns.append(piece.reshape(27, coeffs, coeffs))
        rows.append(jnp.concatenate(columns, axis=2))
    return jnp.concatenate(rows, axis=1)


def translate(padded, kernels, extent):
    size_x, size_y, size_z = extent
    group_width = padded.shape[3]
    row_count = size_x * size_y * size_z

    def one_offset(position, running):
        position = jnp.asarray(position).astype(jnp.int32)
        shift_x = position // 9
        shift_y = position // 3 % 3
        shift_z = position % 3
        source = lax.dynamic_slice(
            padded, (shift_x, shift_y, shift_z, shift_x * 0), (size_x, size_y, size_z, group_width)
        )
        kernel = lax.dynamic_index_in_dim(kernels, position, 0, keepdims=False)
        return running + jnp.dot(
            source.reshape(row_count, group_width), kernel, preferred_element_type=jnp.float32
        )

    running = lax.fori_loop(0, 27, one_offset, jnp.zeros((row_count, group_width), jnp.float32))
    return running.reshape(size_x, size_y, size_z, group_width)


def group_parents(boxes):
    size_x, size_y, size_z, coeffs = boxes.shape
    unpacked = boxes.reshape(size_x // 2, 2, size_y // 2, 2, size_z // 2, 2, coeffs)
    return unpacked.transpose(0, 2, 4, 1, 3, 5, 6).reshape(
        size_x // 2, size_y // 2, size_z // 2, 8 * coeffs
    )


def spread_children(grouped):
    size_x, size_y, size_z, group_width = grouped.shape
    coeffs = group_width // 8
    unpacked = grouped.reshape(size_x, size_y, size_z, 2, 2, 2, coeffs)
    return unpacked.transpose(0, 3, 1, 4, 2, 5, 6).reshape(
        2 * size_x, 2 * size_y, 2 * size_z, coeffs
    )


def lift(grouped, upward_weight):
    leading = grouped.shape[:3]
    product = jnp.dot(
        grouped.reshape(-1, grouped.shape[3]), upward_weight, preferred_element_type=jnp.float32
    )
    return product.astype(jnp.bfloat16).reshape(leading + (upward_weight.shape[1],))


def descend(boxes, downward_weight):
    leading = boxes.shape[:3]
    product = jnp.dot(
        boxes.astype(jnp.bfloat16).reshape(-1, boxes.shape[3]),
        downward_weight,
        preferred_element_type=jnp.float32,
    )
    return product.reshape(leading + (downward_weight.shape[1],))


def shards(densities, upward_weight, transfer_weight, downward_weight):
    kernels = kernel_table(transfer_weight)
    padded_leaf = with_halo(densities, (("gx", 0), ("gy", 1), ("gz", 2)), 1)
    far_leaf = translate(padded_leaf, kernels, densities.shape[:3])
    middle_group = group_parents(lift(densities, upward_weight))
    padded_middle = with_halo(middle_group, (("gx", 0), ("gy", 1), ("gz", 2)), 1)
    far_middle = translate(padded_middle, kernels, middle_group.shape[:3])
    coarse = lift(middle_group, upward_weight)
    haloed = with_halo(coarse, (("gx", 0), ("gy", 1), ("gz", 2)), 2)
    padded_top = group_parents(haloed)
    top_extent = (coarse.shape[0] // 2, coarse.shape[1] // 2, coarse.shape[2] // 2)
    far_top = translate(padded_top, kernels, top_extent)
    local_top = spread_children(far_top)
    local_middle = far_middle + descend(local_top, downward_weight)
    return far_leaf + descend(spread_children(local_middle), downward_weight)


def solution(mesh):
    placed = (P("gx", "gy", "gz", None), P(), P(), P())
    return jax.shard_map(
        shards, mesh=mesh, in_specs=placed, out_specs=P("gx", "gy", "gz", None), check_vma=False
    )
```

profile of v0, /device:TPU:30, one launch (start us, length us, event | category | flops | bytes accessed | tf_op | source)
XLA Modules:
  0.0 447.6 jit_solution(7567597201501394892)
XLA Ops:
  15.3 3.6 collective-permute-start.13
  30.5 20.6 %stack.4 = bf16[343,56,56]{0,2,1:T(8,128)(2,1)} concatenate(bf16[114,56,56]{0,2,1:T(8,128)(2,1)} %get-tuple-element.537, bf16[1,56,56]{0,2,1:T(8,128)(2,1)S(1)} %broadcast.6, bf16[2,56,56]{0,2,1:T(8,128)(2,1)S(1)} %broadcast.7, bf16[4,56,56]{0,2,1:T(8,128)(2,1)} %get-tuple-element.543, bf16[1,56,56]{0,2,1:T(8,128)(2,1)S(1)} %broadcast.6, bf16[2,56,56]{0,2,1:T(8,128)(2,1)S(1)} %broadcast.7, ...), dimensions={0} | concatenate | bytes 4302592 | tf_op jit(solution)/shard_map/stack | solution.py:33
  51.1 10.0 %copy.98 = bf16[343,56,56]{2,1,0:T(8,128)(2,1)} copy(bf16[343,56,56]{0,2,1:T(8,128)(2,1)} %stack.4) | data formatting | bytes 4302592 | tf_op jit(solution)/shard_map/stack | solution.py:33
  61.1 6.3 %fusion.12 = (bf16[3,3,3,56,56]{4,3,2,1,0:T(8,128)(2,1)}, bf16[3,3,3,56,56]{4,3,2,1,0:T(8,128)(2,1)}, bf16[3,3,3,56,56]{4,3,2,1,0:T(8,128)(2,1)}, bf16[3,3,3,56,...) fusion(bf16[7,7,7,56,56]{4,3,2,1,0:T(8,128)(2,1)} %bitcast.88), kind=kLoop, calls=%fused_computation.47 | loop fusion | bytes 6435072 | tf_op jit(solution)/shard_map/slice | solution.py:41
  68.8 4.9 %concatenate.64 = bf16[27,56,448]{2,1,0:T(8,128)(2,1)} concatenate(bf16[27,56,56]{2,1,0:T(8,128)(2,1)} %bitcast.155, bf16[27,56,56]{2,1,0:T(8,128)(2,1)} %bitcast.138, bf16[27,56,56]{2,1,0:T(8,128)(2,1)} %bitcast.136, bf16[27,56,56]{2,1,0:T(8,128)(2,1)S(1)} %bitcast.106, bf16[27,56,56]{2,1,0:T(8,128)(2,1)} %bitcast.130, bf16[27,56,56]{2,1,0:T(8,128)(2,1)S(1)} %bitcast.102, ...), dimensions={2} | concatenate | bytes 2709504 | tf_op jit(solution)/shard_map/concatenate | solution.py:47
  73.7 5.4 %concatenate.63 = bf16[27,56,448]{2,1,0:T(8,128)(2,1)} concatenate(bf16[27,56,56]{2,1,0:T(8,128)(2,1)} %bitcast.139, bf16[27,56,56]{2,1,0:T(8,128)(2,1)} %bitcast.154, bf16[27,56,56]{2,1,0:T(8,128)(2,1)S(1)} %bitcast.107, bf16[27,56,56]{2,1,0:T(8,128)(2,1)} %bitcast.134, bf16[27,56,56]{2,1,0:T(8,128)(2,1)S(1)} %bitcast.103, bf16[27,56,56]{2,1,0:T(8,128)(2,1)} %bitcast.128, ...), dimensions={2} | concatenate | bytes 2709504 | tf_op jit(solution)/shard_map/concatenate | solution.py:47
  79.1 5.3 %concatenate.62 = bf16[27,56,448]{2,1,0:T(8,128)(2,1)} concatenate(bf16[27,56,56]{2,1,0:T(8,128)(2,1)} %bitcast.137, bf16[27,56,56]{2,1,0:T(8,128)(2,1)S(1)} %bitcast.108, bf16[27,56,56]{2,1,0:T(8,128)(2,1)} %bitcast.153, bf16[27,56,56]{2,1,0:T(8,128)(2,1)} %bitcast.132, bf16[27,56,56]{2,1,0:T(8,128)(2,1)S(1)} %bitcast.99, bf16[27,56,56]{2,1,0:T(8,128)(2,1)S(1)} %bitcast.92, ...), dimensions={2} | concatenate | bytes 2709504 | tf_op jit(solution)/shard_map/concatenate | solution.py:47
  84.4 5.4 %concatenate.61 = bf16[27,56,448]{2,1,0:T(8,128)(2,1)} concatenate(bf16[27,56,56]{2,1,0:T(8,128)(2,1)S(1)} %bitcast.109, bf16[27,56,56]{2,1,0:T(8,128)(2,1)} %bitcast.135, bf16[27,56,56]{2,1,0:T(8,128)(2,1)} %bitcast.133, bf16[27,56,56]{2,1,0:T(8,128)(2,1)} %bitcast.152, bf16[27,56,56]{2,1,0:T(8,128)(2,1)S(1)} %bitcast.93, bf16[27,56,56]{2,1,0:T(8,128)(2,1)} %bitcast.119, ...), dimensions={2} | concatenate | bytes 2709504 | tf_op jit(solution)/shard_map/concatenate | solution.py:47
  89.8 5.5 %concatenate.60 = bf16[27,56,448]{2,1,0:T(8,128)(2,1)} concatenate(bf16[27,56,56]{2,1,0:T(8,128)(2,1)} %bitcast.131, bf16[27,56,56]{2,1,0:T(8,128)(2,1)S(1)} %bitcast.104, bf16[27,56,56]{2,1,0:T(8,128)(2,1)S(1)} %bitcast.100, bf16[27,56,56]{2,1,0:T(8,128)(2,1)S(1)} %bitcast.94, bf16[27,56,56]{2,1,0:T(8,128)(2,1)} %bitcast.151, bf16[27,56,56]{2,1,0:T(8,128)(2,1)} %bitcast.126, ...), dimensions={2} | concatenate | bytes 2709504 | tf_op jit(solution)/shard_map/concatenate | solution.py:47
  95.3 5.6 %concatenate.59 = bf16[27,56,448]{2,1,0:T(8,128)(2,1)} concatenate(bf16[27,56,56]{2,1,0:T(8,128)(2,1)S(1)} %bitcast.105, bf16[27,56,56]{2,1,0:T(8,128)(2,1)} %bitcast.129, bf16[27,56,56]{2,1,0:T(8,128)(2,1)S(1)} %bitcast.95, bf16[27,56,56]{2,1,0:T(8,128)(2,1)S(1)} %bitcast.120, bf16[27,56,56]{2,1,0:T(8,128)(2,1)} %bitcast.127, bf16[27,56,56]{2,1,0:T(8,128)(2,1)} %bitcast.150, ...), dimensions={2} | concatenate | bytes 2709504 | tf_op jit(solution)/shard_map/concatenate | solution.py:47
  100.9 5.6 %concatenate.58 = bf16[27,56,448]{2,1,0:T(8,128)(2,1)} concatenate(bf16[27,56,56]{2,1,0:T(8,128)(2,1)S(1)} %bitcast.101, bf16[27,56,56]{2,1,0:T(8,128)(2,1)S(1)} %bitcast.96, bf16[27,56,56]{2,1,0:T(8,128)(2,1)} %bitcast.125, bf16[27,56,56]{2,1,0:T(8,128)(2,1)S(1)} %bitcast.116, bf16[27,56,56]{2,1,0:T(8,128)(2,1)} %bitcast.123, bf16[27,56,56]{2,1,0:T(8,128)(2,1)S(1)} %bitcast.112, ...), dimensions={2} | concatenate | bytes 2709504 | tf_op jit(solution)/shard_map/concatenate | solution.py:47
  106.5 5.7 %concatenate.57 = bf16[27,56,448]{2,1,0:T(8,128)(2,1)} concatenate(bf16[27,56,56]{2,1,0:T(8,128)(2,1)S(1)} %bitcast.97, bf16[27,56,56]{2,1,0:T(8,128)(2,1)S(1)} %bitcast.121, bf16[27,56,56]{2,1,0:T(8,128)(2,1)S(1)} %bitcast.117, bf16[27,56,56]{2,1,0:T(8,128)(2,1)} %bitcast.145, bf16[27,56,56]{2,1,0:T(8,128)(2,1)S(1)} %bitcast.113, bf16[27,56,56]{2,1,0:T(8,128)(2,1)} %bitcast.143, ...), dimensions={2} | concatenate | bytes 2709504 | tf_op jit(solution)/shard_map/concatenate | solution.py:47
  118.8 4.4 copy-done.11
  123.8 3.6 collective-permute-start.1
  128.9 4.5 %collective-permute-start.15 = (bf16[20,2,2,56]{3,2,1,0:T(2,128)(2,1)S(1)}, bf16[20,2,2,56]{3,2,1,0:T(2,128)(2,1)S(1)}, u32[]{:S(2)}, u32[]{:S(2)}) collective-permute-start(bf16[20,2,2,56]{3,2,1,0:T(2,128)(2,1)S(1)} %get-tuple-element.559), channel_id=1, source_target_pairs={{2,0},{4,2},{6,4},{3,1},{5,3},{7,5},{10,8},{12,10},{14,12},{11,9},... | collective-permute-start | bytes 26888 | tf_op jit(solution)/shard_map/ppermute | solution.py:15
  135.6 4.5 %collective-permute-start.9 = (bf16[18,1,2,448]{3,0,2,1:T(8,128)(2,1)S(1)}, bf16[18,1,2,448]{3,0,2,1:T(8,128)(2,1)S(1)}, u32[]{:S(2)}, u32[]{:S(2)}) collective-permute-start(bf16[18,1,2,448]{3,0,2,1:T(8,128)(2,1)S(1)} %get-tuple-element.557), channel_id=1, source_target_pairs={{2,0},{4,2},{6,4},{3,1},{5,3},{7,5},{10,8},{12,10},{14,12},{11,9},... | collective-permute-start | bytes 96776 | tf_op jit(solution)/shard_map/ppermute | solution.py:15
  141.6 4.6 %collective-permute-start.17 = (bf16[20,8,2,56]{3,2,1,0:T(2,128)(2,1)S(1)}, bf16[20,8,2,56]{3,2,1,0:T(2,128)(2,1)S(1)}, u32[]{:S(2)}, u32[]{:S(2)}) collective-permute-start(bf16[20,8,2,56]{3,2,1,0:T(2,128)(2,1)S(1)} %pad_maximum_fusion.12), channel_id=1, source_target_pairs={{1,0},{3,2},{5,4},{7,6},{9,8},{11,10},{13,12},{15,14},{17,16},{19,... | collective-permute-start | bytes 107528 | tf_op jit(solution)/shard_map/ppermute | solution.py:15
  148.3 4.7 %collective-permute-start.3 = (bf16[34,1,4,448]{3,0,2,1:T(8,128)(2,1)S(1)}, bf16[34,1,4,448]{3,0,2,1:T(8,128)(2,1)S(1)}, u32[]{:S(2)}, u32[]{:S(2)}) collective-permute-start(bf16[34,1,4,448]{3,0,2,1:T(8,128)(2,1)S(1)} %get-tuple-element.549), channel_id=1, source_target_pairs={{2,0},{4,2},{6,4},{3,1},{5,3},{7,5},{10,8},{12,10},{14,12},{11,9},... | collective-permute-start | bytes 365576 | tf_op jit(solution)/shard_map/ppermute | solution.py:15
  154.5 4.6 %collective-permute-start.11 = (bf16[18,6,1,448]{3,0,2,1:T(8,128)(2,1)S(1)}, bf16[18,6,1,448]{3,0,2,1:T(8,128)(2,1)S(1)}, u32[]{:S(2)}, u32[]{:S(2)}) collective-permute-start(bf16[18,6,1,448]{3,0,2,1:T(8,128)(2,1)S(1)} %get-tuple-element.553), channel_id=1, source_target_pairs={{1,0},{3,2},{5,4},{7,6},{9,8},{11,10},{13,12},{15,14},{17,16},{19,... | collective-permute-start | bytes 290312 | tf_op jit(solution)/shard_map/ppermute | solution.py:15
  160.0 34.1 %while.53 = (s32[]{:T(128)}, f32[16,448]{1,0:T(8,128)S(1)}, bf16[10,4,3,448]{3,1,0,2:T(4,128)(2,1)S(1)}, bf16[27,448,448]{2,1,0:T(8,128)(2,1)}, s32[]{:T(128)}, ...) while((s32[]{:T(128)}, f32[16,448]{1,0:T(8,128)S(1)}, ...), condition=%wide.region_5.6_spmd.clone, body=%wide.region_4.5_spmd.clone.sunk | while | flops 6436900 | bytes 588755 | solution.py:69
  197.6 5.3 %collective-permute-start.5 = (bf16[34,10,1,448]{3,0,2,1:T(8,128)(2,1)}, bf16[34,10,1,448]{3,0,2,1:T(8,128)(2,1)}, u32[]{:S(2)}, u32[]{:S(2)}) collective-permute-start(bf16[34,10,1,448]{3,0,2,1:T(8,128)(2,1)} %get-tuple-element.547), channel_id=1, source_target_pairs={{1,0},{3,2},{5,4},{7,6},{9,8},{11,10},{13,12},{15,14},{17,16},{19,... | collective-permute-start | bytes 913928 | tf_op jit(solution)/shard_map/ppermute | solution.py:15
  203.0 48.8 %while.52 = (s32[]{:T(128)}, f32[128,448]{0,1:T(8,128)S(1)}, bf16[18,6,4,448]{3,0,2,1:T(8,128)(2,1)S(1)}, bf16[27,448,448]{2,1,0:T(8,128)(2,1)}, s32[]{:T(128)},...) while((s32[]{:T(128)}, f32[128,448]{0,1:T(8,128)S(1)}, ...), condition=%wide.region_3.4_spmd.clone, body=%wide.region_2.3_spmd.clone.sunk | while | flops 51494948 | bytes 1721307 | solution.py:69
  255.8 183.1 %while.51 = (s32[]{:T(128)}, f32[1024,448]{0,1:T(8,128)}, bf16[34,10,6,448]{3,0,2,1:T(8,128)(2,1)}, bf16[27,448,448]{2,1,0:T(8,128)(2,1)}, s32[]{:T(128)}, /*ind...) while((s32[]{:T(128)}, f32[1024,448]{0,1:T(8,128)}, ...), condition=%wide.region_1.2_spmd.clone, body=%wide.region_0.1_spmd.clone.sunk | while | flops 411959328 | bytes 10552283 | solution.py:69
  265.2 3.6 select_add_fusion.2
  272.0 3.6 select_add_fusion.2
  278.8 3.6 select_add_fusion.2
  285.6 3.6 select_add_fusion.2
  292.4 3.6 select_add_fusion.2
  299.3 3.6 select_add_fusion.2
  306.1 3.6 select_add_fusion.2
  312.9 3.6 select_add_fusion.2
  319.7 3.6 select_add_fusion.2
  326.5 3.6 select_add_fusion.2
  333.3 3.6 select_add_fusion.2
  340.1 3.6 select_add_fusion.2
  346.9 3.6 select_add_fusion.2
  353.7 3.6 select_add_fusion.2
  360.5 3.6 select_add_fusion.2
  367.3 3.6 select_add_fusion.2
  374.1 3.6 select_add_fusion.2
  380.9 3.6 select_add_fusion.2
  387.7 3.6 select_add_fusion.2
  394.5 3.6 select_add_fusion.2
  401.3 3.6 select_add_fusion.2
  408.1 3.6 select_add_fusion.2
  414.9 3.6 select_add_fusion.2
  421.7 3.6 select_add_fusion.2
  435.3 3.6 select_add_fusion.2
  (394 shorter events, 232.9 us)
Async XLA Ops:
  0.0 252.1 %copy-start = (bf16[56,448]{1,0:T(8,128)(2,1)S(1)}, bf16[56,448]{1,0:T(8,128)(2,1)}, u32[]{:S(2)}) copy-start(bf16[56,448]{1,0:T(8,128)(2,1)} %param.13) | copy-start | bytes 150532
  1.6 21.8 %copy-start.2 = (bf16[316,56,56]{0,2,1:T(8,128)(2,1)S(1)}, bf16[316,56,56]{0,2,1:T(8,128)(2,1)}, u32[]{:S(2)}) copy-start(bf16[316,56,56]{0,2,1:T(8,128)(2,1)} %param.12) | copy-start | bytes 5945860
  4.8 10.5 %copy-start.13 = (bf16[1024,56]{1,0:T(8,128)(2,1)}, bf16[1024,56]{1,0:T(8,128)(2,1)S(1)}, u32[]{:S(2)}) copy-start(bf16[1024,56]{1,0:T(8,128)(2,1)S(1)} %copy.101) | copy-start | bytes 344068
  5.5 128.7 %collective-permute-start.7 = (bf16[1,4,2,448]{3,0,2,1:T(2,128)(2,1)}, bf16[1,4,2,448]{3,0,2,1:T(2,128)(2,1)S(1)}, u32[]{:S(2)}, u32[]{:S(2)}) collective-permute-start(bf16[1,4,2,448]{3,0,2,1:T(2,128)(2,1)} %slice.185), channel_id=1, source_target_pairs={{8,0},{16,8},{24,16},{9,1},{17,9},{25,17},{10,2},{18,10},{26,18},{... | collective-permute-start | bytes 21512 | tf_op jit(solution)/shard_map/ppermute | solution.py:15
  8.1 120.8 %collective-permute-start.6 = (bf16[1,4,2,448]{3,2,1,0:T(2,128)(2,1)}, bf16[1,4,2,448]{3,2,1,0:T(2,128)(2,1)}, u32[]{:S(2)}, u32[]{:S(2)}) collective-permute-start(bf16[1,4,2,448]{3,2,1,0:T(2,128)(2,1)} %slice.172), channel_id=1, source_target_pairs={{0,8},{8,16},{16,24},{1,9},{9,17},{17,25},{2,10},{10,18},{18,26},{... | collective-permute-start | bytes 21512 | tf_op jit(solution)/shard_map/ppermute | solution.py:12
  12.7 111.1 %collective-permute-start.12 = (bf16[2,4,2,56]{3,2,1,0:T(2,128)(2,1)}, bf16[2,4,2,56]{3,2,1,0:T(2,128)(2,1)S(1)}, u32[]{:S(2)}, u32[]{:S(2)}) collective-permute-start(bf16[2,4,2,56]{3,2,1,0:T(2,128)(2,1)} %bitcast.31), channel_id=1, source_target_pairs={{0,8},{8,16},{16,24},{1,9},{9,17},{17,25},{2,10},{10,18},{18,26},{... | collective-permute-start | bytes 5384 | tf_op jit(solution)/shard_map/ppermute | solution.py:12
  15.3 112.2 %collective-permute-start.13 = (bf16[2,4,2,56]{3,2,1,0:T(2,128)(2,1)}, bf16[2,4,2,56]{3,2,1,0:T(2,128)(2,1)S(1)}, u32[]{:S(2)}, u32[]{:S(2)}) collective-permute-start(bf16[2,4,2,56]{3,2,1,0:T(2,128)(2,1)} %bitcast.33), channel_id=1, source_target_pairs={{8,0},{16,8},{24,16},{9,1},{17,9},{25,17},{10,2},{18,10},{26,18},{... | collective-permute-start | bytes 5384 | tf_op jit(solution)/shard_map/ppermute | solution.py:15
  21.5 120.1 %collective-permute-start = (bf16[1,8,4,448]{3,0,2,1:T(2,128)(2,1)}, bf16[1,8,4,448]{3,0,2,1:T(2,128)(2,1)}, u32[]{:S(2)}, u32[]{:S(2)}) collective-permute-start(bf16[1,8,4,448]{3,0,2,1:T(2,128)(2,1)} %get-tuple-element.550), channel_id=1, source_target_pairs={{0,8},{8,16},{16,24},{1,9},{9,17},{17,25},{2,10},{10,18},{18,26},{... | collective-permute-start | bytes 86024 | tf_op jit(solution)/shard_map/ppermute | solution.py:12
  61.1 6.3 %copy-start.1 = (bf16[343,56,56]{2,1,0:T(8,128)(2,1)S(1)}, bf16[343,56,56]{2,1,0:T(8,128)(2,1)}, u32[]{:S(2)}) copy-start(bf16[343,56,56]{2,1,0:T(8,128)(2,1)} %copy.98) | copy-start | bytes 6453892
  89.8 5.5 %copy-start.3 = (bf16[3,3,3,56,56]{4,3,2,1,0:T(8,128)(2,1)S(1)}, bf16[3,3,3,56,56]{4,3,2,1,0:T(8,128)(2,1)}, u32[]{:S(2)}) copy-start(bf16[3,3,3,56,56]{4,3,2,1,0:T(8,128)(2,1)} %get-tuple-element.534) | copy-start | bytes 508036
  100.9 5.6 %copy-start.12 = (bf16[3,3,3,56,56]{4,3,2,1,0:T(8,128)(2,1)S(1)}, bf16[3,3,3,56,56]{4,3,2,1,0:T(8,128)(2,1)}, u32[]{:S(2)}) copy-start(bf16[3,3,3,56,56]{4,3,2,1,0:T(8,128)(2,1)} %get-tuple-element.529) | copy-start | bytes 508036
  112.2 1.9 copy-start.10
  112.2 2.3 copy-start.9
  114.1 1.5 copy-start.8
  114.6 1.5 copy-start.7
  115.6 1.5 copy-start.6
  116.0 1.5 copy-start.5
  117.1 1.5 copy-start.4
  117.5 5.7 %copy-start.14 = (bf16[1024,56]{1,0:T(8,128)(2,1)S(1)}, bf16[1024,56]{1,0:T(8,128)(2,1)}, u32[]{:S(2)}) copy-start(bf16[1024,56]{1,0:T(8,128)(2,1)} %copy-done.13) | copy-start | bytes 344068
  118.6 5.2 %copy-start.15 = (bf16[1,8,4,448]{3,0,2,1:T(2,128)(2,1)S(1)}, bf16[1,8,4,448]{3,0,2,1:T(2,128)(2,1)}, u32[]{:S(2)}) copy-start(bf16[1,8,4,448]{3,0,2,1:T(2,128)(2,1)} %get-tuple-element.551) | copy-start | bytes 86020
  118.8 4.5 copy-start.11
  123.8 22.3 %collective-permute-start.1 = (bf16[1,8,4,448]{3,0,2,1:T(2,128)(2,1)S(1)}, bf16[1,8,4,448]{3,0,2,1:T(2,128)(2,1)S(1)}, u32[]{:S(2)}, u32[]{:S(2)}) collective-permute-start(bf16[1,8,4,448]{3,0,2,1:T(2,128)(2,1)S(1)} %copy-done.15), channel_id=1, source_target_pairs={{8,0},{16,8},{24,16},{9,1},{17,9},{25,17},{10,2},{18,10},{26,18},{... | collective-permute-start | bytes 86024 | tf_op jit(solution)/shard_map/ppermute | solution.py:15
  127.6 7.9 %collective-permute-start.14 = (bf16[20,2,2,56]{3,2,1,0:T(2,128)(2,1)S(1)}, bf16[20,2,2,56]{3,2,1,0:T(2,128)(2,1)S(1)}, u32[]{:S(2)}, u32[]{:S(2)}) collective-permute-start(bf16[20,2,2,56]{3,2,1,0:T(2,128)(2,1)S(1)} %get-tuple-element.558), channel_id=1, source_target_pairs={{0,2},{2,4},{4,6},{1,3},{3,5},{5,7},{8,10},{10,12},{12,14},{9,11},... | collective-permute-start | bytes 26888 | tf_op jit(solution)/shard_map/ppermute | solution.py:12
  128.9 11.2 %collective-permute-start.15 = (bf16[20,2,2,56]{3,2,1,0:T(2,128)(2,1)S(1)}, bf16[20,2,2,56]{3,2,1,0:T(2,128)(2,1)S(1)}, u32[]{:S(2)}, u32[]{:S(2)}) collective-permute-start(bf16[20,2,2,56]{3,2,1,0:T(2,128)(2,1)S(1)} %get-tuple-element.559), channel_id=1, source_target_pairs={{2,0},{4,2},{6,4},{3,1},{5,3},{7,5},{10,8},{12,10},{14,12},{11,9},... | collective-permute-start | bytes 26888 | tf_op jit(solution)/shard_map/ppermute | solution.py:15
  134.3 14.1 %collective-permute-start.8 = (bf16[18,1,2,448]{3,0,2,1:T(8,128)(2,1)S(1)}, bf16[18,1,2,448]{3,0,2,1:T(8,128)(2,1)S(1)}, u32[]{:S(2)}, u32[]{:S(2)}) collective-permute-start(bf16[18,1,2,448]{3,0,2,1:T(8,128)(2,1)S(1)} %get-tuple-element.556), channel_id=1, source_target_pairs={{0,2},{2,4},{4,6},{1,3},{3,5},{5,7},{8,10},{10,12},{12,14},{9,11},... | collective-permute-start | bytes 96776 | tf_op jit(solution)/shard_map/ppermute | solution.py:12
  135.6 17.5 %collective-permute-start.9 = (bf16[18,1,2,448]{3,0,2,1:T(8,128)(2,1)S(1)}, bf16[18,1,2,448]{3,0,2,1:T(8,128)(2,1)S(1)}, u32[]{:S(2)}, u32[]{:S(2)}) collective-permute-start(bf16[18,1,2,448]{3,0,2,1:T(8,128)(2,1)S(1)} %get-tuple-element.557), channel_id=1, source_target_pairs={{2,0},{4,2},{6,4},{3,1},{5,3},{7,5},{10,8},{12,10},{14,12},{11,9},... | collective-permute-start | bytes 96776 | tf_op jit(solution)/shard_map/ppermute | solution.py:15
  140.3 14.2 %collective-permute-start.16 = (bf16[20,8,2,56]{3,2,1,0:T(2,128)(2,1)S(1)}, bf16[20,8,2,56]{3,2,1,0:T(2,128)(2,1)S(1)}, u32[]{:S(2)}, u32[]{:S(2)}) collective-permute-start(bf16[20,8,2,56]{3,2,1,0:T(2,128)(2,1)S(1)} %pad_maximum_fusion.12), channel_id=1, source_target_pairs={{0,1},{2,3},{4,5},{6,7},{8,9},{10,11},{12,13},{14,15},{16,17},{18,... | collective-permute-start | bytes 107528 | tf_op jit(solution)/shard_map/ppermute | solution.py:12
  141.6 17.5 %collective-permute-start.17 = (bf16[20,8,2,56]{3,2,1,0:T(2,128)(2,1)S(1)}, bf16[20,8,2,56]{3,2,1,0:T(2,128)(2,1)S(1)}, u32[]{:S(2)}, u32[]{:S(2)}) collective-permute-start(bf16[20,8,2,56]{3,2,1,0:T(2,128)(2,1)S(1)} %pad_maximum_fusion.12), channel_id=1, source_target_pairs={{1,0},{3,2},{5,4},{7,6},{9,8},{11,10},{13,12},{15,14},{17,16},{19,... | collective-permute-start | bytes 107528 | tf_op jit(solution)/shard_map/ppermute | solution.py:15
  147.0 47.3 %collective-permute-start.2 = (bf16[34,1,4,448]{3,0,2,1:T(8,128)(2,1)S(1)}, bf16[34,1,4,448]{3,0,2,1:T(8,128)(2,1)S(1)}, u32[]{:S(2)}, u32[]{:S(2)}) collective-permute-start(bf16[34,1,4,448]{3,0,2,1:T(8,128)(2,1)S(1)} %get-tuple-element.548), channel_id=1, source_target_pairs={{0,2},{2,4},{4,6},{1,3},{3,5},{5,7},{8,10},{10,12},{12,14},{9,11},... | collective-permute-start | bytes 365576 | tf_op jit(solution)/shard_map/ppermute | solution.py:12
  148.3 46.0 %collective-permute-start.3 = (bf16[34,1,4,448]{3,0,2,1:T(8,128)(2,1)S(1)}, bf16[34,1,4,448]{3,0,2,1:T(8,128)(2,1)S(1)}, u32[]{:S(2)}, u32[]{:S(2)}) collective-permute-start(bf16[34,1,4,448]{3,0,2,1:T(8,128)(2,1)S(1)} %get-tuple-element.549), channel_id=1, source_target_pairs={{2,0},{4,2},{6,4},{3,1},{5,3},{7,5},{10,8},{12,10},{14,12},{11,9},... | collective-permute-start | bytes 365576 | tf_op jit(solution)/shard_map/ppermute | solution.py:15
  153.2 41.0 %collective-permute-start.10 = (bf16[18,6,1,448]{3,0,2,1:T(8,128)(2,1)S(1)}, bf16[18,6,1,448]{3,0,2,1:T(8,128)(2,1)S(1)}, u32[]{:S(2)}, u32[]{:S(2)}) collective-permute-start(bf16[18,6,1,448]{3,0,2,1:T(8,128)(2,1)S(1)} %get-tuple-element.552), channel_id=1, source_target_pairs={{0,1},{2,3},{4,5},{6,7},{8,9},{10,11},{12,13},{14,15},{16,17},{18,... | collective-permute-start | bytes 290312 | tf_op jit(solution)/shard_map/ppermute | solution.py:12
  154.5 39.7 %collective-permute-start.11 = (bf16[18,6,1,448]{3,0,2,1:T(8,128)(2,1)S(1)}, bf16[18,6,1,448]{3,0,2,1:T(8,128)(2,1)S(1)}, u32[]{:S(2)}, u32[]{:S(2)}) collective-permute-start(bf16[18,6,1,448]{3,0,2,1:T(8,128)(2,1)S(1)} %get-tuple-element.553), channel_id=1, source_target_pairs={{1,0},{3,2},{5,4},{7,6},{9,8},{11,10},{13,12},{15,14},{17,16},{19,... | collective-permute-start | bytes 290312 | tf_op jit(solution)/shard_map/ppermute | solution.py:15
  196.4 56.4 %collective-permute-start.4 = (bf16[34,10,1,448]{3,0,2,1:T(8,128)(2,1)}, bf16[34,10,1,448]{3,0,2,1:T(8,128)(2,1)S(1)}, u32[]{:S(2)}, u32[]{:S(2)}) collective-permute-start(bf16[34,10,1,448]{3,0,2,1:T(8,128)(2,1)} %get-tuple-element.546), channel_id=1, source_target_pairs={{0,1},{2,3},{4,5},{6,7},{8,9},{10,11},{12,13},{14,15},{16,17},{18,... | collective-permute-start | bytes 913928 | tf_op jit(solution)/shard_map/ppermute | solution.py:12
  197.6 55.1 %collective-permute-start.5 = (bf16[34,10,1,448]{3,0,2,1:T(8,128)(2,1)}, bf16[34,10,1,448]{3,0,2,1:T(8,128)(2,1)}, u32[]{:S(2)}, u32[]{:S(2)}) collective-permute-start(bf16[34,10,1,448]{3,0,2,1:T(8,128)(2,1)} %get-tuple-element.547), channel_id=1, source_target_pairs={{1,0},{3,2},{5,4},{7,6},{9,8},{11,10},{13,12},{15,14},{17,16},{19,... | collective-permute-start | bytes 913928 | tf_op jit(solution)/shard_map/ppermute | solution.py:15
where the time goes:
time: 456 us; the launch traced here: 448 us
  local copies, waits for them, and re-layouts  215 us (47%)
  matrix products  169 us (37%)
  starting transfers between devices  51.4 us (11%)
  other arithmetic  6.71 us (1%)
    dot_general x81, matrix products, one_offset(): jnp.dot(source.reshape(row_count, group_width), kernel, preferred_element...  165 us
    dynamic_slice x135, local copies, waits for them, and re-layouts, one_offset(): lax.dynamic_slice(padded, (shift_x, shift_y, shift_z, shift_x * 0), (size...  76.8 us
    concatenate x8, local copies, waits for them, and re-layouts, kernel_table(): rows.append(jnp.concatenate(columns, axis=2))  43.4 us
    ppermute x9, starting transfers between devices, with_halo(): lax.ppermute(lax.slice_in_dim(block, 0, width, axis=dim), axis, backward)  37.4 us
    another operation x2, local copies, waits for them, and re-layouts, kernel_table(): grid = jnp.stack(blocks).reshape(7, 7, 7, coeffs, coeffs)  30.6 us
    reshape x81, local copies, waits for them, and re-layouts, one_offset(): source.reshape(row_count, group_width)  19.3 us
    ppermute x9, starting transfers between devices, with_halo(): lax.ppermute(lax.slice_in_dim(block, block.shape[dim] - width, None, axis...  14 us
    unnamed x42, local copies, waits for them, and re-layouts  13.1 us
  transfers between devices with their start and end apart: 18, of which 0 were waited for; matrix products, arithmetic and copies ran while one was open for 41% of the time, Pallas kernels for 0%

commit v1 on v0

v1 whole, which is shorter than its diff:
```python
import functools

import jax
import jax.numpy as jnp
from jax import lax
from jax.experimental import pallas as pl
from jax.experimental.pallas import tpu as pltpu
from jax.sharding import PartitionSpec as P

BF = jnp.bfloat16
F32 = jnp.float32
WHOLE = pl.BlockSpec(memory_space=pltpu.VMEM)


def params(mib):
    return pltpu.CompilerParams(vmem_limit_bytes=mib * 2**20)


def exchange(low, high, axis):
    count = lax.axis_size(axis)
    odd = lax.axis_index(axis) % 2 == 1

    def swap(block, first):
        pairs = []
        for i in range(first, count - 1, 2):
            pairs += [(i, i + 1), (i + 1, i)]
        return lax.ppermute(block, axis, pairs)

    got = swap(jnp.where(odd, low, high), 0)
    if count > 2:
        other = swap(jnp.where(odd, high, low), 1)
    else:
        other = jnp.zeros_like(got)
    return jnp.where(odd, got, other), jnp.where(odd, other, got)


def lift_kernel(base, weight, middle, top):
    size_y, size_z, size_x, width = base.shape
    half, part = size_x // 2, size_x // 4
    coeffs = weight.shape[1]
    up = weight[...]

    def lift(rows):
        return jnp.dot(rows, up, preferred_element_type=F32).astype(BF).astype(F32)

    boxes = {}
    for y in range(size_y):
        for z in range(size_z):
            boxes[y, z] = lift(base[y, z])
    coarse = {}
    for y in range(size_y // 2):
        for z in range(size_z // 2):
            pieces = []
            for u in range(2):
                for v in range(2):
                    for w in range(2):
                        pieces.append(boxes[2 * y + v, 2 * z + w][u * half : (u + 1) * half])
            group = jnp.concatenate(pieces, axis=1).astype(BF)
            middle[y, z] = group
            coarse[y, z] = lift(group)
    for y in range(size_y // 4):
        for z in range(size_z // 4):
            pieces = []
            for u in range(2):
                for v in range(2):
                    for w in range(2):
                        pieces.append(coarse[2 * y + v, 2 * z + w][u * part : (u + 1) * part])
            group = jnp.concatenate(pieces, axis=1)
            top[y, z] = jnp.concatenate([group, jnp.zeros_like(group)], axis=0).astype(BF)


def lifted(base, upward_weight):
    size_y, size_z, size_x, width = base.shape
    return pl.pallas_call(
        lift_kernel,
        out_shape=(
            jax.ShapeDtypeStruct((size_y // 2, size_z // 2, size_x // 2, width), BF),
            jax.ShapeDtypeStruct((size_y // 4, size_z // 4, size_x // 2, width), BF),
        ),
        in_specs=[WHOLE, WHOLE],
        out_specs=(WHOLE, WHOLE),
        compiler_params=params(40),
        name="lift",
    )(base, upward_weight)


def table_kernel(weight, table):
    coeffs = weight.shape[1]

    def one(position, carry):
        first = position // 7
        second = position % 7
        mid_first = jnp.logical_and(first >= 2, first <= 4)
        mid = jnp.logical_and(mid_first, jnp.logical_and(second >= 2, second <= 4))
        skipped = 9 * jnp.clip(first - 2, 0, 3) + jnp.where(
            mid_first, 3 * jnp.clip(second - 2, 0, 3), 0
        )
        start = 7 * position - skipped
        blocks = []
        for third in range(7):
            if third in (2, 3, 4):
                place = jnp.where(mid, 0, start + third)
                block = weight[place].astype(F32)
                block = jnp.where(mid, jnp.zeros_like(block), block)
            else:
                place = start + third - jnp.where(mid, min(max(third - 2, 0), 3), 0)
                block = weight[place].astype(F32)
            blocks.append(block)
        for third in range(3):
            rows = [
                jnp.concatenate([blocks[2 * third + s + 1], blocks[2 * third + s]], axis=1)
                for s in range(2)
            ]
            table[first, second, third] = jnp.concatenate(rows, axis=0).astype(BF)
        return carry

    lax.fori_loop(0, 49, one, 0)


def tabled(transfer_weight):
    coeffs = transfer_weight.shape[1]
    return pl.pallas_call(
        table_kernel,
        out_shape=jax.ShapeDtypeStruct((7, 7, 3, 2 * coeffs, 2 * coeffs), BF),
        in_specs=[WHOLE],
        out_specs=WHOLE,
        compiler_params=params(40),
        name="table",
    )(transfer_weight)


def far_kernel(
    table, leaf, leaf_x, middle, middle_x, top, top_x, down, out,
    leaf_lo, leaf_hi, middle_lo, middle_hi, top_lo, top_hi, kernels, total,
):
    size_y, size_z = leaf.shape[0] - 2, leaf.shape[1] - 2
    size_x, width = leaf.shape[2:]
    half, part = size_x // 2, size_x // 4
    coeffs = width // 8
    pair = 2 * coeffs

    def after(rows, last):
        return jnp.concatenate([rows[1:], last], axis=0)

    def before(rows, first):
        return jnp.concatenate([first, rows[:-1]], axis=0)

    def move_leaf(position, carry):
        y, z = position // (size_z + 2), position % (size_z + 2)
        rows = leaf[y, z].astype(F32)
        low, high = leaf_x[0, pl.ds(position, 1)], leaf_x[1, pl.ds(position, 1)]
        q = [rows[i * part : (i + 1) * part] for i in range(4)]
        leaf_lo[y, z] = jnp.concatenate([before(q[3], low), q[2], q[0], q[1]], axis=0).astype(BF)
        leaf_hi[y, z] = jnp.concatenate([q[2], q[3], q[1], after(q[0], high)], axis=0).astype(BF)
        return carry

    lax.fori_loop(0, (size_y + 2) * (size_z + 2), move_leaf, 0)
    wide = middle.shape[1]
    for y in range(middle.shape[0]):
        for z in range(wide):
            rows = middle[y, z].astype(F32)
            at = y * wide + z
            low, high = middle_x[0, at : at + 1], middle_x[1, at : at + 1]
            q = [rows[:part], rows[part:]]
            middle_lo[y, z] = jnp.concatenate([before(q[1], low), q[0]], axis=0).astype(BF)
            middle_hi[y, z] = jnp.concatenate([q[1], after(q[0], high)], axis=0).astype(BF)
    wide = top.shape[1]
    for y in range(top.shape[0]):
        for z in range(wide):
            rows = top[y, z].astype(F32)[:part]
            at = y * wide + z
            low, high = top_x[0, at : at + 1], top_x[1, at : at + 1]
            none = jnp.zeros_like(rows)
            top_lo[y, z] = jnp.concatenate([before(rows, low), none], axis=0).astype(BF)
            top_hi[y, z] = jnp.concatenate([after(rows, high), none], axis=0).astype(BF)

    leaves = (leaf_lo, leaf, leaf_hi)
    middles = (middle_lo, middle, middle_hi)
    tops = (top_lo, top, top_hi)
    leaf_rows = size_y * size_z * size_x
    step = 2 * size_z * size_x
    slot = 0
    for dx in range(3):
        for dy in range(3):
            for dz in range(3):
                if (dx, dy, dz) == (1, 1, 1):
                    continue
                for sx in range(2):
                    for sy in range(2):
                        parts = [
                            table[2 * dx + sx - tx + 1, 2 * dy + sy - ty + 1, dz]
                            for tx in range(2)
                            for ty in range(2)
                        ]
                        at = (2 * sx + sy) * pair
                        kernels[slot, at : at + pair] = jnp.concatenate(parts, axis=1)
                kernel = kernels[slot]
                first = slot == 0

                def add(rows, at):
                    product = jnp.dot(rows, kernel, preferred_element_type=F32)
                    where = slice(at, at + rows.shape[0])
                    total[where] = product if first else total[where] + product

                for y in range(0, size_y, 2):
                    rows = leaves[dx][y + dy : y + dy + 2, dz : dz + size_z]
                    add(rows.reshape(step, width), y // 2 * step)
                rows = [
                    middles[dx][dy : dy + size_y // 2, dz : dz + size_z // 2].reshape(-1, width),
                    tops[dx][dy : dy + size_y // 4, dz : dz + size_z // 4].reshape(-1, width),
                ]
                add(jnp.concatenate(rows, axis=0), leaf_rows)
                slot += 1

    weight = down[...]

    def spread(values, rows):
        pieces = []
        for y in range(2 * values[0]):
            for z in range(2 * values[1]):
                for u in range(2):
                    octant = 4 * u + 2 * (y % 2) + z % 2
                    parent = values[2](y // 2, z // 2)
                    pieces.append(parent[:rows, octant * coeffs : (octant + 1) * coeffs])
        return jnp.concatenate(pieces, axis=0).astype(BF)

    middle_rows = leaf_rows // 8
    at_top = leaf_rows + middle_rows

    def top_of(y, z):
        at = at_top + (y * (size_z // 4) + z) * half
        return total[at : at + half]

    boxes = spread((size_y // 4, size_z // 4, top_of), part)
    local = total[leaf_rows:at_top] + jnp.dot(boxes, weight, preferred_element_type=F32)

    def middle_of(y, z):
        at = (y * (size_z // 2) + z) * half
        return local[at : at + half]

    boxes = spread((size_y // 2, size_z // 2, middle_of), half)
    out[...] = total[:leaf_rows] + jnp.dot(boxes, weight, preferred_element_type=F32)


def far(table, leaf, leaf_x, middle, middle_x, top, top_x, down):
    size_y, size_z = leaf.shape[0] - 2, leaf.shape[1] - 2
    size_x, width = leaf.shape[2:]
    rows = size_y * size_z * size_x
    more = rows // 8 + (size_y // 4) * (size_z // 4) * (size_x // 2)
    scratch = [pltpu.VMEM(a.shape, BF) for a in (leaf, leaf, middle, middle, top, top)]
    return pl.pallas_call(
        far_kernel,
        out_shape=jax.ShapeDtypeStruct((rows, width), F32),
        in_specs=[WHOLE] * 8,
        out_specs=WHOLE,
        scratch_shapes=scratch
        + [pltpu.VMEM((26, width, width), BF), pltpu.VMEM((rows + more, width), F32)],
        compiler_params=params(60),
        name="far",
    )(table, leaf, leaf_x, middle, middle_x, top, top_x, down)


def shards(densities, upward_weight, transfer_weight, downward_weight):
    size_x, size_y, size_z, width = densities.shape
    base = densities.reshape(size_x // 4, 2, 2, size_y, size_z, width)
    base = base.transpose(3, 4, 2, 1, 0, 5).reshape(size_y, size_z, size_x, width)
    middle, top = lifted(base, upward_weight)
    table = tabled(transfer_weight)
    levels = [base, middle, top]
    lasts = [size_x, size_x // 2, size_x // 4]

    def packed(pieces):
        return jnp.concatenate([piece.reshape(-1, width) for piece in pieces], axis=0)

    def unpacked(flat, shapes):
        pieces, at = [], 0
        for shape in shapes:
            count = shape[0] * shape[1] * (shape[2] if len(shape) > 2 else 1)
            pieces.append(flat[at : at + count].reshape(shape + (width,)))
            at += count
        return pieces

    low = packed([level[:, :, 0] for level in levels])
    high = packed([level[:, :, last - 1] for level, last in zip(levels, lasts)])
    shapes = [level.shape[:2] for level in levels]
    below, above = exchange(low, high, "gx")
    sides = [
        jnp.stack(both) for both in zip(unpacked(below, shapes), unpacked(above, shapes))
    ]

    def grown(arrays, dims, axis):
        def face(where):
            picked = []
            for array, dim in zip(arrays, dims):
                at = 0 if where == 0 else array.shape[dim] - 1
                picked.append(lax.slice_in_dim(array, at, at + 1, axis=dim))
            return picked

        shapes = [piece.shape[:-1] for piece in face(0)]
        rows = [piece.reshape(-1, width).shape[0] for piece in face(0)]
        below, above = exchange(packed(face(0)), packed(face(1)), axis)
        result, at = [], 0
        for array, dim, shape, count in zip(arrays, dims, shapes, rows):
            one = below[at : at + count].reshape(shape + (width,))
            two = above[at : at + count].reshape(shape + (width,))
            result.append(jnp.concatenate([one, array, two], axis=dim))
            at += count
        return result

    arrays = levels + sides
    arrays = grown(arrays, (1, 1, 1, 2, 2, 2), "gz")
    arrays = grown(arrays, (0, 0, 0, 1, 1, 1), "gy")
    levels, sides = arrays[:3], [side.reshape(2, -1, width).astype(F32) for side in arrays[3:]]
    result = far(
        table, levels[0], sides[0], levels[1], sides[1], levels[2], sides[2], downward_weight
    )
    result = result.reshape(size_y, size_z, 2, 2, size_x // 4, width)
    return result.transpose(4, 3, 2, 0, 1, 5).reshape(densities.shape)


def solution(mesh):
    placed = (P("gx", "gy", "gz", None), P(), P(), P())
    return jax.shard_map(
        shards, mesh=mesh, in_specs=placed, out_specs=P("gx", "gy", "gz", None), check_vma=False
    )
```

time: 456 us -> 81.7 us (0.18)
  the two profiles are of different devices: /device:TPU:30 before, /device:TPU:8 now
where the time goes in v1:
time: 81.7 us; the launch traced here: 81.3 us
  Pallas kernels  29.7 us (36%)
  local copies, waits for them, and re-layouts  25.5 us (31%)
  waiting for transfers between devices  11 us (13%)
  starting transfers between devices  10.3 us (13%)
  other arithmetic  3.83 us (5%)
  between operations  0.93 us (1%)
    pallas_call x1, Pallas kernels, far(): pl.pallas_call(far_kernel, out_shape=jax.ShapeDtypeStruct((rows, width),...  23.3 us
    unnamed x54, local copies, waits for them, and re-layouts  15.1 us
    ppermute x5, waiting for transfers between devices, swap(): return lax.ppermute(block, axis, pairs)  11 us
    ppermute x5, starting transfers between devices, swap(): return lax.ppermute(block, axis, pairs)  10.3 us
    pallas_call x1, Pallas kernels, tabled(): pl.pallas_call(table_kernel, out_shape=jax.ShapeDtypeStruct((7, 7, 3, 2 *...  5.3 us
    transpose x1, local copies, waits for them, and re-layouts, shards(): return result.transpose(4, 3, 2, 0, 1, 5).reshape(densities.shape)  4.26 us
    concatenate x6, other arithmetic, grown(): result.append(jnp.concatenate([one, array, two], axis=dim))  3.26 us
    convert_element_type x6, local copies, waits for them, and re-layouts, shards(): side.reshape(2, -1, width).astype(F32)  2.35 us
  transfers between devices with their start and end apart: 5, of which 2 were waited for; matrix products, arithmetic and copies ran while one was open for 12% of the time, Pallas kernels for 7%

profile of v1, /device:TPU:8, one launch (start us, length us, event | category | flops | bytes accessed | tf_op | source)
XLA Modules:
  0.0 81.3 jit_solution(11973015895387199216)
XLA Ops:
  0.0 1.8 %copy.19 = bf16[8,2,2,8,4,448]{5,0,1,2,4,3:T(8,128)(2,1)S(1)} copy(bf16[8,2,2,8,4,448]{5,4,3,2,1,0:T(4,128)(2,1)} %bitcast.80) | data formatting | bytes 1835008 | tf_op jit(solution)/shard_map/reshape | solution.py:265
  1.8 0.0 copy-done.12
  1.8 0.1 copy.20.weight
  2.0 0.3 slice_reduce_fusion.1
  2.3 1.1 %lift.1 = (bf16[4,2,16,448]{3,2,1,0:T(8,128)(2,1)S(1)}, bf16[2,1,16,448]{3,2,1,0:T(8,128)(2,1)S(1)}) custom-call(bf16[8,4,32,448]{3,2,1,0:T(8,128)(2,1)S(1)} %bitcast.70, bf16[448,56]{1,0:T(8,128)(2,1)S(1)} %copy.20.weight), custom_call_target="tpu_custom_call" | custom-call | tf_op jit(solution)/shard_map/lift/pallas_call | solution.py:74
  3.4 0.1 slice_reduce_fusion.3
  3.6 0.7 collective-permute-start.1
  4.3 2.9 %collective-permute-start = (bf16[42,448]{1,0:T(8,128)(2,1)S(1)}, bf16[42,448]{1,0:T(8,128)(2,1)S(1)}, u32[]{:S(2)}, u32[]{:S(2)}) collective-permute-start(bf16[42,448]{1,0:T(8,128)(2,1)S(1)} %get-tuple-element.36), channel_id=1, source_target_pairs={{0,8},{8,0},{16,24},{24,16},{1,9},{9,1},{17,25},{25,17},{2,10},{10... | collective-permute-start | bytes 112904 | tf_op jit(solution)/shard_map/ppermute | solution.py:27
  7.4 0.0 collective-permute-done.1
  7.4 0.7 collective-permute-done
  8.5 1.6 %collective-permute-start.2 = (bf16[380,448]{1,0:T(8,128)(2,1)S(1)}, bf16[380,448]{1,0:T(8,128)(2,1)S(1)}, u32[]{:S(2)}, u32[]{:S(2)}) collective-permute-start(bf16[380,448]{1,0:T(8,128)(2,1)S(1)} %broadcast_select_fusion.2), channel_id=1, source_target_pairs={{0,1},{1,0},{2,3},{3,2},{4,5},{5,4},{6,7},{7,6},{8,9},{9,8},{10,11... | collective-permute-start | bytes 1021448 | tf_op jit(solution)/shard_map/ppermute | solution.py:27
  10.1 10.3 %collective-permute-done.2 = bf16[380,448]{1,0:T(8,128)(2,1)S(1)} collective-permute-done((bf16[380,448]{1,0:T(8,128)(2,1)S(1)}, bf16[380,448]{1,0:T(8,128)(2,1)S(1)}, u32[]{:S(2)}, u32[]{:S(2)}) %collective-permute-start.2) | collective-permute-done | bytes 340512 | tf_op jit(solution)/shard_map/ppermute | solution.py:27
  20.4 0.1 broadcast_select_fusion.1
  20.6 0.0 copy-start.4
  20.6 0.0 copy-start.6
  20.8 0.0 copy-start.8
  21.1 0.1 slice_reduce_fusion.5
  21.2 0.4 copy-done.13
  21.7 0.0 copy-done.10
  21.7 0.1 pad_maximum_fusion.4
  21.7 0.0 copy-done.4
  21.7 0.0 copy-done.6
  21.8 0.3 concatenate.64
  22.1 0.3 concatenate.65
  22.4 0.1 broadcast_select_fusion.6
  22.5 0.5 collective-permute-start.3
  23.0 4.6 %collective-permute-start.4 = (bf16[330,448]{1,0:T(8,128)(2,1)S(1)}, bf16[330,448]{1,0:T(8,128)(2,1)S(1)}, u32[]{:S(2)}, u32[]{:S(2)}) collective-permute-start(bf16[330,448]{1,0:T(8,128)(2,1)S(1)} %get-tuple-element.22), channel_id=1, source_target_pairs={{2,4},{4,2},{3,5},{5,3},{10,12},{12,10},{11,13},{13,11},{18,20},{2... | collective-permute-start | bytes 887048 | tf_op jit(solution)/shard_map/ppermute | solution.py:27
  27.6 9.9 %copy.18.weight = bf16[316,56,56]{2,1,0:T(8,128)(2,1)} copy(bf16[316,56,56]{0,2,1:T(8,128)(2,1)} %param.6) | data formatting | bytes 3963904 | tf_op args[2]
  37.5 2.3 %copy-done = bf16[316,56,56]{2,1,0:T(8,128)(2,1)S(1)} copy-done((bf16[316,56,56]{2,1,0:T(8,128)(2,1)S(1)}, bf16[316,56,56]{2,1,0:T(8,128)(2,1)}, u32[]{:S(2)}) %copy-start) | copy-done | bytes 1981976
  39.8 5.3 %table.1 = bf16[7,7,3,112,112]{4,3,2,1,0:T(8,128)(2,1)S(1)} custom-call(bf16[316,56,56]{2,1,0:T(8,128)(2,1)S(1)} %copy-done), custom_call_target="tpu_custom_call" | custom-call | tf_op jit(solution)/shard_map/table/pallas_call | solution.py:122
  45.1 2.0 %copy-done.1 = bf16[7,7,3,112,112]{4,3,2,1,0:T(8,128)(2,1)} copy-done((bf16[7,7,3,112,112]{4,3,2,1,0:T(8,128)(2,1)}, bf16[7,7,3,112,112]{4,3,2,1,0:T(8,128)(2,1)S(1)}, u32[]{:S(2)}) %copy-start.1) | copy-done | bytes 3687960
  47.1 0.0 collective-permute-done.3
  47.1 0.0 collective-permute-done.4
  47.1 0.1 broadcast_select_fusion.4
  47.5 0.3 copy-done.5
  47.8 0.0 copy-done.7
  47.8 0.1 maximum_convert_fusion
  47.9 0.2 copy.33
  48.1 0.8 copy.40.leaf_x
  48.9 0.1 maximum_convert_fusion.1
  49.0 0.1 copy.36
  49.1 0.7 reshape.212.middle_x
  49.9 0.6 copy.41.top_x
  50.5 1.6 %pad_maximum_fusion.leaf = bf16[10,6,32,448]{3,2,1,0:T(8,128)(2,1)} fusion(bf16[1,6,32,448]{3,2,1,0:T(8,128)(2,1)S(1)} %bitcast.84, bf16[8,1,32,448]{3,2,1,0:T(8,128)(2,1)S(1)} %bitcast.77, bf16[8,4,32,448]{3,2,1,0:T(8,128)(2,1)S(1)} %bitcast.73, bf16[8,1,32,448]{3,2,1,0:T(8,128)(2,1)S(1)} %bitcast.79, bf16[1,6,32,448]{3,2,1,0:T(8,128)(2,1)S(1)} %bitcast.85), kind=kLoop, calls=%fused_computation | loop fusion | flops 3440640 | bytes 3440640 | tf_op jit(solution)/shard_map/concatenate | solution.py:306
  52.2 0.8 %pad_maximum_fusion.1.middle = bf16[6,4,16,448]{3,2,1,0:T(8,128)(2,1)} fusion(bf16[1,4,16,448]{3,2,1,0:T(8,128)(2,1)S(1)} %bitcast.96, bf16[4,1,16,448]{3,2,1,0:T(8,128)(2,1)S(1)} %bitcast.89, bf16[4,2,16,448]{3,2,1,0:T(8,128)(2,1)S(1)} %get-tuple-element.7, bf16[4,1,16,448]{3,2,1,0:T(8,128)(2,1)S(1)} %bitcast.91, bf16[1,4,16,448]{3,2,1,0:T(8,128)(2,1)S(1)} %bitcast.97), kind=kLoop, calls=%fused_computation.1 | loop fusion | flops 688128 | bytes 688128 | tf_op jit(solution)/shard_map/concatenate | solution.py:306
  53.0 0.7 pad_maximum_fusion.5.top
  53.7 23.3 %far.1 = f32[1024,448]{1,0:T(8,128)} custom-call(bf16[7,7,3,112,112]{4,3,2,1,0:T(8,128)(2,1)} %copy-done.1, bf16[10,6,32,448]{3,2,1,0:T(8,128)(2,1)} %pad_maximum_fusion.leaf, f32[2,60,448]{2,1,0:T(8,128)} %copy.40.leaf_x, bf16[6,4,16,448]{3,2,1,0:T(8,128)(2,1)} %pad_maximum_fusion.1.middle, f32[2,24,448]{2,1,0:T(8,128)} %reshape.212.middle_x, ...), custom_call_target="tpu_custom_call" | custom-call | tf_op jit(solution)/shard_map/far/pallas_call | solution.py:251
  77.1 4.3 %copy.42 = f32[8,2,2,8,4,448]{5,4,3,2,1,0:T(4,128)} copy(f32[8,2,2,8,4,448]{5,0,1,2,4,3:T(8,128)} %bitcast.75) | data formatting | bytes 3670016 | tf_op jit(solution)/shard_map/transpose | solution.py:318
  (125 shorter events, 1.4 us)
Async XLA Ops:
  0.0 1.8 %copy-start.12 = (bf16[448,56]{0,1:T(8,128)(2,1)S(1)}, bf16[448,56]{0,1:T(8,128)(2,1)}, u32[]{:S(2)}) copy-start(bf16[448,56]{0,1:T(8,128)(2,1)} %param.5) | copy-start | bytes 150532
  3.6 3.7 %collective-permute-start.1 = (bf16[42,448]{1,0:T(8,128)(2,1)S(1)}, bf16[42,448]{1,0:T(8,128)(2,1)S(1)}, u32[]{:S(2)}, u32[]{:S(2)}) collective-permute-start(bf16[42,448]{1,0:T(8,128)(2,1)S(1)} %get-tuple-element.35), channel_id=1, source_target_pairs={{8,16},{16,8},{9,17},{17,9},{10,18},{18,10},{11,19},{19,11},{12,20... | collective-permute-start | bytes 112904 | tf_op jit(solution)/shard_map/ppermute | solution.py:27
  4.3 3.8 %collective-permute-start = (bf16[42,448]{1,0:T(8,128)(2,1)S(1)}, bf16[42,448]{1,0:T(8,128)(2,1)S(1)}, u32[]{:S(2)}, u32[]{:S(2)}) collective-permute-start(bf16[42,448]{1,0:T(8,128)(2,1)S(1)} %get-tuple-element.36), channel_id=1, source_target_pairs={{0,8},{8,0},{16,24},{24,16},{1,9},{9,1},{17,25},{25,17},{2,10},{10... | collective-permute-start | bytes 112904 | tf_op jit(solution)/shard_map/ppermute | solution.py:27
  8.2 12.9 %copy-start.17 = (bf16[1,2,1,448]{3,1,2,0:T(2,128)(2,1)}, bf16[1,2,1,448]{3,1,2,0:T(2,128)(2,1)S(1)}, u32[]{:S(2)}) copy-start(bf16[1,2,1,448]{3,1,2,0:T(2,128)(2,1)S(1)} %slice_bitcast_fusion.4) | copy-start | bytes 5380
  8.2 12.9 %copy-start.19 = (bf16[1,2,1,448]{3,1,2,0:T(2,128)(2,1)}, bf16[1,2,1,448]{3,1,2,0:T(2,128)(2,1)S(1)}, u32[]{:S(2)}) copy-start(bf16[1,2,1,448]{3,1,2,0:T(2,128)(2,1)S(1)} %slice_bitcast_fusion.5) | copy-start | bytes 5380
  8.5 11.9 %collective-permute-start.2 = (bf16[380,448]{1,0:T(8,128)(2,1)S(1)}, bf16[380,448]{1,0:T(8,128)(2,1)S(1)}, u32[]{:S(2)}, u32[]{:S(2)}) collective-permute-start(bf16[380,448]{1,0:T(8,128)(2,1)S(1)} %broadcast_select_fusion.2), channel_id=1, source_target_pairs={{0,1},{1,0},{2,3},{3,2},{4,5},{5,4},{6,7},{7,6},{8,9},{9,8},{10,11... | collective-permute-start | bytes 1021448 | tf_op jit(solution)/shard_map/ppermute | solution.py:27
  20.6 1.5 %copy-start.2 = (bf16[32,448]{1,0:T(8,128)(2,1)}, bf16[32,448]{1,0:T(8,128)(2,1)S(1)}, u32[]{:S(2)}) copy-start(bf16[32,448]{1,0:T(8,128)(2,1)S(1)} %slice.242) | copy-start | bytes 86020
  20.6 1.1 %copy-start.4 = (bf16[2,8,1,448]{3,1,0,2:T(8,128)(2,1)}, bf16[2,8,1,448]{3,1,0,2:T(8,128)(2,1)S(1)}, u32[]{:S(2)}) copy-start(bf16[2,8,1,448]{3,1,0,2:T(8,128)(2,1)S(1)} %slice_bitcast_fusion) | copy-start | bytes 43012
  20.6 1.1 %copy-start.6 = (bf16[2,8,1,448]{3,1,0,2:T(8,128)(2,1)}, bf16[2,8,1,448]{3,1,0,2:T(8,128)(2,1)S(1)}, u32[]{:S(2)}) copy-start(bf16[2,8,1,448]{3,1,0,2:T(8,128)(2,1)S(1)} %slice_bitcast_fusion.1) | copy-start | bytes 43012
  20.8 1.3 %copy-start.8 = (bf16[2,4,1,448]{3,1,0,2:T(4,128)(2,1)}, bf16[2,4,1,448]{3,1,0,2:T(4,128)(2,1)S(1)}, u32[]{:S(2)}) copy-start(bf16[2,4,1,448]{3,1,0,2:T(4,128)(2,1)S(1)} %reshape.186) | copy-start | bytes 21508
  20.9 0.8 copy-start.10
  21.0 0.6 copy-start.13
  21.0 0.7 copy-start.15
  22.5 24.6 %collective-permute-start.3 = (bf16[330,448]{1,0:T(8,128)(2,1)S(1)}, bf16[330,448]{1,0:T(8,128)(2,1)S(1)}, u32[]{:S(2)}, u32[]{:S(2)}) collective-permute-start(bf16[330,448]{1,0:T(8,128)(2,1)S(1)} %get-tuple-element.21), channel_id=1, source_target_pairs={{0,2},{2,0},{4,6},{6,4},{1,3},{3,1},{5,7},{7,5},{8,10},{10,8},{12,... | collective-permute-start | bytes 887048 | tf_op jit(solution)/shard_map/ppermute | solution.py:27
  23.0 24.0 %collective-permute-start.4 = (bf16[330,448]{1,0:T(8,128)(2,1)S(1)}, bf16[330,448]{1,0:T(8,128)(2,1)S(1)}, u32[]{:S(2)}, u32[]{:S(2)}) collective-permute-start(bf16[330,448]{1,0:T(8,128)(2,1)S(1)} %get-tuple-element.22), channel_id=1, source_target_pairs={{2,4},{4,2},{3,5},{5,3},{10,12},{12,10},{11,13},{13,11},{18,20},{2... | collective-permute-start | bytes 887048 | tf_op jit(solution)/shard_map/ppermute | solution.py:27
  37.5 2.3 %copy-start = (bf16[316,56,56]{2,1,0:T(8,128)(2,1)S(1)}, bf16[316,56,56]{2,1,0:T(8,128)(2,1)}, u32[]{:S(2)}) copy-start(bf16[316,56,56]{2,1,0:T(8,128)(2,1)} %copy.18.weight) | copy-start | bytes 5945860
  45.1 2.0 %copy-start.1 = (bf16[7,7,3,112,112]{4,3,2,1,0:T(8,128)(2,1)}, bf16[7,7,3,112,112]{4,3,2,1,0:T(8,128)(2,1)S(1)}, u32[]{:S(2)}) copy-start(bf16[7,7,3,112,112]{4,3,2,1,0:T(8,128)(2,1)S(1)} %table.1) | copy-start | bytes 11063812
  47.0 0.7 copy-start.5
  47.0 0.7 copy-start.7
  47.1 1.8 %copy-start.9 = (bf16[2,4,1,448]{3,1,0,2:T(4,128)(2,1)S(1)}, bf16[2,4,1,448]{3,1,0,2:T(4,128)(2,1)}, u32[]{:S(2)}) copy-start(bf16[2,4,1,448]{3,1,0,2:T(4,128)(2,1)} %copy-done.8) | copy-start | bytes 21508
  47.1 1.8 %copy-start.11 = (bf16[2,4,1,448]{3,1,0,2:T(4,128)(2,1)S(1)}, bf16[2,4,1,448]{3,1,0,2:T(4,128)(2,1)}, u32[]{:S(2)}) copy-start(bf16[2,4,1,448]{3,1,0,2:T(4,128)(2,1)} %copy-done.10) | copy-start | bytes 21508
  47.1 2.6 %copy-start.14 = (bf16[2,2,1,448]{3,1,0,2:T(2,128)(2,1)S(1)}, bf16[2,2,1,448]{3,1,0,2:T(2,128)(2,1)}, u32[]{:S(2)}) copy-start(bf16[2,2,1,448]{3,1,0,2:T(2,128)(2,1)} %copy-done.13) | copy-start | bytes 10756
  47.1 2.6 %copy-start.16 = (bf16[2,2,1,448]{3,1,0,2:T(2,128)(2,1)S(1)}, bf16[2,2,1,448]{3,1,0,2:T(2,128)(2,1)}, u32[]{:S(2)}) copy-start(bf16[2,2,1,448]{3,1,0,2:T(2,128)(2,1)} %copy-done.15) | copy-start | bytes 10756
  47.2 2.6 %copy-start.18 = (bf16[1,2,1,448]{3,1,2,0:T(2,128)(2,1)S(1)}, bf16[1,2,1,448]{3,1,2,0:T(2,128)(2,1)}, u32[]{:S(2)}) copy-start(bf16[1,2,1,448]{3,1,2,0:T(2,128)(2,1)} %copy-done.17) | copy-start | bytes 5380
  47.2 2.6 %copy-start.20 = (bf16[1,2,1,448]{3,1,2,0:T(2,128)(2,1)S(1)}, bf16[1,2,1,448]{3,1,2,0:T(2,128)(2,1)}, u32[]{:S(2)}) copy-start(bf16[1,2,1,448]{3,1,2,0:T(2,128)(2,1)} %copy-done.19) | copy-start | bytes 5380
  50.5 2.5 %copy-start.3 = (bf16[32,448]{1,0:T(8,128)(2,1)S(1)}, bf16[32,448]{1,0:T(8,128)(2,1)}, u32[]{:S(2)}) copy-start(bf16[32,448]{1,0:T(8,128)(2,1)} %copy-done.2) | copy-start | bytes 86020

commit v2 on v1

v2 whole, which is shorter than its diff:
```python
import functools

import jax
import jax.numpy as jnp
from jax import lax
from jax.experimental import pallas as pl
from jax.experimental.pallas import tpu as pltpu
from jax.sharding import PartitionSpec as P

BF = jnp.bfloat16
F32 = jnp.float32
WHOLE = pl.BlockSpec(memory_space=pltpu.VMEM)


def params(mib):
    return pltpu.CompilerParams(vmem_limit_bytes=mib * 2**20)


def exchange(low, high, axis):
    count = lax.axis_size(axis)
    odd = lax.axis_index(axis) % 2 == 1

    def swap(block, first):
        pairs = []
        for i in range(first, count - 1, 2):
            pairs += [(i, i + 1), (i + 1, i)]
        return lax.ppermute(block, axis, pairs)

    got = swap(jnp.where(odd, low, high), 0)
    if count > 2:
        other = swap(jnp.where(odd, high, low), 1)
    else:
        other = jnp.zeros_like(got)
    return jnp.where(odd, got, other), jnp.where(odd, other, got)


def lift_kernel(base, weight, middle, top):
    size_y, size_z, size_x, width = base.shape
    half, part = size_x // 2, size_x // 4
    coeffs = weight.shape[1]
    up = weight[...]

    def lift(rows):
        return jnp.dot(rows, up, preferred_element_type=F32).astype(BF).astype(F32)

    boxes = {}
    for y in range(size_y):
        for z in range(size_z):
            boxes[y, z] = lift(base[y, z])
    coarse = {}
    for y in range(size_y // 2):
        for z in range(size_z // 2):
            pieces = []
            for u in range(2):
                for v in range(2):
                    for w in range(2):
                        pieces.append(boxes[2 * y + v, 2 * z + w][u * half : (u + 1) * half])
            group = jnp.concatenate(pieces, axis=1).astype(BF)
            middle[y, z] = group
            coarse[y, z] = lift(group)
    for y in range(size_y // 4):
        for z in range(size_z // 4):
            pieces = []
            for u in range(2):
                for v in range(2):
                    for w in range(2):
                        pieces.append(coarse[2 * y + v, 2 * z + w][u * part : (u + 1) * part])
            group = jnp.concatenate(pieces, axis=1)
            top[y, z] = jnp.concatenate([group, jnp.zeros_like(group)], axis=0).astype(BF)


def lifted(base, upward_weight):
    size_y, size_z, size_x, width = base.shape
    return pl.pallas_call(
        lift_kernel,
        out_shape=(
            jax.ShapeDtypeStruct((size_y // 2, size_z // 2, size_x // 2, width), BF),
            jax.ShapeDtypeStruct((size_y // 4, size_z // 4, size_x // 2, width), BF),
        ),
        in_specs=[WHOLE, WHOLE],
        out_specs=(WHOLE, WHOLE),
        compiler_params=params(40),
        name="lift",
    )(base, upward_weight)


def table_kernel(weight, table, blocks):
    coeffs, _, count = weight.shape
    lanes = 128

    def turn(source, carry):
        rows = weight[source].astype(F32)
        for at in range(0, count, lanes):
            part = rows[:, at : min(at + lanes, count)]
            if part.shape[1] < lanes:
                fill = jnp.zeros((coeffs, lanes - part.shape[1]), F32)
                part = jnp.concatenate([part, fill], axis=1)
            fill = jnp.zeros((lanes, lanes - coeffs), F32)
            turned = jnp.concatenate([part.T, fill], axis=1)
            blocks[pl.ds(at * coeffs + source, lanes, stride=coeffs), :] = turned
        return carry

    lax.fori_loop(0, coeffs, turn, 0, unroll=4)

    def one(position, carry):
        first = position // 7
        second = position % 7
        mid_first = jnp.logical_and(first >= 2, first <= 4)
        mid = jnp.logical_and(mid_first, jnp.logical_and(second >= 2, second <= 4))
        skipped = 9 * jnp.clip(first - 2, 0, 3) + jnp.where(
            mid_first, 3 * jnp.clip(second - 2, 0, 3), 0
        )
        start = 7 * position - skipped
        found = []
        for third in range(7):
            near = third in (2, 3, 4)
            if near:
                place = jnp.where(mid, 0, start + third)
            else:
                place = start + third - jnp.where(mid, min(max(third - 2, 0), 3), 0)
            block = blocks[pl.ds(pl.multiple_of(place * coeffs, 8), coeffs)]
            found.append(jnp.where(mid, 0.0, block) if near else block)
        moved = [pltpu.roll(block, coeffs, 1) for block in found[:6]]
        for third in range(3):
            rows = [found[2 * third + s + 1] + moved[2 * third + s] for s in range(2)]
            rows = jnp.concatenate(rows, axis=0)
            table[first, second, third] = rows[:, : 2 * coeffs].astype(BF)
        return carry

    lax.fori_loop(0, 49, one, 0, unroll=7)


def tabled(transfer_weight):
    count, coeffs, _ = transfer_weight.shape
    return pl.pallas_call(
        table_kernel,
        out_shape=jax.ShapeDtypeStruct((7, 7, 3, 2 * coeffs, 2 * coeffs), BF),
        in_specs=[WHOLE],
        out_specs=WHOLE,
        scratch_shapes=[pltpu.VMEM((-(-count // 128) * 128 * coeffs, 128), F32)],
        compiler_params=params(40),
        cost_estimate=pl.CostEstimate(flops=6 * 10**9, bytes_accessed=10**7, transcendentals=0),
        name="table",
    )(transfer_weight.transpose(1, 2, 0))


SHIFTS = [
    (dx, dy, dz)
    for dy in (1, 0, 2)
    for dz in (1, 0, 2)
    for dx in range(3)
    if (dx, dy, dz) != (1, 1, 1)
]


def moved_rows(rows, low, high):
    part = 8
    q = [rows[i : i + part] for i in range(0, rows.shape[0], part)]
    count = len(q)
    before = jnp.concatenate([low, q[-1][:-1]], axis=0)
    after = jnp.concatenate([q[0][1:], high], axis=0)
    if count == 4:
        return [before, q[2], q[0], q[1]], [q[2], q[3], q[1], after]
    if count == 2:
        return [before, q[0]], [q[1], after]
    return [before], [after]


def store_moved(rows, low, high, down, up, fill=False):
    rows = rows.astype(F32)
    one, two = moved_rows(rows, low, high)
    if fill:
        one, two = one + [jnp.zeros_like(rows)], two + [jnp.zeros_like(rows)]
    down[...] = jnp.concatenate(one, axis=0).astype(BF)
    up[...] = jnp.concatenate(two, axis=0).astype(BF)


def operator(table, shift, kernels, slot):
    dx, dy, dz = shift
    pair = table.shape[3]
    for sx in range(2):
        for sy in range(2):
            parts = [
                table[2 * dx + sx - tx + 1, 2 * dy + sy - ty + 1, dz]
                for tx in range(2)
                for ty in range(2)
            ]
            at = (2 * sx + sy) * pair
            kernels[slot, at : at + pair] = jnp.concatenate(parts, axis=1)
    return kernels[slot]


def near_kernel(table, leaf, below, above, out, leaf_lo, leaf_hi, kernels):
    size_y, size_z, size_x, width = leaf.shape
    low = below[: size_y * size_z].astype(F32)
    high = above[: size_y * size_z].astype(F32)
    for y in range(size_y):
        for z in range(size_z):
            at = y * size_z + z
            store_moved(
                leaf[y, z], low[at : at + 1], high[at : at + 1],
                leaf_lo.at[y, z], leaf_hi.at[y, z],
            )
    leaves = (leaf_lo, leaf, leaf_hi)
    for slot, (dx, dy, dz) in enumerate(SHIFTS):
        kernel = operator(table, (dx, dy, dz), kernels, slot)
        first_z, last_z = max(0, 1 - dz), size_z - max(0, dz - 1)
        first_y, last_y = max(0, 1 - dy), size_y - max(0, dy - 1)
        count = (last_z - first_z) * size_x
        for y in range(first_y, last_y, 2):
            many = min(2, last_y - y)
            rows = leaves[dx][
                y + dy - 1 : y + dy - 1 + many, first_z + dz - 1 : last_z + dz - 1
            ].reshape(many * count, width)
            product = jnp.dot(rows, kernel, preferred_element_type=F32)
            for i in range(many):
                at = ((y + i) * size_z + first_z) * size_x
                piece = product[i * count : (i + 1) * count]
                out[at : at + count] = piece if slot == 0 else out[at : at + count] + piece


def near(table, leaf, below, above):
    size_y, size_z, size_x, width = leaf.shape
    rows = size_y * size_z * size_x
    return pl.pallas_call(
        near_kernel,
        out_shape=jax.ShapeDtypeStruct((rows, width), F32),
        in_specs=[WHOLE] * 4,
        out_specs=WHOLE,
        scratch_shapes=[
            pltpu.VMEM(leaf.shape, BF),
            pltpu.VMEM(leaf.shape, BF),
            pltpu.VMEM((26, width, width), BF),
        ],
        compiler_params=params(60),
        cost_estimate=pl.CostEstimate(flops=10**10, bytes_accessed=10**7, transcendentals=0),
        name="near",
    )(table, leaf, below, above)


def far_kernel(
    total, table, middle, top, below_x, above_x, below_z, above_z, below_y, above_y, down, out,
    leaves, middles, tops, kernels, upper,
):
    size_y, size_z = 2 * middle.shape[0], 2 * middle.shape[1]
    half, width = middle.shape[2:]
    size_x = 2 * half
    coeffs = width // 8
    none = jnp.zeros((1, width), F32)

    sizes = [(size_y, size_z, size_x), (size_y // 2, size_z // 2, half), (size_y // 4, size_z // 4, half)]
    own = (None, middle, top)
    slabs = [{}, {}, {}]
    for side in range(2):
        x_block = (below_x, above_x)[side][...].astype(F32)
        z_block, y_block = (below_z, above_z)[side], (below_y, above_y)[side]
        at_x = at_z = at_y = 0
        for level, (count_y, count_z, rows) in enumerate(sizes):
            for y in range(count_y):
                if level > 0:
                    for z in range(count_z):
                        slabs[level].setdefault((y + 1, z + 1), [own[level][y, z], none, none])[
                            1 + side
                        ] = x_block[at_x + y * count_z + z : at_x + y * count_z + z + 1]
                slabs[level][y + 1, side * (count_z + 1)] = [
                    z_block[at_z + y * rows : at_z + (y + 1) * rows], none, none,
                ]
            for z in range(count_z + 2):
                slabs[level][side * (count_y + 1), z] = [
                    y_block[at_y + z * rows : at_y + (z + 1) * rows], none, none,
                ]
            at_x += count_y * count_z
            at_z += count_y * rows
            at_y += (count_z + 2) * rows
    for side in range(2):
        z_tail = (below_z, above_z)[side]
        y_tail = (below_y, above_y)[side]
        start_z = sum(c * r for c, _, r in sizes)
        start_y = sum((c + 2) * r for _, c, r in sizes)
        z_tail = z_tail[start_z:].astype(F32)
        y_tail = y_tail[start_y:].astype(F32)
        at_z = at_y = 0
        for level, (count_y, count_z, rows) in enumerate(sizes):
            for end in range(2):
                for y in range(count_y):
                    slabs[level][y + 1, side * (count_z + 1)][1 + end] = z_tail[at_z : at_z + 1]
                    at_z += 1
                for z in range(count_z + 2):
                    slabs[level][side * (count_y + 1), z][1 + end] = y_tail[at_y : at_y + 1]
                    at_y += 1

    copies = (leaves, middles, tops)
    for level in range(3):
        for (y, z), (rows, low, high) in slabs[level].items():
            copy = copies[level]
            copy[1, y, z] = rows
            if level == 2:
                rows = rows[: half // 2]
            store_moved(rows, low, high, copy.at[0, y, z], copy.at[2, y, z], level == 2)

    leaf_rows = size_y * size_z * size_x
    out[...] = total[...]
    for slot, (dx, dy, dz) in enumerate(SHIFTS):
        kernel = operator(table, (dx, dy, dz), kernels, slot)
        places, rows = [], []
        for y in range(size_y):
            for z in range(size_z):
                if y + dy in (0, size_y + 1) or z + dz in (0, size_z + 1):
                    places.append((y * size_z + z) * size_x)
                    rows.append(leaves[dx, y + dy, z + dz])
        rows += [
            middles[dx, dy : dy + size_y // 2, dz : dz + size_z // 2].reshape(-1, width),
            tops[dx, dy : dy + size_y // 4, dz : dz + size_z // 4].reshape(-1, width),
        ]
        product = jnp.dot(jnp.concatenate(rows, axis=0), kernel, preferred_element_type=F32)
        for i, at in enumerate(places):
            out[at : at + size_x] += product[i * size_x : (i + 1) * size_x]
        rest = product[len(places) * size_x :]
        upper[...] = rest if slot == 0 else upper[...] + rest

    weight = down[...]

    def spread(count_y, count_z, parent, rows):
        pieces = []
        for y in range(2 * count_y):
            for z in range(2 * count_z):
                for u in range(2):
                    octant = 4 * u + 2 * (y % 2) + z % 2
                    values = parent(y // 2, z // 2)
                    pieces.append(values[:rows, octant * coeffs : (octant + 1) * coeffs])
        return jnp.concatenate(pieces, axis=0).astype(BF)

    middle_rows = leaf_rows // 8

    def top_of(y, z):
        at = middle_rows + (y * (size_z // 4) + z) * half
        return upper[at : at + half]

    boxes = spread(size_y // 4, size_z // 4, top_of, half // 2)
    local = upper[:middle_rows] + jnp.dot(boxes, weight, preferred_element_type=F32)

    def middle_of(y, z):
        at = (y * (size_z // 2) + z) * half
        return local[at : at + half]

    boxes = spread(size_y // 2, size_z // 2, middle_of, half)
    out[...] += jnp.dot(boxes, weight, preferred_element_type=F32)


def far(total, table, middle, top, halos, down):
    width = total.shape[1]
    size_y, size_z, half = 2 * middle.shape[0], 2 * middle.shape[1], middle.shape[2]
    upper = half * ((size_y // 2) * (size_z // 2) + (size_y // 4) * (size_z // 4))
    return pl.pallas_call(
        far_kernel,
        out_shape=jax.ShapeDtypeStruct(total.shape, F32),
        in_specs=[WHOLE] * 11,
        out_specs=WHOLE,
        scratch_shapes=[
            pltpu.VMEM((3, size_y + 2, size_z + 2, 2 * half, width), BF),
            pltpu.VMEM((3, size_y // 2 + 2, size_z // 2 + 2, half, width), BF),
            pltpu.VMEM((3, size_y // 4 + 2, size_z // 4 + 2, half, width), BF),
            pltpu.VMEM((26, width, width), BF),
            pltpu.VMEM((upper, width), F32),
        ],
        compiler_params=params(60),
        name="far",
    )(total, table, middle, top, *halos, down)


def shards(densities, upward_weight, transfer_weight, downward_weight):
    size_x, size_y, size_z, width = densities.shape
    base = densities.reshape(size_x // 4, 2, 2, size_y, size_z, width)
    base = base.transpose(3, 4, 2, 1, 0, 5).reshape(size_y, size_z, size_x, width)
    middle, top = lifted(base, upward_weight)
    levels = [base, middle, top]
    lasts = [size_x, size_x // 2, size_x // 4]

    def packed(pieces):
        rows = jnp.concatenate([piece.reshape(-1, width) for piece in pieces], axis=0)
        return jnp.pad(rows, ((0, -rows.shape[0] % 16), (0, 0)))

    def unpacked(flat, shapes):
        pieces, at = [], 0
        for shape in shapes:
            count = 1
            for extent in shape:
                count *= extent
            pieces.append(flat[at : at + count].reshape(shape + (width,)))
            at += count
        return pieces

    low = packed([level[:, :, 0] for level in levels])
    high = packed([level[:, :, last - 1] for level, last in zip(levels, lasts)])
    below_x, above_x = exchange(low, high, "gx")
    shapes = [level.shape[:2] for level in levels]
    sides = [
        jnp.stack(both) for both in zip(unpacked(below_x, shapes), unpacked(above_x, shapes))
    ]

    low_z = [level[:, 0] for level in levels] + [side[:, :, 0] for side in sides]
    high_z = [level[:, -1] for level in levels] + [side[:, :, -1] for side in sides]
    shapes = [piece.shape[:-1] for piece in low_z]
    low_z, high_z = packed(low_z), packed(high_z)
    low_z, high_z, transfer_weight = lax.optimization_barrier((low_z, high_z, transfer_weight))
    table = tabled(transfer_weight)
    below_z, above_z = exchange(low_z, high_z, "gz")

    lows, highs = unpacked(below_z, shapes), unpacked(above_z, shapes)

    def face(at):
        rows = [
            jnp.concatenate([one[at][None], level[at], two[at][None]], axis=0)
            for one, level, two in zip(lows[:3], levels, highs[:3])
        ]
        rows += [
            jnp.concatenate([one[:, at, None], side[:, at], two[:, at, None]], axis=1)
            for one, side, two in zip(lows[3:], sides, highs[3:])
        ]
        return packed(rows)

    low_y, high_y = face(0), face(-1)
    low_y, high_y, table = lax.optimization_barrier((low_y, high_y, table))
    below_y, above_y = exchange(low_y, high_y, "gy")
    total = near(table, base, below_x, above_x)
    halos = (below_x, above_x, below_z, above_z, below_y, above_y)
    result = far(total, table, middle, top, halos, downward_weight)
    result = result.reshape(size_y, size_z, 2, 2, size_x // 4, width)
    return result.transpose(4, 3, 2, 0, 1, 5).reshape(densities.shape)


def solution(mesh):
    placed = (P("gx", "gy", "gz", None), P(), P(), P())
    return jax.shard_map(
        shards, mesh=mesh, in_specs=placed, out_specs=P("gx", "gy", "gz", None), check_vma=False
    )
```

time: 81.7 us -> 62.4 us (0.76)
  the two profiles are of different devices: /device:TPU:8 before, /device:TPU:0 now
where the time goes in v2:
time: 62.4 us; the launch traced here: 62.1 us
  Pallas kernels  34 us (54%)
  local copies, waits for them, and re-layouts  12.6 us (20%)
  starting transfers between devices  11.9 us (19%)
  other arithmetic  1.54 us (2%)
  waiting for transfers between devices  1.25 us (2%)
  between operations  0.75 us (1%)
    pallas_call x1, Pallas kernels, near(): pl.pallas_call(near_kernel, out_shape=jax.ShapeDtypeStruct((rows, width),...  15.1 us
    ppermute x5, starting transfers between devices, swap(): return lax.ppermute(block, axis, pairs)  11.9 us
    pallas_call x1, Pallas kernels, far(): pl.pallas_call(far_kernel, out_shape=jax.ShapeDtypeStruct(total.shape, F3...  11.8 us
    pallas_call x1, Pallas kernels, tabled(): pl.pallas_call(table_kernel, out_shape=jax.ShapeDtypeStruct((7, 7, 3, 2 *...  6.04 us
    unnamed x33, local copies, waits for them, and re-layouts  4.73 us
    transpose x1, local copies, waits for them, and re-layouts, shards(): return result.transpose(4, 3, 2, 0, 1, 5).reshape(densities.shape)  4.26 us
    reshape x1, local copies, waits for them, and re-layouts, shards(): base = densities.reshape(size_x // 4, 2, 2, size_y, size_z, width)  1.81 us
    ppermute x5, waiting for transfers between devices, swap(): return lax.ppermute(block, axis, pairs)  1.25 us
  transfers between devices with their start and end apart: 5, of which 2 were waited for; matrix products, arithmetic and copies ran while one was open for 0% of the time, Pallas kernels for 34%

profile of v2, /device:TPU:0, one launch (start us, length us, event | category | flops | bytes accessed | tf_op | source)
XLA Modules:
  0.0 62.1 jit_solution(2191951667289582550)
XLA Ops:
  0.0 1.0 %copy.25.weight = bf16[448,56]{1,0:T(8,128)(2,1)S(1)} copy(bf16[448,56]{0,1:T(8,128)(2,1)} %param.5) | data formatting | bytes 100352 | tf_op args[1]
  1.0 1.8 %copy.61 = bf16[8,2,2,8,4,448]{5,0,1,2,4,3:T(8,128)(2,1)S(1)} copy(bf16[8,2,2,8,4,448]{5,4,3,2,1,0:T(4,128)(2,1)} %bitcast.104) | data formatting | bytes 1835008 | tf_op jit(solution)/shard_map/reshape | solution.py:373
  2.8 0.0 copy-start
  2.8 0.3 slice_reduce_fusion.1
  3.1 1.1 %lift.1 = (bf16[4,2,16,448]{3,2,1,0:T(8,128)(2,1)S(1)}, bf16[2,1,16,448]{3,2,1,0:T(8,128)(2,1)S(1)}) custom-call(bf16[8,4,32,448]{3,2,1,0:T(8,128)(2,1)S(1)} %bitcast.97, bf16[448,56]{1,0:T(8,128)(2,1)S(1)} %copy.25.weight), custom_call_target="tpu_custom_call" | custom-call | tf_op jit(solution)/shard_map/lift/pallas_call | solution.py:74
  4.2 0.0 copy-start.2
  4.2 0.0 copy-start.3
  4.2 0.1 slice_reduce_fusion.3
  4.5 0.7 %collective-permute-start.1 = (bf16[48,448]{1,0:T(8,128)(2,1)S(1)}, bf16[48,448]{1,0:T(8,128)(2,1)S(1)}, u32[]{:S(2)}, u32[]{:S(2)}) collective-permute-start(bf16[48,448]{1,0:T(8,128)(2,1)S(1)} %get-tuple-element.57), channel_id=1, source_target_pairs={{8,16},{16,8},{9,17},{17,9},{10,18},{18,10},{11,19},{19,11},{12,20... | collective-permute-start | bytes 129032 | tf_op jit(solution)/shard_map/ppermute | solution.py:27
  5.1 4.4 %collective-permute-start = (bf16[48,448]{1,0:T(8,128)(2,1)S(1)}, bf16[48,448]{1,0:T(8,128)(2,1)S(1)}, u32[]{:S(2)}, u32[]{:S(2)}) collective-permute-start(bf16[48,448]{1,0:T(8,128)(2,1)S(1)} %get-tuple-element.58), channel_id=1, source_target_pairs={{0,8},{8,0},{16,24},{24,16},{1,9},{9,1},{17,25},{25,17},{2,10},{10... | collective-permute-start | bytes 129032 | tf_op jit(solution)/shard_map/ppermute | solution.py:27
  9.6 0.0 copy-done
  9.7 0.0 collective-permute-done.1
  9.7 0.6 %collective-permute-done = bf16[48,448]{1,0:T(8,128)(2,1)S(1)} collective-permute-done((bf16[48,448]{1,0:T(8,128)(2,1)S(1)}, bf16[48,448]{1,0:T(8,128)(2,1)S(1)}, u32[]{:S(2)}, u32[]{:S(2)}) %collective-permute-start) | collective-permute-done | bytes 43040 | tf_op jit(solution)/shard_map/ppermute | solution.py:27
  10.4 0.0 copy-done.2
  10.4 0.0 copy-done.3
  10.4 0.0 copy-start.7
  10.4 0.0 copy-start.8
  10.6 0.1 slice_maximum_fusion
  10.7 0.1 fusion.11
  11.1 1.6 %collective-permute-start.2 = (bf16[384,448]{1,0:T(8,128)(2,1)S(1)}, bf16[384,448]{1,0:T(8,128)(2,1)S(1)}, u32[]{:S(2)}, u32[]{:S(2)}) collective-permute-start(bf16[384,448]{1,0:T(8,128)(2,1)S(1)} %broadcast_select_fusion.2), channel_id=1, source_target_pairs={{0,1},{1,0},{2,3},{3,2},{4,5},{5,4},{6,7},{7,6},{8,9},{9,8},{10,11... | collective-permute-start | bytes 1032200 | tf_op jit(solution)/shard_map/ppermute | solution.py:27
  12.7 0.0 copy-start.4
  12.7 1.7 %copy-done.4 = bf16[316,56,56]{0,2,1:T(8,128)(2,1)S(1)} copy-done((bf16[316,56,56]{0,2,1:T(8,128)(2,1)S(1)}, bf16[316,56,56]{0,2,1:T(8,128)(2,1)}, u32[]{:S(2)}) %copy-start.4) | copy-done | bytes 1981976
  14.4 6.0 %table.1 = bf16[7,7,3,112,112]{4,3,2,1,0:T(8,128)(2,1)S(1)} custom-call(bf16[56,56,316]{2,1,0:T(8,128)(2,1)S(1)} %bitcast.102), custom_call_target="tpu_custom_call" | custom-call | flops 6000000000 | bytes 10000000 | tf_op jit(solution)/shard_map/table/pallas_call | solution.py:135
  20.4 0.0 copy-done.7
  20.5 0.0 copy-done.8
  20.5 0.0 copy-start.1
  20.5 2.0 %copy-done.1 = bf16[7,7,3,112,112]{4,3,2,1,0:T(8,128)(2,1)} copy-done((bf16[7,7,3,112,112]{4,3,2,1,0:T(8,128)(2,1)}, bf16[7,7,3,112,112]{4,3,2,1,0:T(8,128)(2,1)S(1)}, u32[]{:S(2)}) %copy-start.1) | copy-done | bytes 3687960
  22.4 0.6 collective-permute-done.2
  23.0 0.1 broadcast_select_fusion.1
  23.1 0.0 copy-start.5
  23.1 0.0 copy-start.6
  23.8 0.3 concatenate.71
  24.3 0.3 concatenate.64
  24.6 0.0 copy-done.5
  24.6 0.0 copy-done.6
  24.6 0.1 broadcast_select_fusion.5
  24.7 0.9 %collective-permute-start.4 = (bf16[336,448]{1,0:T(8,128)(2,1)S(1)}, bf16[336,448]{1,0:T(8,128)(2,1)S(1)}, u32[]{:S(2)}, u32[]{:S(2)}) collective-permute-start(bf16[336,448]{1,0:T(8,128)(2,1)S(1)} %get-tuple-element.33), channel_id=1, source_target_pairs={{2,4},{4,2},{3,5},{5,3},{10,12},{12,10},{11,13},{13,11},{18,20},{2... | collective-permute-start | bytes 903176 | tf_op jit(solution)/shard_map/ppermute | solution.py:27
  25.6 4.4 %collective-permute-start.3 = (bf16[336,448]{1,0:T(8,128)(2,1)S(1)}, bf16[336,448]{1,0:T(8,128)(2,1)S(1)}, u32[]{:S(2)}, u32[]{:S(2)}) collective-permute-start(bf16[336,448]{1,0:T(8,128)(2,1)S(1)} %get-tuple-element.34), channel_id=1, source_target_pairs={{0,2},{2,0},{4,6},{6,4},{1,3},{3,1},{5,7},{7,5},{8,10},{10,8},{12,... | collective-permute-start | bytes 903176 | tf_op jit(solution)/shard_map/ppermute | solution.py:27
  30.0 15.1 %near.1.total = f32[1024,448]{1,0:T(8,128)} custom-call(bf16[7,7,3,112,112]{4,3,2,1,0:T(8,128)(2,1)} %copy-done.1, bf16[8,4,32,448]{3,2,1,0:T(8,128)(2,1)} %bitcast.100, bf16[48,448]{1,0:T(8,128)(2,1)} %copy-done.8, bf16[48,448]{1,0:T(8,128)(2,1)} %copy-done.7), custom_call_target="tpu_custom_call" | custom-call | flops 10000000000 | bytes 10000000 | tf_op jit(solution)/shard_map/near/pallas_call | solution.py:225
  45.1 0.0 collective-permute-done.4
  45.1 0.0 collective-permute-done.3
  45.1 0.9 %broadcast_select_fusion.3 = (bf16[336,448]{1,0:T(8,128)(2,1)}, bf16[336,448]{1,0:T(8,128)(2,1)}) fusion(bf16[336,448]{1,0:T(8,128)(2,1)S(1)} %collective-permute-done.4, bf16[336,448]{1,0:T(8,128)(2,1)S(1)} %collective-permute-done.3, pred[]{:T(512)S(6)} %eq.15), kind=kLoop, calls=%fused_computation.3 | loop fusion | flops 301056 | bytes 1204225 | tf_op jit(solution)/shard_map/jit(_where)/select_n | solution.py:34
  46.0 11.8 %far.1 = f32[1024,448]{1,0:T(8,128)} custom-call(f32[1024,448]{1,0:T(8,128)} %near.1.total, bf16[7,7,3,112,112]{4,3,2,1,0:T(8,128)(2,1)} %copy-done.1, bf16[4,2,16,448]{3,2,1,0:T(8,128)(2,1)} %copy-done.2, bf16[2,1,16,448]{3,2,1,0:T(8,128)(2,1)} %copy-done.3, bf16[48,448]{1,0:T(8,128)(2,1)} %copy-done.8, bf16[48,448]{1,0:T(8,128)(2,1)} %copy-done.7, ...), custom_call_target="tpu_custom_call" | custom-call | tf_op jit(solution)/shard_map/far/pallas_call | solution.py:354
  57.9 4.3 %copy.42 = f32[8,2,2,8,4,448]{5,4,3,2,1,0:T(4,128)} copy(f32[8,2,2,8,4,448]{5,0,1,2,4,3:T(8,128)} %bitcast.103) | data formatting | bytes 3670016 | tf_op jit(solution)/shard_map/transpose | solution.py:429
  (89 shorter events, 1.3 us)
Async XLA Ops:
  2.8 6.9 %copy-start = (bf16[8,2,2,8,4,448]{5,0,1,2,4,3:T(8,128)(2,1)}, bf16[8,2,2,8,4,448]{5,0,1,2,4,3:T(8,128)(2,1)S(1)}, u32[]{:S(2)}) copy-start(bf16[8,2,2,8,4,448]{5,0,1,2,4,3:T(8,128)(2,1)S(1)} %copy.61) | copy-start | bytes 2752516
  4.2 6.2 %copy-start.2 = (bf16[4,2,16,448]{3,2,1,0:T(8,128)(2,1)}, bf16[4,2,16,448]{3,2,1,0:T(8,128)(2,1)S(1)}, u32[]{:S(2)}) copy-start(bf16[4,2,16,448]{3,2,1,0:T(8,128)(2,1)S(1)} %get-tuple-element.13.middle) | copy-start | bytes 344068
  4.2 6.2 %copy-start.3 = (bf16[2,1,16,448]{3,2,1,0:T(8,128)(2,1)}, bf16[2,1,16,448]{3,2,1,0:T(8,128)(2,1)S(1)}, u32[]{:S(2)}) copy-start(bf16[2,1,16,448]{3,2,1,0:T(8,128)(2,1)S(1)} %get-tuple-element.14.top) | copy-start | bytes 86020
  4.5 5.3 %collective-permute-start.1 = (bf16[48,448]{1,0:T(8,128)(2,1)S(1)}, bf16[48,448]{1,0:T(8,128)(2,1)S(1)}, u32[]{:S(2)}, u32[]{:S(2)}) collective-permute-start(bf16[48,448]{1,0:T(8,128)(2,1)S(1)} %get-tuple-element.57), channel_id=1, source_target_pairs={{8,16},{16,8},{9,17},{17,9},{10,18},{18,10},{11,19},{19,11},{12,20... | collective-permute-start | bytes 129032 | tf_op jit(solution)/shard_map/ppermute | solution.py:27
  5.1 5.2 %collective-permute-start = (bf16[48,448]{1,0:T(8,128)(2,1)S(1)}, bf16[48,448]{1,0:T(8,128)(2,1)S(1)}, u32[]{:S(2)}, u32[]{:S(2)}) collective-permute-start(bf16[48,448]{1,0:T(8,128)(2,1)S(1)} %get-tuple-element.58), channel_id=1, source_target_pairs={{0,8},{8,0},{16,24},{24,16},{1,9},{9,1},{17,25},{25,17},{2,10},{10... | collective-permute-start | bytes 129032 | tf_op jit(solution)/shard_map/ppermute | solution.py:27
  10.4 10.0 %copy-start.7 = (bf16[48,448]{1,0:T(8,128)(2,1)}, bf16[48,448]{1,0:T(8,128)(2,1)S(1)}, u32[]{:S(2)}) copy-start(bf16[48,448]{1,0:T(8,128)(2,1)S(1)} %get-tuple-element.55.above.above_x) | copy-start | bytes 129028
  10.4 10.0 %copy-start.8 = (bf16[48,448]{1,0:T(8,128)(2,1)}, bf16[48,448]{1,0:T(8,128)(2,1)S(1)}, u32[]{:S(2)}) copy-start(bf16[48,448]{1,0:T(8,128)(2,1)S(1)} %get-tuple-element.56.below.below_x) | copy-start | bytes 129028
  11.1 11.9 %collective-permute-start.2 = (bf16[384,448]{1,0:T(8,128)(2,1)S(1)}, bf16[384,448]{1,0:T(8,128)(2,1)S(1)}, u32[]{:S(2)}, u32[]{:S(2)}) collective-permute-start(bf16[384,448]{1,0:T(8,128)(2,1)S(1)} %broadcast_select_fusion.2), channel_id=1, source_target_pairs={{0,1},{1,0},{2,3},{3,2},{4,5},{5,4},{6,7},{7,6},{8,9},{9,8},{10,11... | collective-permute-start | bytes 1032200 | tf_op jit(solution)/shard_map/ppermute | solution.py:27
  12.7 1.7 %copy-start.4 = (bf16[316,56,56]{0,2,1:T(8,128)(2,1)S(1)}, bf16[316,56,56]{0,2,1:T(8,128)(2,1)}, u32[]{:S(2)}) copy-start(bf16[316,56,56]{0,2,1:T(8,128)(2,1)} %param.6) | copy-start | bytes 5945860
  20.5 2.0 %copy-start.1 = (bf16[7,7,3,112,112]{4,3,2,1,0:T(8,128)(2,1)}, bf16[7,7,3,112,112]{4,3,2,1,0:T(8,128)(2,1)S(1)}, u32[]{:S(2)}) copy-start(bf16[7,7,3,112,112]{4,3,2,1,0:T(8,128)(2,1)S(1)} %table.1) | copy-start | bytes 11063812
  23.1 1.5 %copy-start.5 = (bf16[384,448]{1,0:T(8,128)(2,1)}, bf16[384,448]{1,0:T(8,128)(2,1)S(1)}, u32[]{:S(2)}) copy-start(bf16[384,448]{1,0:T(8,128)(2,1)S(1)} %get-tuple-element.49.below_z) | copy-start | bytes 1032196
  23.1 1.5 %copy-start.6 = (bf16[384,448]{1,0:T(8,128)(2,1)}, bf16[384,448]{1,0:T(8,128)(2,1)S(1)}, u32[]{:S(2)}) copy-start(bf16[384,448]{1,0:T(8,128)(2,1)S(1)} %get-tuple-element.50.above_z) | copy-start | bytes 1032196
  24.7 20.4 %collective-permute-start.4 = (bf16[336,448]{1,0:T(8,128)(2,1)S(1)}, bf16[336,448]{1,0:T(8,128)(2,1)S(1)}, u32[]{:S(2)}, u32[]{:S(2)}) collective-permute-start(bf16[336,448]{1,0:T(8,128)(2,1)S(1)} %get-tuple-element.33), channel_id=1, source_target_pairs={{2,4},{4,2},{3,5},{5,3},{10,12},{12,10},{11,13},{13,11},{18,20},{2... | collective-permute-start | bytes 903176 | tf_op jit(solution)/shard_map/ppermute | solution.py:27
  25.6 19.5 %collective-permute-start.3 = (bf16[336,448]{1,0:T(8,128)(2,1)S(1)}, bf16[336,448]{1,0:T(8,128)(2,1)S(1)}, u32[]{:S(2)}, u32[]{:S(2)}) collective-permute-start(bf16[336,448]{1,0:T(8,128)(2,1)S(1)} %get-tuple-element.34), channel_id=1, source_target_pairs={{0,2},{2,0},{4,6},{6,4},{1,3},{3,1},{5,7},{7,5},{8,10},{10,8},{12,... | collective-permute-start | bytes 903176 | tf_op jit(solution)/shard_map/ppermute | solution.py:27

commit v3 on v2

v3 whole, which is shorter than its diff:
```python
import functools

import jax
import jax.numpy as jnp
from jax import lax
from jax.experimental import pallas as pl
from jax.experimental.pallas import tpu as pltpu
from jax.sharding import PartitionSpec as P

BF = jnp.bfloat16
F32 = jnp.float32
ANYWHERE = pl.BlockSpec(memory_space=pl.ANY)
HBM = pl.BlockSpec(memory_space=pltpu.HBM)
WHOLE = pl.BlockSpec(memory_space=pltpu.VMEM)


def params(mib):
    return pltpu.CompilerParams(vmem_limit_bytes=mib * 2**20)


def rounds(axis):
    count = lax.axis_size(axis)
    return [[(i, i + 1) for i in range(first, count - 1, 2)] for first in (0, 1)]


def swapped(block, axis, pairs):
    both = pairs + [(two, one) for one, two in pairs]
    return lax.ppermute(block, axis, both) if pairs else jnp.zeros_like(block)


def is_odd(axis):
    return lax.axis_index(axis) % 2 == 1


def exchange(low, high, axis):
    odd = is_odd(axis)
    first, other = rounds(axis)
    got = swapped(jnp.where(odd, low, high), axis, first)
    return got, swapped(jnp.where(odd, high, low), axis, other)


def exchange_corners(faces, axis_y, axis_z):
    odd_y, odd_z = is_odd(axis_y), is_odd(axis_z)
    count_z = lax.axis_size(axis_z)
    result = []
    for round_y, pairs_y in enumerate(rounds(axis_y)):
        low_y, high_y = faces if round_y == 0 else faces[::-1]
        for round_z, pairs_z in enumerate(rounds(axis_z)):
            low = [jnp.where(odd_y, one, two) for one, two in zip(low_y, high_y)]
            low = low if round_z == 0 else low[::-1]
            pairs = []
            for one, two in pairs_y:
                for three, four in pairs_z:
                    pairs.append((one * count_z + three, two * count_z + four))
                    pairs.append((one * count_z + four, two * count_z + three))
            face = jnp.where(odd_z, low[0], low[1])
            result.append(swapped(face, (axis_y, axis_z), pairs))
    return jnp.stack(result).reshape(2, 2, *result[0].shape)


def lift_kernel(base, weight, middle, top):
    size_y, size_z, size_x, width = base.shape
    half, part = size_x // 2, size_x // 4
    coeffs = weight.shape[1]
    up = weight[...]

    def lift(rows):
        return jnp.dot(rows, up, preferred_element_type=F32).astype(BF).astype(F32)

    boxes = {}
    for y in range(size_y):
        for z in range(size_z):
            boxes[y, z] = lift(base[y, z])
    coarse = {}
    for y in range(size_y // 2):
        for z in range(size_z // 2):
            pieces = []
            for u in range(2):
                for v in range(2):
                    for w in range(2):
                        pieces.append(boxes[2 * y + v, 2 * z + w][u * half : (u + 1) * half])
            group = jnp.concatenate(pieces, axis=1).astype(BF)
            middle[y, z] = group
            coarse[y, z] = lift(group)
    for y in range(size_y // 4):
        for z in range(size_z // 4):
            pieces = []
            for u in range(2):
                for v in range(2):
                    for w in range(2):
                        pieces.append(coarse[2 * y + v, 2 * z + w][u * part : (u + 1) * part])
            group = jnp.concatenate(pieces, axis=1)
            top[y, z] = jnp.concatenate([group, jnp.zeros_like(group)], axis=0).astype(BF)


def lifted(base, upward_weight):
    size_y, size_z, size_x, width = base.shape
    return pl.pallas_call(
        lift_kernel,
        out_shape=(
            jax.ShapeDtypeStruct((size_y // 2, size_z // 2, size_x // 2, width), BF),
            jax.ShapeDtypeStruct((size_y // 4, size_z // 4, size_x // 2, width), BF),
        ),
        in_specs=[WHOLE, WHOLE],
        out_specs=(WHOLE, WHOLE),
        compiler_params=params(24),
        name="lift",
    )(base, upward_weight)


def fill_table(weight, arriving, table, blocks):
    coeffs, _, count = weight.shape
    lanes, batch = 128, coeffs // len(arriving)

    def turn(source, carry):
        rows = weight[source].astype(F32)
        for at in range(0, count, lanes):
            part = widened(rows[:, at : min(at + lanes, count)])
            turned = widened(part.T)
            blocks[pl.ds(at * coeffs + source, lanes, stride=coeffs), :] = turned
        return carry

    for i, copy in enumerate(arriving):
        copy.wait()
        lax.fori_loop(i * batch, (i + 1) * batch, turn, 0, unroll=4)

    def one(position, carry):
        first = position // 7
        second = position % 7
        mid_first = jnp.logical_and(first >= 2, first <= 4)
        mid = jnp.logical_and(mid_first, jnp.logical_and(second >= 2, second <= 4))
        skipped = 9 * jnp.clip(first - 2, 0, 3) + jnp.where(
            mid_first, 3 * jnp.clip(second - 2, 0, 3), 0
        )
        start = 7 * position - skipped
        found = []
        for third in range(7):
            near = third in (2, 3, 4)
            if near:
                place = jnp.where(mid, 0, start + third)
            else:
                place = start + third - jnp.where(mid, min(max(third - 2, 0), 3), 0)
            block = blocks[pl.ds(pl.multiple_of(place * coeffs, 8), coeffs)]
            found.append(jnp.where(mid, 0.0, block) if near else block)
        moved = [pltpu.roll(block, coeffs, 1) for block in found[:6]]
        for third in range(3):
            rows = [found[2 * third + s + 1] + moved[2 * third + s] for s in range(2)]
            rows = jnp.concatenate(rows, axis=0)
            table[third, first, second] = rows[:, : 2 * coeffs].astype(BF)
        return carry

    lax.fori_loop(0, 49, one, 0, unroll=7)


SLOTS = 8
SHIFTS = [
    (dx, dy, dz)
    for dz in (1, 0, 2)
    for dy in (1, 0, 2)
    for dx in range(3)
    if (dx, dy, dz) != (1, 1, 1)
]


def moved_rows(rows, low, high):
    part = 8
    q = [rows[i : i + part] for i in range(0, rows.shape[0], part)]
    count = len(q)
    before = jnp.concatenate([low, q[-1][:-1]], axis=0)
    after = jnp.concatenate([q[0][1:], high], axis=0)
    if count == 4:
        return [before, q[2], q[0], q[1]], [q[2], q[3], q[1], after]
    if count == 2:
        return [before, q[0]], [q[1], after]
    return [before], [after]


def widened(rows):
    fill = -rows.shape[1] % 128
    if fill:
        zeros = jnp.zeros((rows.shape[0], fill), rows.dtype)
        rows = jnp.concatenate([rows, zeros], axis=1)
    return rows


def store_moved(rows, low, high, copies, y, z, fill=False):
    rows = widened(rows.astype(F32))
    one, two = moved_rows(rows, widened(low), widened(high))
    three = [one, [rows], two]
    for dx in range(3):
        if fill:
            three[dx] = three[dx] + [jnp.zeros_like(rows)]
        copies[dx, y, z] = jnp.concatenate(three[dx], axis=0).astype(BF)


def operator(table, shift, kernels, slot):
    dx, dy, dz = shift
    slot = slot % kernels.shape[0]
    pair = table.shape[4]
    for sx in range(2):
        for sy in range(2):
            parts = [
                table[dz, 2 * dx + sx - tx + 1, 2 * dy + sy - ty + 1]
                for tx in range(2)
                for ty in range(2)
            ]
            at = (2 * sx + sy) * pair
            kernels[slot, at : at + pair] = widened(jnp.concatenate(parts, axis=1))
    rows = kernels.shape[1]
    if rows > 4 * pair:
        kernels[slot, 4 * pair :] = jnp.zeros((rows - 4 * pair, kernels.shape[2]), BF)
    return kernels[slot]


def add_near(slots, table, leaf, below, above, leaves, kernels, total, ready=None):
    size_y, size_z, size_x, width = leaf.shape
    low = below[: size_y * size_z].astype(F32)
    high = above[: size_y * size_z].astype(F32)
    for y in range(size_y):
        for z in range(size_z):
            at = y * size_z + z
            store_moved(leaf[y, z], low[at : at + 1], high[at : at + 1], leaves, y, z)
    if slots[0] > 0:
        total[...] = jnp.zeros_like(total)
    for slot in slots:
        dx, dy, dz = SHIFTS[slot]
        if ready is not None:
            ready(dz)
        kernel = operator(table, (dx, dy, dz), kernels, slot)
        first_z, last_z = max(0, 1 - dz), size_z - max(0, dz - 1)
        first_y, last_y = max(0, 1 - dy), size_y - max(0, dy - 1)
        count = (last_z - first_z) * size_x
        rows = leaves[
            dx, first_y + dy - 1 : last_y + dy - 1, first_z + dz - 1 : last_z + dz - 1
        ].reshape(-1, leaves.shape[4])
        product = jnp.dot(rows, kernel, preferred_element_type=F32)
        for i in range(last_y - first_y):
            at = ((first_y + i) * size_z + first_z) * size_x
            piece = product[i * count : (i + 1) * count]
            total[at : at + count] = piece if slot == 0 else total[at : at + count] + piece


def first_kernel(
    given, leaf, below, above, _, table, total, weight, blocks, leaves, kernels, arrived
):
    coeffs = given.shape[0]
    count = arrived.shape[0]
    batch = coeffs // count
    arriving = []
    for i in range(count):
        part = pl.ds(i * batch, batch)
        arriving.append(pltpu.make_async_copy(given.at[part], weight.at[part], arrived.at[i]))
        arriving[i].start()
    fill_table(weight, arriving, table, blocks)
    add_near(range(len(SHIFTS)), table, leaf, below, above, leaves, kernels, total)


def first_part(transfer_weight, leaf, below, above, after):
    count, coeffs, _ = transfer_weight.shape
    size_y, size_z, size_x, width = leaf.shape
    wide = -(-width // 128) * 128
    return pl.pallas_call(
        first_kernel,
        out_shape=(
            jax.ShapeDtypeStruct((3, 7, 7, 2 * coeffs, 2 * coeffs), BF),
            jax.ShapeDtypeStruct((size_y * size_z * size_x, wide), F32),
        ),
        in_specs=[HBM] + [WHOLE] * 3 + [ANYWHERE],
        out_specs=(WHOLE, WHOLE),
        scratch_shapes=[
            pltpu.VMEM((coeffs, coeffs, count), BF),
            pltpu.VMEM((-(-count // 128) * 128 * coeffs, 128), F32),
            pltpu.VMEM((3, size_y, size_z, size_x, wide), BF),
            pltpu.VMEM((SLOTS, wide, wide), BF),
            pltpu.SemaphoreType.DMA((7,)),
        ],
        compiler_params=params(32),
        cost_estimate=pl.CostEstimate(flops=2 * 10**10, bytes_accessed=10**7, transcendentals=0),
        name="first",
    )(transfer_weight.transpose(1, 2, 0), leaf, below, above, after)


def far_kernel(
    odd, near, table, middle, top, below_x, above_x, got_z, got_y, got_yz, down, out,
    total, leaves, middles, tops, kernels, upper, turned,
):
    size_y, size_z = 2 * middle.shape[0], 2 * middle.shape[1]
    half, width = middle.shape[2:]
    size_x = 2 * half
    coeffs = width // 8
    none = jnp.zeros((1, width), F32)
    odd_y, odd_z = odd[0] == 1, odd[1] == 1

    def chosen(is_odd, side, got, rows):
        first, other = got[0, rows], got[1, rows]
        pair = (first, other) if side == 0 else (other, first)
        return jnp.where(is_odd, pair[0], pair[1])

    def corner(side_y, side_z, rows):
        near_y = [chosen(odd_z, side_z, got_yz.at[i], rows) for i in range(2)]
        pair = near_y if side_y == 0 else near_y[::-1]
        return jnp.where(odd_y, pair[0], pair[1])

    sizes = [(size_y, size_z, size_x), (size_y // 2, size_z // 2, half), (size_y // 4, size_z // 4, half)]
    own = (None, middle, top)
    slabs = [{}, {}, {}]
    at_x = 0
    sides_x = [below_x[...].astype(F32), above_x[...].astype(F32)]
    for level, (count_y, count_z, rows) in enumerate(sizes):
        for y in range(count_y):
            for z in range(count_z):
                if level > 0:
                    ends = [side[at_x : at_x + 1] for side in sides_x]
                    slabs[level][y + 1, z + 1] = [own[level][y, z], *ends]
                at_x += 1

    def unpack(read, spots):
        at = 0
        for level, (_, _, rows) in enumerate(sizes):
            for spot in spots(level):
                slabs[level][spot] = [read(slice(at, at + rows))]
                at += rows
        count = 2 * sum(len(spots(level)) for level in range(3))
        tail = read(slice(at, at + -(-count // 16) * 16)).astype(F32)
        at = 0
        for level in range(3):
            for end in range(2):
                for spot in spots(level):
                    slabs[level][spot].append(tail[at : at + 1])
                    at += 1

    for side in range(2):
        unpack(
            functools.partial(chosen, odd_z, side, got_z),
            lambda level: [(y + 1, side * (sizes[level][1] + 1)) for y in range(sizes[level][0])],
        )
        unpack(
            functools.partial(chosen, odd_y, side, got_y),
            lambda level: [(side * (sizes[level][0] + 1), z + 1) for z in range(sizes[level][1])],
        )
        for other in range(2):
            unpack(
                functools.partial(corner, side, other),
                lambda level: [(side * (sizes[level][0] + 1), other * (sizes[level][1] + 1))],
            )

    copies = (leaves, middles, tops)
    for level in range(3):
        for (y, z), (rows, low, high) in slabs[level].items():
            if level == 2:
                rows = rows[: half // 2]
            store_moved(rows, low, high, copies[level], y, z, level == 2)

    total[...] = near[...]
    leaf_rows = size_y * size_z * size_x
    wide = kernels.shape[1]
    for slot, (dx, dy, dz) in enumerate(SHIFTS):
        kernel = operator(table, (dx, dy, dz), kernels, slot)
        places, rows = [], []
        for y in range(size_y):
            for z in range(size_z):
                if y + dy in (0, size_y + 1) or z + dz in (0, size_z + 1):
                    places.append((y * size_z + z) * size_x)
                    rows.append(leaves[dx, y + dy, z + dz])
        rows += [
            middles[dx, dy : dy + size_y // 2, dz : dz + size_z // 2].reshape(-1, wide),
            tops[dx, dy : dy + size_y // 4, dz : dz + size_z // 4].reshape(-1, wide),
        ]
        product = jnp.dot(jnp.concatenate(rows, axis=0), kernel, preferred_element_type=F32)
        for i, at in enumerate(places):
            total[at : at + size_x] += product[i * size_x : (i + 1) * size_x]
        rest = product[len(places) * size_x :, :width]
        upper[...] = rest if slot == 0 else upper[...] + rest

    weight = down[...]

    def spread(count_y, count_z, parent, rows):
        pieces = []
        for y in range(2 * count_y):
            for z in range(2 * count_z):
                for u in range(2):
                    octant = 4 * u + 2 * (y % 2) + z % 2
                    values = parent(y // 2, z // 2)
                    pieces.append(values[:rows, octant * coeffs : (octant + 1) * coeffs])
        return jnp.concatenate(pieces, axis=0).astype(BF)

    middle_rows = leaf_rows // 8

    def top_of(y, z):
        at = middle_rows + (y * (size_z // 4) + z) * half
        return upper[at : at + half]

    boxes = spread(size_y // 4, size_z // 4, top_of, half // 2)
    local = upper[:middle_rows] + jnp.dot(boxes, weight, preferred_element_type=F32)

    def middle_of(y, z):
        at = (y * (size_z // 2) + z) * half
        return local[at : at + half]

    boxes = spread(size_y // 2, size_z // 2, middle_of, half)
    product = jnp.dot(boxes, weight, preferred_element_type=F32)
    lanes = turned.shape[2]
    for y in range(size_y):
        for z in range(size_z):
            at = (y * size_z + z) * size_x
            part = slice(at, at + size_x)
            rows = total[part] + widened(product[part])
            for a in range(2):
                for b in range(2):
                    piece = rows[(2 * a + b) * 8 : (2 * a + b + 1) * 8]
                    start = ((2 * b + a) * size_y + y) * size_z + z
                    for c in range(wide // lanes):
                        turned[c, pl.ds(start, 8, stride=4 * size_y * size_z), :] = piece[
                            :, c * lanes : (c + 1) * lanes
                        ]
    def write(x, carry):
        for y in range(size_y):
            at = pl.ds((x * size_y + y) * size_z, size_z)
            rows = [turned[c, at] for c in range(wide // lanes)]
            out[x, y] = jnp.concatenate(rows, axis=1)[:, :width]
        return carry

    lax.fori_loop(0, size_x, write, 0, unroll=4)


def far(odd, near, table, middle, top, halos, down):
    rows, wide = near.shape
    width = middle.shape[3]
    size_y, size_z, half = 2 * middle.shape[0], 2 * middle.shape[1], middle.shape[2]
    upper = half * ((size_y // 2) * (size_z // 2) + (size_y // 4) * (size_z // 4))
    return pl.pallas_call(
        far_kernel,
        out_shape=jax.ShapeDtypeStruct((2 * half, size_y, size_z, width), F32),
        in_specs=[pl.BlockSpec(memory_space=pltpu.SMEM)] + [WHOLE] * 10,
        out_specs=WHOLE,
        scratch_shapes=[
            pltpu.VMEM((rows, wide), F32),
            pltpu.VMEM((3, size_y + 2, size_z + 2, 2 * half, wide), BF),
            pltpu.VMEM((3, size_y // 2 + 2, size_z // 2 + 2, half, wide), BF),
            pltpu.VMEM((3, size_y // 4 + 2, size_z // 4 + 2, half, wide), BF),
            pltpu.VMEM((SLOTS, wide, wide), BF),
            pltpu.VMEM((upper, width), F32),
            pltpu.VMEM((wide // 128, rows, 128), F32),
        ],
        compiler_params=params(32),
        name="far",
    )(odd, near, table, middle, top, *halos, down)


def shards(densities, upward_weight, transfer_weight, downward_weight):
    size_x, size_y, size_z, width = densities.shape
    base = densities.reshape(size_x // 4, 2, 2, size_y, size_z, width)
    base = base.transpose(3, 4, 2, 1, 0, 5).reshape(size_y, size_z, size_x, width)
    middle, top = lifted(base, upward_weight)
    levels = [base, middle, top]
    lasts = [size_x, size_x // 2, size_x // 4]

    def packed(pieces):
        rows = jnp.concatenate([piece.reshape(-1, width) for piece in pieces], axis=0)
        return jnp.pad(rows, ((0, -rows.shape[0] % 16), (0, 0)))

    def unpacked(flat, shapes):
        pieces, at = [], 0
        for shape in shapes:
            count = 1
            for extent in shape:
                count *= extent
            pieces.append(flat[at : at + count].reshape(shape + (width,)))
            at += count
        return pieces

    low = packed([level[:, :, 0] for level in levels])
    high = packed([level[:, :, last - 1] for level, last in zip(levels, lasts)])
    first, other = exchange(low, high, "gx")
    odd = is_odd("gx")
    below_x, above_x = jnp.where(odd, first, other), jnp.where(odd, other, first)
    shapes = [level.shape[:2] for level in levels]
    sides = [
        jnp.stack(both) for both in zip(unpacked(below_x, shapes), unpacked(above_x, shapes))
    ]

    def face_z(at):
        return packed([level[:, at] for level in levels] + [side[:, :, at] for side in sides])

    def face_y(at):
        return packed([level[at] for level in levels] + [side[:, at] for side in sides])

    def corner(at_y, at_z):
        rows = [level[at_y, at_z] for level in levels] + [side[:, at_y, at_z] for side in sides]
        return packed(rows)

    low_z = face_z(0)
    got_z = jnp.stack(exchange(low_z, face_z(-1), "gz"))
    got_y = jnp.stack(exchange(face_y(0), face_y(-1), "gy"))
    got_yz = exchange_corners([[corner(y, z) for z in (0, -1)] for y in (0, -1)], "gy", "gz")
    table, near = first_part(transfer_weight, base, below_x, above_x, low_z)
    odd = jnp.stack([is_odd("gy"), is_odd("gz")]).astype(jnp.int32)
    halos = (below_x, above_x, got_z, got_y, got_yz)
    return far(odd, near, table, middle, top, halos, downward_weight)


def solution(mesh):
    placed = (P("gx", "gy", "gz", None), P(), P(), P())
    return jax.shard_map(
        shards, mesh=mesh, in_specs=placed, out_specs=P("gx", "gy", "gz", None), check_vma=False
    )
```

time: 62.4 us -> 51.6 us (0.83)
  local copies, waits for them, and re-layouts: 12.6 us -> 4.56 us
  Pallas kernels: 34 us -> 30 us
  starting transfers between devices: 11.9 us -> 14.9 us
  other arithmetic: 1.54 us -> 0.81 us
  waiting for transfers between devices: 1.25 us -> 0.57 us
    transpose x1 -> x0, local copies, waits for them, and re-layouts: 4.26 us -> none  [shards(): return result.transpose(4, 3, 2, 0, 1, 5).reshape(densities.shape)]
    pallas_call x3 -> x2, Pallas kernels: 33 us -> 28.9 us  [the longest x1 18 us: first_part(): pl.pallas_call(first_kernel, out_shape=(jax.ShapeDtypeStruct((3, 7, 7, 2...]
    unnamed x33 -> x13, local copies, waits for them, and re-layouts: 4.73 us -> 1.59 us
    ppermute x5 -> x7, starting transfers between devices: 11.9 us -> 14.9 us  [swapped(): return lax.ppermute(block, axis, both) if pairs else jnp.zeros_like(block)]
    select_n x6 -> x5, other arithmetic: 1.1 us -> 0.35 us  [the longest x2 0.24 us: exchange(): got = swapped(jnp.where(odd, low, high), axis, first)]
    ppermute x5 -> x7, waiting for transfers between devices: 1.25 us -> 0.57 us  [swapped(): return lax.ppermute(block, axis, both) if pairs else jnp.zeros_like(block)]
  transfers between devices with their start and end apart: 5 -> 7, of which waited for: 2 -> 1; matrix products, arithmetic and copies ran while one was open for 0% -> 1% of each run, Pallas kernels for 34% -> 35%
where the time goes in v3:
time: 51.6 us; the launch traced here: 51.3 us
  Pallas kernels  30 us (58%)
  starting transfers between devices  14.9 us (29%)
  local copies, waits for them, and re-layouts  4.56 us (9%)
  other arithmetic  0.81 us (2%)
  waiting for transfers between devices  0.57 us (1%)
    pallas_call x1, Pallas kernels, first_part(): pl.pallas_call(first_kernel, out_shape=(jax.ShapeDtypeStruct((3, 7, 7, 2...  18 us
    ppermute x7, starting transfers between devices, swapped(): return lax.ppermute(block, axis, both) if pairs else jnp.zeros_like(block)  14.9 us
    pallas_call x1, Pallas kernels, far(): pl.pallas_call(far_kernel, out_shape=jax.ShapeDtypeStruct((2 * half, size...  10.9 us
    reshape x1, local copies, waits for them, and re-layouts, shards(): base = densities.reshape(size_x // 4, 2, 2, size_y, size_z, width)  1.81 us
    unnamed x13, local copies, waits for them, and re-layouts  1.59 us
    pallas_call x1, Pallas kernels, lifted(): pl.pallas_call(lift_kernel, out_shape=(jax.ShapeDtypeStruct((size_y // 2,...  1.08 us
  transfers between devices with their start and end apart: 7, of which 1 were waited for; matrix products, arithmetic and copies ran while one was open for 1% of the time, Pallas kernels for 35%

profile of v3, /device:TPU:0, one launch (start us, length us, event | category | flops | bytes accessed | tf_op | source)
XLA Modules:
  0.0 51.3 jit_solution(1563307398029807897)
XLA Ops:
  0.0 1.0 %copy.41.weight = bf16[448,56]{1,0:T(8,128)(2,1)S(1)} copy(bf16[448,56]{0,1:T(8,128)(2,1)} %param.5) | data formatting | bytes 100352 | tf_op args[1]
  1.0 1.8 %copy.67 = bf16[8,2,2,8,4,448]{5,0,1,2,4,3:T(8,128)(2,1)S(1)} copy(bf16[8,2,2,8,4,448]{5,4,3,2,1,0:T(4,128)(2,1)} %bitcast.99) | data formatting | bytes 1835008 | tf_op jit(solution)/shard_map/reshape | solution.py:452
  2.8 0.3 slice_reduce_fusion.1
  3.1 1.1 %lift.1 = (bf16[4,2,16,448]{3,2,1,0:T(8,128)(2,1)S(1)}, bf16[2,1,16,448]{3,2,1,0:T(8,128)(2,1)S(1)}) custom-call(bf16[8,4,32,448]{3,2,1,0:T(8,128)(2,1)S(1)} %bitcast.91, bf16[448,56]{1,0:T(8,128)(2,1)S(1)} %copy.41.weight), custom_call_target="tpu_custom_call" | custom-call | tf_op jit(solution)/shard_map/lift/pallas_call | solution.py:98
  4.2 0.1 slice_reduce_fusion.3
  4.4 0.7 %collective-permute-start.1 = (bf16[48,448]{1,0:T(8,128)(2,1)S(1)}, bf16[48,448]{1,0:T(8,128)(2,1)S(1)}, u32[]{:S(2)}, u32[]{:S(2)}) collective-permute-start(bf16[48,448]{1,0:T(8,128)(2,1)S(1)} %get-tuple-element.50), channel_id=1, source_target_pairs={{8,16},{16,8},{9,17},{17,9},{10,18},{18,10},{11,19},{19,11},{12,20... | collective-permute-start | bytes 129032 | tf_op jit(solution)/shard_map/ppermute | solution.py:28
  5.1 4.4 %collective-permute-start = (bf16[48,448]{1,0:T(8,128)(2,1)S(1)}, bf16[48,448]{1,0:T(8,128)(2,1)S(1)}, u32[]{:S(2)}, u32[]{:S(2)}) collective-permute-start(bf16[48,448]{1,0:T(8,128)(2,1)S(1)} %get-tuple-element.51), channel_id=1, source_target_pairs={{0,8},{16,24},{8,0},{24,16},{1,9},{17,25},{9,1},{25,17},{2,10},{18... | collective-permute-start | bytes 129032 | tf_op jit(solution)/shard_map/ppermute | solution.py:28
  9.7 0.1 add_convert_fusion.odd
  9.8 0.0 collective-permute-done.1
  9.8 0.6 %collective-permute-done = bf16[48,448]{1,0:T(8,128)(2,1)S(1)} collective-permute-done((bf16[48,448]{1,0:T(8,128)(2,1)S(1)}, bf16[48,448]{1,0:T(8,128)(2,1)S(1)}, u32[]{:S(2)}, u32[]{:S(2)}) %collective-permute-start) | collective-permute-done | bytes 43040 | tf_op jit(solution)/shard_map/ppermute | solution.py:28
  10.8 0.1 slice_maximum_fusion
  11.2 0.1 select_select_fusion.1
  11.3 2.6 %collective-permute-start.5 = (bf16[80,448]{1,0:T(8,128)(2,1)S(1)}, bf16[80,448]{1,0:T(8,128)(2,1)S(1)}, u32[]{:S(2)}, u32[]{:S(2)}) collective-permute-start(bf16[80,448]{1,0:T(8,128)(2,1)S(1)} %get-tuple-element.31), channel_id=1, source_target_pairs={{0,3},{1,2},{4,7},{5,6},{3,0},{2,1},{7,4},{6,5},{8,11},{9,10},{12,... | collective-permute-start | bytes 215048 | tf_op jit(solution)/shard_map/ppermute | solution.py:28
  13.9 0.7 %collective-permute-start.6 = (bf16[80,448]{1,0:T(8,128)(2,1)S(1)}, bf16[80,448]{1,0:T(8,128)(2,1)S(1)}, u32[]{:S(2)}, u32[]{:S(2)}) collective-permute-start(bf16[80,448]{1,0:T(8,128)(2,1)S(1)} %get-tuple-element.32), channel_id=1, source_target_pairs={{2,5},{3,4},{5,2},{4,3},{10,13},{11,12},{13,10},{12,11},{18,21},{1... | collective-permute-start | bytes 215048 | tf_op jit(solution)/shard_map/ppermute | solution.py:28
  14.6 0.0 copy-start.1
  14.6 0.1 broadcast_select_fusion.1
  14.7 4.4 %collective-permute-start.3 = (bf16[192,448]{1,0:T(8,128)(2,1)S(1)}, bf16[192,448]{1,0:T(8,128)(2,1)S(1)}, u32[]{:S(2)}, u32[]{:S(2)}) collective-permute-start(bf16[192,448]{1,0:T(8,128)(2,1)S(1)} %get-tuple-element.27), channel_id=1, source_target_pairs={{0,2},{4,6},{2,0},{6,4},{1,3},{5,7},{3,1},{7,5},{8,10},{12,14},{10... | collective-permute-start | bytes 516104 | tf_op jit(solution)/shard_map/ppermute | solution.py:28
  19.1 0.7 %collective-permute-start.4 = (bf16[192,448]{1,0:T(8,128)(2,1)S(1)}, bf16[192,448]{1,0:T(8,128)(2,1)S(1)}, u32[]{:S(2)}, u32[]{:S(2)}) collective-permute-start(bf16[192,448]{1,0:T(8,128)(2,1)S(1)} %get-tuple-element.28), channel_id=1, source_target_pairs={{2,4},{4,2},{3,5},{5,3},{10,12},{12,10},{11,13},{13,11},{18,20},{2... | collective-permute-start | bytes 516104 | tf_op jit(solution)/shard_map/ppermute | solution.py:28
  19.9 0.2 pad_select_fusion
  20.0 1.6 %collective-permute-start.2 = (bf16[384,448]{1,0:T(8,128)(2,1)S(1)}, bf16[384,448]{1,0:T(8,128)(2,1)S(1)}, u32[]{:S(2)}, u32[]{:S(2)}) collective-permute-start(bf16[384,448]{1,0:T(8,128)(2,1)S(1)} %get-tuple-element.29), channel_id=1, source_target_pairs={{0,1},{1,0},{2,3},{3,2},{4,5},{5,4},{6,7},{7,6},{8,9},{9,8},{10,11... | collective-permute-start | bytes 1032200 | tf_op jit(solution)/shard_map/ppermute | solution.py:28
  21.6 0.0 copy-done.1
  21.6 18.0 %first.1 = (bf16[3,7,7,112,112]{4,3,2,1,0:T(8,128)(2,1)S(1)}, f32[1024,512]{1,0:T(8,128)S(1)}) custom-call(bf16[56,56,316]{2,1,0:T(8,128)(2,1)S(1)} %bitcast.98, bf16[8,4,32,448]{3,2,1,0:T(8,128)(2,1)S(1)} %bitcast.95, bf16[48,448]{1,0:T(8,128)(2,1)S(1)} %get-tuple-element.49.below.below_x, bf16[48,448]{1,0:T(8,128)(2,1)S(1)} %get-tuple-element.48.above.above_x, ...), custom_call_target="tpu_custom_call" | custom-call | flops 20000000000 | bytes 10000000 | tf_op jit(solution)/shard_map/first/pallas_call | solution.py:262
  39.6 0.0 copy-start
  39.6 0.0 collective-permute-done.5
  39.7 0.0 collective-permute-done.6
  39.7 0.1 pad_maximum_fusion.1
  39.7 0.0 collective-permute-done.3
  39.8 0.0 collective-permute-done.4
  39.8 0.0 collective-permute-done.2
  39.8 0.1 stack.49.got_z
  39.9 0.6 %copy-done = bf16[56,448]{1,0:T(8,128)(2,1)S(1)} copy-done((bf16[56,448]{1,0:T(8,128)(2,1)S(1)}, bf16[56,448]{1,0:T(8,128)(2,1)}, u32[]{:S(2)}) %copy-start) | copy-done | bytes 50200
  40.5 10.9 %far.1 = f32[32,8,4,448]{3,2,1,0:T(4,128)} custom-call(s32[2]{0:T(128)S(1)} %add_convert_fusion.odd, f32[1024,512]{1,0:T(8,128)S(1)} %get-tuple-element.11.near, bf16[3,7,7,112,112]{4,3,2,1,0:T(8,128)(2,1)S(1)} %get-tuple-element.12.table, bf16[4,2,16,448]{3,2,1,0:T(8,128)(2,1)S(1)} %get-tuple-element.9.middle, ...), custom_call_target="tpu_custom_call" | custom-call | tf_op jit(solution)/shard_map/far/pallas_call | solution.py:431
  (63 shorter events, 1.1 us)
Async XLA Ops:
  4.4 5.4 %collective-permute-start.1 = (bf16[48,448]{1,0:T(8,128)(2,1)S(1)}, bf16[48,448]{1,0:T(8,128)(2,1)S(1)}, u32[]{:S(2)}, u32[]{:S(2)}) collective-permute-start(bf16[48,448]{1,0:T(8,128)(2,1)S(1)} %get-tuple-element.50), channel_id=1, source_target_pairs={{8,16},{16,8},{9,17},{17,9},{10,18},{18,10},{11,19},{19,11},{12,20... | collective-permute-start | bytes 129032 | tf_op jit(solution)/shard_map/ppermute | solution.py:28
  5.1 5.2 %collective-permute-start = (bf16[48,448]{1,0:T(8,128)(2,1)S(1)}, bf16[48,448]{1,0:T(8,128)(2,1)S(1)}, u32[]{:S(2)}, u32[]{:S(2)}) collective-permute-start(bf16[48,448]{1,0:T(8,128)(2,1)S(1)} %get-tuple-element.51), channel_id=1, source_target_pairs={{0,8},{16,24},{8,0},{24,16},{1,9},{17,25},{9,1},{25,17},{2,10},{18... | collective-permute-start | bytes 129032 | tf_op jit(solution)/shard_map/ppermute | solution.py:28
  11.3 28.3 %collective-permute-start.5 = (bf16[80,448]{1,0:T(8,128)(2,1)S(1)}, bf16[80,448]{1,0:T(8,128)(2,1)S(1)}, u32[]{:S(2)}, u32[]{:S(2)}) collective-permute-start(bf16[80,448]{1,0:T(8,128)(2,1)S(1)} %get-tuple-element.31), channel_id=1, source_target_pairs={{0,3},{1,2},{4,7},{5,6},{3,0},{2,1},{7,4},{6,5},{8,11},{9,10},{12,... | collective-permute-start | bytes 215048 | tf_op jit(solution)/shard_map/ppermute | solution.py:28
  13.9 25.8 %collective-permute-start.6 = (bf16[80,448]{1,0:T(8,128)(2,1)S(1)}, bf16[80,448]{1,0:T(8,128)(2,1)S(1)}, u32[]{:S(2)}, u32[]{:S(2)}) collective-permute-start(bf16[80,448]{1,0:T(8,128)(2,1)S(1)} %get-tuple-element.32), channel_id=1, source_target_pairs={{2,5},{3,4},{5,2},{4,3},{10,13},{11,12},{13,10},{12,11},{18,21},{1... | collective-permute-start | bytes 215048 | tf_op jit(solution)/shard_map/ppermute | solution.py:28
  14.6 7.0 %copy-start.1 = (bf16[316,56,56]{0,2,1:T(8,128)(2,1)S(1)}, bf16[316,56,56]{0,2,1:T(8,128)(2,1)}, u32[]{:S(2)}) copy-start(bf16[316,56,56]{0,2,1:T(8,128)(2,1)} %param.6) | copy-start | bytes 5945860
  14.7 25.0 %collective-permute-start.3 = (bf16[192,448]{1,0:T(8,128)(2,1)S(1)}, bf16[192,448]{1,0:T(8,128)(2,1)S(1)}, u32[]{:S(2)}, u32[]{:S(2)}) collective-permute-start(bf16[192,448]{1,0:T(8,128)(2,1)S(1)} %get-tuple-element.27), channel_id=1, source_target_pairs={{0,2},{4,6},{2,0},{6,4},{1,3},{5,7},{3,1},{7,5},{8,10},{12,14},{10... | collective-permute-start | bytes 516104 | tf_op jit(solution)/shard_map/ppermute | solution.py:28
  19.1 20.6 %collective-permute-start.4 = (bf16[192,448]{1,0:T(8,128)(2,1)S(1)}, bf16[192,448]{1,0:T(8,128)(2,1)S(1)}, u32[]{:S(2)}, u32[]{:S(2)}) collective-permute-start(bf16[192,448]{1,0:T(8,128)(2,1)S(1)} %get-tuple-element.28), channel_id=1, source_target_pairs={{2,4},{4,2},{3,5},{5,3},{10,12},{12,10},{11,13},{13,11},{18,20},{2... | collective-permute-start | bytes 516104 | tf_op jit(solution)/shard_map/ppermute | solution.py:28
  20.0 19.8 %collective-permute-start.2 = (bf16[384,448]{1,0:T(8,128)(2,1)S(1)}, bf16[384,448]{1,0:T(8,128)(2,1)S(1)}, u32[]{:S(2)}, u32[]{:S(2)}) collective-permute-start(bf16[384,448]{1,0:T(8,128)(2,1)S(1)} %get-tuple-element.29), channel_id=1, source_target_pairs={{0,1},{1,0},{2,3},{3,2},{4,5},{5,4},{6,7},{7,6},{8,9},{9,8},{10,11... | collective-permute-start | bytes 1032200 | tf_op jit(solution)/shard_map/ppermute | solution.py:28
  39.6 0.8 %copy-start = (bf16[56,448]{1,0:T(8,128)(2,1)S(1)}, bf16[56,448]{1,0:T(8,128)(2,1)}, u32[]{:S(2)}) copy-start(bf16[56,448]{1,0:T(8,128)(2,1)} %down.1) | copy-start | bytes 150532

commit v4 on v3

--- a/solution.py
+++ b/solution.py
@@ -58,57 +58,73 @@
     return jnp.stack(result).reshape(2, 2, *result[0].shape)
 
 
-def lift_kernel(base, weight, middle, top):
+def lift_kernel(base, weight, middle, top, low, high):
     size_y, size_z, size_x, width = base.shape
     half, part = size_x // 2, size_x // 4
-    coeffs = weight.shape[1]
     up = weight[...]
 
     def lift(rows):
-        return jnp.dot(rows, up, preferred_element_type=F32).astype(BF).astype(F32)
+        product = lax.dot_general(rows, up, (((1,), (1,)), ((), ())), preferred_element_type=F32)
+        return product.astype(BF).astype(F32)
+
+    lows, highs = [], []
+
+    def ends(rows):
+        lows.append(rows[:1])
+        highs.append(rows[rows.shape[0] - 1 :])
 
     boxes = {}
     for y in range(size_y):
         for z in range(size_z):
-            boxes[y, z] = lift(base[y, z])
+            rows = base[y, z]
+            boxes[y, z] = lift(rows)
+            ends(rows.astype(F32))
+
+    def grouped(boxes, y, z, rows):
+        pieces = []
+        for u in range(2):
+            for v in range(2):
+                for w in range(2):
+                    pieces.append(boxes[2 * y + v, 2 * z + w][u * rows : (u + 1) * rows])
+        return jnp.concatenate(pieces, axis=1)
+
     coarse = {}
     for y in range(size_y // 2):
         for z in range(size_z // 2):
-            pieces = []
-            for u in range(2):
-                for v in range(2):
-                    for w in range(2):
-                        pieces.append(boxes[2 * y + v, 2 * z + w][u * half : (u + 1) * half])
-            group = jnp.concatenate(pieces, axis=1).astype(BF)
-            middle[y, z] = group
-            coarse[y, z] = lift(group)
+            group = grouped(boxes, y, z, half)
+            ends(group)
+            middle[y, z] = group.astype(BF)
+            coarse[y, z] = lift(group.astype(BF))
     for y in range(size_y // 4):
         for z in range(size_z // 4):
-            pieces = []
-            for u in range(2):
-                for v in range(2):
-                    for w in range(2):
-                        pieces.append(coarse[2 * y + v, 2 * z + w][u * part : (u + 1) * part])
-            group = jnp.concatenate(pieces, axis=1)
+            group = grouped(coarse, y, z, part)
+            ends(group)
             top[y, z] = jnp.concatenate([group, jnp.zeros_like(group)], axis=0).astype(BF)
+    fill = [jnp.zeros((-len(lows) % 16, width), F32)]
+    low[...] = jnp.concatenate(lows + fill, axis=0).astype(BF)
+    high[...] = jnp.concatenate(highs + fill, axis=0).astype(BF)
 
 
 def lifted(base, upward_weight):
     size_y, size_z, size_x, width = base.shape
+    count = size_y * size_z + (size_y // 2) * (size_z // 2) + (size_y // 4) * (size_z // 4)
+    ends = jax.ShapeDtypeStruct((-(-count // 16) * 16, width), BF)
     return pl.pallas_call(
         lift_kernel,
         out_shape=(
             jax.ShapeDtypeStruct((size_y // 2, size_z // 2, size_x // 2, width), BF),
             jax.ShapeDtypeStruct((size_y // 4, size_z // 4, size_x // 2, width), BF),
+            ends,
+            ends,
         ),
-        in_specs=[WHOLE, WHOLE],
-        out_specs=(WHOLE, WHOLE),
+        in_specs=[WHOLE] * 2,
+        out_specs=(WHOLE,) * 4,
         compiler_params=params(24),
         name="lift",
-    )(base, upward_weight)
-
-
-def fill_table(weight, arriving, table, blocks):
+    )(base, upward_weight.T)
+
+
+def turn_operators(weight, arriving, blocks):
     coeffs, _, count = weight.shape
     lanes, batch = 128, coeffs // len(arriving)
 
@@ -124,32 +140,23 @@
         copy.wait()
         lax.fori_loop(i * batch, (i + 1) * batch, turn, 0, unroll=4)
 
-    def one(position, carry):
-        first = position // 7
-        second = position % 7
-        mid_first = jnp.logical_and(first >= 2, first <= 4)
-        mid = jnp.logical_and(mid_first, jnp.logical_and(second >= 2, second <= 4))
-        skipped = 9 * jnp.clip(first - 2, 0, 3) + jnp.where(
-            mid_first, 3 * jnp.clip(second - 2, 0, 3), 0
-        )
-        start = 7 * position - skipped
-        found = []
-        for third in range(7):
-            near = third in (2, 3, 4)
-            if near:
-                place = jnp.where(mid, 0, start + third)
-            else:
-                place = start + third - jnp.where(mid, min(max(third - 2, 0), 3), 0)
-            block = blocks[pl.ds(pl.multiple_of(place * coeffs, 8), coeffs)]
-            found.append(jnp.where(mid, 0.0, block) if near else block)
-        moved = [pltpu.roll(block, coeffs, 1) for block in found[:6]]
-        for third in range(3):
-            rows = [found[2 * third + s + 1] + moved[2 * third + s] for s in range(2)]
-            rows = jnp.concatenate(rows, axis=0)
-            table[third, first, second] = rows[:, : 2 * coeffs].astype(BF)
-        return carry
-
-    lax.fori_loop(0, 49, one, 0, unroll=7)
+
+def fill_entry(blocks, table, first, second, third, coeffs):
+    def found(at):
+        spot = (first, second, at)
+        if all(2 <= i <= 4 for i in spot):
+            return jnp.zeros((coeffs, blocks.shape[1]), F32)
+        before = 0
+        for i in range(spot[0] * 49 + spot[1] * 7 + at):
+            before += not all(2 <= j <= 4 for j in (i // 49, i // 7 % 7, i % 7))
+        return blocks[before * coeffs : (before + 1) * coeffs]
+
+    rows = []
+    for s in range(2):
+        at = 2 * third + s
+        rows.append(found(at + 1) + pltpu.roll(found(at), coeffs, 1))
+    rows = jnp.concatenate(rows, axis=0)
+    table[third, first, second] = rows[:, : 2 * coeffs].astype(BF)
 
 
 SLOTS = 8
@@ -212,7 +219,7 @@
     return kernels[slot]
 
 
-def add_near(slots, table, leaf, below, above, leaves, kernels, total, ready=None):
+def add_near(prepare, table, leaf, below, above, leaves, kernels, total):
     size_y, size_z, size_x, width = leaf.shape
     low = below[: size_y * size_z].astype(F32)
     high = above[: size_y * size_z].astype(F32)
@@ -220,12 +227,8 @@
         for z in range(size_z):
             at = y * size_z + z
             store_moved(leaf[y, z], low[at : at + 1], high[at : at + 1], leaves, y, z)
-    if slots[0] > 0:
-        total[...] = jnp.zeros_like(total)
-    for slot in slots:
-        dx, dy, dz = SHIFTS[slot]
-        if ready is not None:
-            ready(dz)
+    for slot, (dx, dy, dz) in enumerate(SHIFTS):
+        prepare(dx, dy, dz)
         kernel = operator(table, (dx, dy, dz), kernels, slot)
         first_z, last_z = max(0, 1 - dz), size_z - max(0, dz - 1)
         first_y, last_y = max(0, 1 - dy), size_y - max(0, dy - 1)
@@ -251,8 +254,19 @@
         part = pl.ds(i * batch, batch)
         arriving.append(pltpu.make_async_copy(given.at[part], weight.at[part], arrived.at[i]))
         arriving[i].start()
-    fill_table(weight, arriving, table, blocks)
-    add_near(range(len(SHIFTS)), table, leaf, below, above, leaves, kernels, total)
+    turn_operators(weight, arriving, blocks)
+    done = set()
+
+    def prepare(dx, dy, dz):
+        for first in range(2 * dx, 2 * dx + 3):
+            for second in range(2 * dy, 2 * dy + 3):
+                if (dz, first, second) not in done:
+                    done.add((dz, first, second))
+                    fill_entry(blocks, table, first, second, dz, coeffs)
+
+    add_near(prepare, table, leaf, below, above, leaves, kernels, total)
+    for dx, dy, dz in [(dx, dy, dz) for dx in range(3) for dy in range(3) for dz in range(3)]:
+        prepare(dx, dy, dz)
 
 
 def first_part(transfer_weight, leaf, below, above, after):
@@ -282,7 +296,7 @@
 
 def far_kernel(
     odd, near, table, middle, top, below_x, above_x, got_z, got_y, got_yz, down, out,
-    total, leaves, middles, tops, kernels, upper, turned,
+    total, leaves, middles, tops, kernels, upper, out_rows, sent,
 ):
     size_y, size_z = 2 * middle.shape[0], 2 * middle.shape[1]
     half, width = middle.shape[2:]
@@ -351,26 +365,18 @@
                 rows = rows[: half // 2]
             store_moved(rows, low, high, copies[level], y, z, level == 2)
 
-    total[...] = near[...]
     leaf_rows = size_y * size_z * size_x
     wide = kernels.shape[1]
+    made = []
     for slot, (dx, dy, dz) in enumerate(SHIFTS):
-        kernel = operator(table, (dx, dy, dz), kernels, slot)
-        places, rows = [], []
-        for y in range(size_y):
-            for z in range(size_z):
-                if y + dy in (0, size_y + 1) or z + dz in (0, size_z + 1):
-                    places.append((y * size_z + z) * size_x)
-                    rows.append(leaves[dx, y + dy, z + dz])
-        rows += [
+        made.append(operator(table, (dx, dy, dz), kernels, slot))
+        rows = [
             middles[dx, dy : dy + size_y // 2, dz : dz + size_z // 2].reshape(-1, wide),
             tops[dx, dy : dy + size_y // 4, dz : dz + size_z // 4].reshape(-1, wide),
         ]
-        product = jnp.dot(jnp.concatenate(rows, axis=0), kernel, preferred_element_type=F32)
-        for i, at in enumerate(places):
-            total[at : at + size_x] += product[i * size_x : (i + 1) * size_x]
-        rest = product[len(places) * size_x :, :width]
-        upper[...] = rest if slot == 0 else upper[...] + rest
+        rows = jnp.concatenate(rows, axis=0)
+        product = jnp.dot(rows, made[slot], preferred_element_type=F32)[:, :width]
+        upper[...] = product if slot == 0 else upper[...] + product
 
     weight = down[...]
 
@@ -398,29 +404,67 @@
         return local[at : at + half]
 
     boxes = spread(size_y // 2, size_z // 2, middle_of, half)
-    product = jnp.dot(boxes, weight, preferred_element_type=F32)
-    lanes = turned.shape[2]
-    for y in range(size_y):
-        for z in range(size_z):
-            at = (y * size_z + z) * size_x
-            part = slice(at, at + size_x)
-            rows = total[part] + widened(product[part])
-            for a in range(2):
-                for b in range(2):
-                    piece = rows[(2 * a + b) * 8 : (2 * a + b + 1) * 8]
-                    start = ((2 * b + a) * size_y + y) * size_z + z
-                    for c in range(wide // lanes):
-                        turned[c, pl.ds(start, 8, stride=4 * size_y * size_z), :] = piece[
-                            :, c * lanes : (c + 1) * lanes
-                        ]
-    def write(x, carry):
-        for y in range(size_y):
-            at = pl.ds((x * size_y + y) * size_z, size_z)
-            rows = [turned[c, at] for c in range(wide // lanes)]
-            out[x, y] = jnp.concatenate(rows, axis=1)[:, :width]
-        return carry
-
-    lax.fori_loop(0, size_x, write, 0, unroll=4)
+    part_x = half // 2
+    step = size_z * size_x
+    touched = set()
+
+    def finish(y):
+        part = slice(y * step, (y + 1) * step)
+        product = []
+
+        def add(z):
+            if not product:
+                product.append(jnp.dot(boxes[part], weight, preferred_element_type=F32))
+            at = z * size_x
+            here = slice(y * step + at, y * step + at + size_x)
+            source = total if here.start in touched else near
+            rows = source[here] + widened(product[0][at : at + size_x])
+            for i in range(size_x):
+                a, b, x = i // half, i // part_x % 2, i % part_x
+                out_rows[4 * x + 2 * b + a, y, z : z + 1] = rows[i : i + 1, :width]
+
+        return [functools.partial(add, z) for z in range(size_z)]
+
+    leaving = []
+
+    def leave(ys):
+        rows = pl.ds(ys.start, len(ys))
+        copy = pltpu.make_async_copy(out_rows.at[:, rows], out.at[:, rows], sent.at[len(leaving)])
+        copy.start()
+        leaving.append(copy)
+
+    steps = []
+    halves = [range(0, size_y // 2), range(size_y // 2, size_y)]
+    for ys in halves:
+        count = -(-len(steps) // (len(SHIFTS) - 2))
+        for slot, (dx, dy, dz) in enumerate(SHIFTS):
+            places, rows = [], []
+            for y in ys:
+                for z in range(size_z):
+                    if y + dy in (0, size_y + 1) or z + dz in (0, size_z + 1):
+                        places.append((y * size_z + z) * size_x)
+                        rows.append(leaves[dx, y + dy, z + dz])
+            if rows:
+                rows = jnp.concatenate(rows, axis=0)
+                product = jnp.dot(rows, kernels[slot], preferred_element_type=F32)
+                for i, at in enumerate(places):
+                    source = total if at in touched else near
+                    touched.add(at)
+                    total[at : at + size_x] = (
+                        source[at : at + size_x] + product[i * size_x : (i + 1) * size_x]
+                    )
+            for one in steps[:count]:
+                one()
+            steps = steps[count:]
+        assert not steps
+        if ys is not halves[0]:
+            leave(halves[0])
+        steps = [one for y in ys for one in finish(y)]
+    for one in steps:
+        one()
+    leave(halves[1])
+    for copy in leaving:
+        copy.wait()
 
 
 def far(odd, near, table, middle, top, halos, down):
@@ -432,17 +476,18 @@
         far_kernel,
         out_shape=jax.ShapeDtypeStruct((2 * half, size_y, size_z, width), F32),
         in_specs=[pl.BlockSpec(memory_space=pltpu.SMEM)] + [WHOLE] * 10,
-        out_specs=WHOLE,
+        out_specs=HBM,
         scratch_shapes=[
             pltpu.VMEM((rows, wide), F32),
             pltpu.VMEM((3, size_y + 2, size_z + 2, 2 * half, wide), BF),
             pltpu.VMEM((3, size_y // 2 + 2, size_z // 2 + 2, half, wide), BF),
             pltpu.VMEM((3, size_y // 4 + 2, size_z // 4 + 2, half, wide), BF),
-            pltpu.VMEM((SLOTS, wide, wide), BF),
+            pltpu.VMEM((len(SHIFTS), wide, wide), BF),
             pltpu.VMEM((upper, width), F32),
-            pltpu.VMEM((wide // 128, rows, 128), F32),
+            pltpu.VMEM((2 * half, size_y, size_z, width), F32),
+            pltpu.SemaphoreType.DMA((2,)),
         ],
-        compiler_params=params(32),
+        compiler_params=params(42),
         name="far",
     )(odd, near, table, middle, top, *halos, down)
 
@@ -451,9 +496,8 @@
     size_x, size_y, size_z, width = densities.shape
     base = densities.reshape(size_x // 4, 2, 2, size_y, size_z, width)
     base = base.transpose(3, 4, 2, 1, 0, 5).reshape(size_y, size_z, size_x, width)
-    middle, top = lifted(base, upward_weight)
+    middle, top, low, high = lifted(base, upward_weight)
     levels = [base, middle, top]
-    lasts = [size_x, size_x // 2, size_x // 4]
 
     def packed(pieces):
         rows = jnp.concatenate([piece.reshape(-1, width) for piece in pieces], axis=0)
@@ -469,8 +513,6 @@
             at += count
         return pieces
 
-    low = packed([level[:, :, 0] for level in levels])
-    high = packed([level[:, :, last - 1] for level, last in zip(levels, lasts)])
     first, other = exchange(low, high, "gx")
     odd = is_odd("gx")
     below_x, above_x = jnp.where(odd, first, other), jnp.where(odd, other, first)

time: 51.6 us -> 46.5 us (0.901)
  Pallas kernels: 30 us -> 25.3 us
  local copies, waits for them, and re-layouts: 4.56 us -> 3.9 us
    pallas_call x1, Pallas kernels: 18 us -> 15.6 us  [first_part(): pl.pallas_call(first_kernel, out_shape=(jax.ShapeDtypeStruct((3, 7, 7, 2...]
    pallas_call x1, Pallas kernels: 10.9 us -> 8.79 us  [far(): pl.pallas_call(far_kernel, out_shape=jax.ShapeDtypeStruct((2 * half, size...]
    unnamed x13 -> x14, local copies, waits for them, and re-layouts: 1.59 us -> 1.45 us
  transfers between devices with their start and end apart: 7 -> 7, of which waited for: 1 -> 1; matrix products, arithmetic and copies ran while one was open for 1% -> 1% of each run, Pallas kernels for 35% -> 34%
where the time goes in v4:
time: 46.5 us; the launch traced here: 46.2 us
  Pallas kernels  25.3 us (54%)
  starting transfers between devices  14.9 us (32%)
  local copies, waits for them, and re-layouts  3.9 us (8%)
  other arithmetic  0.8 us (2%)
  between operations  0.64 us (1%)
  waiting for transfers between devices  0.56 us (1%)
    pallas_call x1, Pallas kernels, first_part(): pl.pallas_call(first_kernel, out_shape=(jax.ShapeDtypeStruct((3, 7, 7, 2...  15.6 us
    ppermute x7, starting transfers between devices, swapped(): return lax.ppermute(block, axis, both) if pairs else jnp.zeros_like(block)  14.9 us
    pallas_call x1, Pallas kernels, far(): pl.pallas_call(far_kernel, out_shape=jax.ShapeDtypeStruct((2 * half, size...  8.79 us
    reshape x1, local copies, waits for them, and re-layouts, shards(): base = densities.reshape(size_x // 4, 2, 2, size_y, size_z, width)  1.8 us
    unnamed x14, local copies, waits for them, and re-layouts  1.45 us
    pallas_call x1, Pallas kernels, lifted(): pl.pallas_call(lift_kernel, out_shape=(jax.ShapeDtypeStruct((size_y // 2,...  0.94 us
  transfers between devices with their start and end apart: 7, of which 1 were waited for; matrix products, arithmetic and copies ran while one was open for 1% of the time, Pallas kernels for 34%

profile of v4, /device:TPU:0, one launch (start us, length us, event | category | flops | bytes accessed | tf_op | source)
XLA Modules:
  0.0 46.2 jit_solution(17945355021694409749)
XLA Ops:
  0.0 1.8 %copy.54 = bf16[8,2,2,8,4,448]{5,0,1,2,4,3:T(8,128)(2,1)S(1)} copy(bf16[8,2,2,8,4,448]{5,4,3,2,1,0:T(4,128)(2,1)} %bitcast.96) | data formatting | bytes 1835008 | tf_op jit(solution)/shard_map/reshape | solution.py:497
  1.8 0.0 copy-start
  1.8 0.8 %copy-done = bf16[448,56]{0,1:T(8,128)(2,1)S(1)} copy-done((bf16[448,56]{0,1:T(8,128)(2,1)S(1)}, bf16[448,56]{0,1:T(8,128)(2,1)}, u32[]{:S(2)}) %copy-start) | copy-done | bytes 50200
  2.6 0.9 %lift.1 = (bf16[4,2,16,448]{3,2,1,0:T(8,128)(2,1)S(1)}, bf16[2,1,16,448]{3,2,1,0:T(8,128)(2,1)S(1)}, bf16[48,448]{1,0:T(8,128)(2,1)S(1)}, bf16[48,448]{1,0:T(8,128)(2,1)S(1)}) custom-call(bf16[8,4,32,448]{3,2,1,0:T(8,128)(2,1)S(1)} %bitcast.87, bf16[56,448]{1,0:T(8,128)(2,1)S(1)} %bitcast.94), custom_call_target="tpu_custom_call" | custom-call | tf_op jit(solution)/shard_map/lift/pallas_call | solution.py:112
  3.6 0.7 %collective-permute-start.1 = (bf16[48,448]{1,0:T(8,128)(2,1)S(1)}, bf16[48,448]{1,0:T(8,128)(2,1)S(1)}, u32[]{:S(2)}, u32[]{:S(2)}) collective-permute-start(bf16[48,448]{1,0:T(8,128)(2,1)S(1)} %get-tuple-element.50), channel_id=1, source_target_pairs={{8,16},{16,8},{9,17},{17,9},{10,18},{18,10},{11,19},{19,11},{12,20... | collective-permute-start | bytes 129032 | tf_op jit(solution)/shard_map/ppermute | solution.py:28
  4.3 4.4 %collective-permute-start = (bf16[48,448]{1,0:T(8,128)(2,1)S(1)}, bf16[48,448]{1,0:T(8,128)(2,1)S(1)}, u32[]{:S(2)}, u32[]{:S(2)}) collective-permute-start(bf16[48,448]{1,0:T(8,128)(2,1)S(1)} %get-tuple-element.51), channel_id=1, source_target_pairs={{0,8},{16,24},{8,0},{24,16},{1,9},{17,25},{9,1},{25,17},{2,10},{18... | collective-permute-start | bytes 129032 | tf_op jit(solution)/shard_map/ppermute | solution.py:28
  8.9 0.1 add_convert_fusion.odd
  9.0 0.0 collective-permute-done.1
  9.0 0.5 %collective-permute-done = bf16[48,448]{1,0:T(8,128)(2,1)S(1)} collective-permute-done((bf16[48,448]{1,0:T(8,128)(2,1)S(1)}, bf16[48,448]{1,0:T(8,128)(2,1)S(1)}, u32[]{:S(2)}, u32[]{:S(2)}) %collective-permute-start) | collective-permute-done | bytes 43040 | tf_op jit(solution)/shard_map/ppermute | solution.py:28
  10.0 0.1 slice_maximum_fusion
  10.4 0.1 select_select_fusion.1
  10.5 2.6 %collective-permute-start.5 = (bf16[80,448]{1,0:T(8,128)(2,1)S(1)}, bf16[80,448]{1,0:T(8,128)(2,1)S(1)}, u32[]{:S(2)}, u32[]{:S(2)}) collective-permute-start(bf16[80,448]{1,0:T(8,128)(2,1)S(1)} %get-tuple-element.31), channel_id=1, source_target_pairs={{0,3},{1,2},{4,7},{5,6},{3,0},{2,1},{7,4},{6,5},{8,11},{9,10},{12,... | collective-permute-start | bytes 215048 | tf_op jit(solution)/shard_map/ppermute | solution.py:28
  13.1 0.7 %collective-permute-start.6 = (bf16[80,448]{1,0:T(8,128)(2,1)S(1)}, bf16[80,448]{1,0:T(8,128)(2,1)S(1)}, u32[]{:S(2)}, u32[]{:S(2)}) collective-permute-start(bf16[80,448]{1,0:T(8,128)(2,1)S(1)} %get-tuple-element.32), channel_id=1, source_target_pairs={{2,5},{3,4},{5,2},{4,3},{10,13},{11,12},{13,10},{12,11},{18,21},{1... | collective-permute-start | bytes 215048 | tf_op jit(solution)/shard_map/ppermute | solution.py:28
  13.8 0.0 copy-start.2
  13.8 0.1 broadcast_select_fusion.1
  13.9 4.4 %collective-permute-start.3 = (bf16[192,448]{1,0:T(8,128)(2,1)S(1)}, bf16[192,448]{1,0:T(8,128)(2,1)S(1)}, u32[]{:S(2)}, u32[]{:S(2)}) collective-permute-start(bf16[192,448]{1,0:T(8,128)(2,1)S(1)} %get-tuple-element.27), channel_id=1, source_target_pairs={{0,2},{4,6},{2,0},{6,4},{1,3},{5,7},{3,1},{7,5},{8,10},{12,14},{10... | collective-permute-start | bytes 516104 | tf_op jit(solution)/shard_map/ppermute | solution.py:28
  18.3 0.7 %collective-permute-start.4 = (bf16[192,448]{1,0:T(8,128)(2,1)S(1)}, bf16[192,448]{1,0:T(8,128)(2,1)S(1)}, u32[]{:S(2)}, u32[]{:S(2)}) collective-permute-start(bf16[192,448]{1,0:T(8,128)(2,1)S(1)} %get-tuple-element.28), channel_id=1, source_target_pairs={{2,4},{4,2},{3,5},{5,3},{10,12},{12,10},{11,13},{13,11},{18,20},{2... | collective-permute-start | bytes 516104 | tf_op jit(solution)/shard_map/ppermute | solution.py:28
  19.0 0.2 pad_select_fusion
  19.2 1.6 %collective-permute-start.2 = (bf16[384,448]{1,0:T(8,128)(2,1)S(1)}, bf16[384,448]{1,0:T(8,128)(2,1)S(1)}, u32[]{:S(2)}, u32[]{:S(2)}) collective-permute-start(bf16[384,448]{1,0:T(8,128)(2,1)S(1)} %get-tuple-element.29), channel_id=1, source_target_pairs={{0,1},{1,0},{2,3},{3,2},{4,5},{5,4},{6,7},{7,6},{8,9},{9,8},{10,11... | collective-permute-start | bytes 1032200 | tf_op jit(solution)/shard_map/ppermute | solution.py:28
  20.8 0.0 copy-done.2
  20.8 15.6 %first.1 = (bf16[3,7,7,112,112]{4,3,2,1,0:T(8,128)(2,1)S(1)}, f32[1024,512]{1,0:T(8,128)S(1)}) custom-call(bf16[56,56,316]{2,1,0:T(8,128)(2,1)S(1)} %bitcast.95, bf16[8,4,32,448]{3,2,1,0:T(8,128)(2,1)S(1)} %bitcast.91, bf16[48,448]{1,0:T(8,128)(2,1)S(1)} %get-tuple-element.49.below.below_x, bf16[48,448]{1,0:T(8,128)(2,1)S(1)} %get-tuple-element.48.above.above_x, ...), custom_call_target="tpu_custom_call" | custom-call | flops 20000000000 | bytes 10000000 | tf_op jit(solution)/shard_map/first/pallas_call | solution.py:276
  36.4 0.0 copy-start.1
  36.4 0.0 collective-permute-done.5
  36.4 0.0 collective-permute-done.6
  36.4 0.1 pad_maximum_fusion.1
  36.5 0.0 collective-permute-done.3
  36.5 0.0 collective-permute-done.4
  36.5 0.1 pad_maximum_fusion.got_y
  36.6 0.0 collective-permute-done.2
  36.6 0.1 stack.49.got_z
  36.6 0.6 %copy-done.1 = bf16[56,448]{1,0:T(8,128)(2,1)S(1)} copy-done((bf16[56,448]{1,0:T(8,128)(2,1)S(1)}, bf16[56,448]{1,0:T(8,128)(2,1)}, u32[]{:S(2)}) %copy-start.1) | copy-done | bytes 50200
  37.2 8.8 %far.1 = f32[32,8,4,448]{3,2,1,0:T(4,128)} custom-call(s32[2]{0:T(128)S(1)} %add_convert_fusion.odd, f32[1024,512]{1,0:T(8,128)S(1)} %get-tuple-element.15.near, bf16[3,7,7,112,112]{4,3,2,1,0:T(8,128)(2,1)S(1)} %get-tuple-element.16.table, bf16[4,2,16,448]{3,2,1,0:T(8,128)(2,1)S(1)} %get-tuple-element.13.middle, ...), custom_call_target="tpu_custom_call" | custom-call | tf_op jit(solution)/shard_map/far/pallas_call | solution.py:475
  (56 shorter events, 0.9 us)
Async XLA Ops:
  1.8 0.8 %copy-start = (bf16[448,56]{0,1:T(8,128)(2,1)S(1)}, bf16[448,56]{0,1:T(8,128)(2,1)}, u32[]{:S(2)}) copy-start(bf16[448,56]{0,1:T(8,128)(2,1)} %param.5) | copy-start | bytes 150532
  3.6 5.4 %collective-permute-start.1 = (bf16[48,448]{1,0:T(8,128)(2,1)S(1)}, bf16[48,448]{1,0:T(8,128)(2,1)S(1)}, u32[]{:S(2)}, u32[]{:S(2)}) collective-permute-start(bf16[48,448]{1,0:T(8,128)(2,1)S(1)} %get-tuple-element.50), channel_id=1, source_target_pairs={{8,16},{16,8},{9,17},{17,9},{10,18},{18,10},{11,19},{19,11},{12,20... | collective-permute-start | bytes 129032 | tf_op jit(solution)/shard_map/ppermute | solution.py:28
  4.3 5.2 %collective-permute-start = (bf16[48,448]{1,0:T(8,128)(2,1)S(1)}, bf16[48,448]{1,0:T(8,128)(2,1)S(1)}, u32[]{:S(2)}, u32[]{:S(2)}) collective-permute-start(bf16[48,448]{1,0:T(8,128)(2,1)S(1)} %get-tuple-element.51), channel_id=1, source_target_pairs={{0,8},{16,24},{8,0},{24,16},{1,9},{17,25},{9,1},{25,17},{2,10},{18... | collective-permute-start | bytes 129032 | tf_op jit(solution)/shard_map/ppermute | solution.py:28
  10.5 25.9 %collective-permute-start.5 = (bf16[80,448]{1,0:T(8,128)(2,1)S(1)}, bf16[80,448]{1,0:T(8,128)(2,1)S(1)}, u32[]{:S(2)}, u32[]{:S(2)}) collective-permute-start(bf16[80,448]{1,0:T(8,128)(2,1)S(1)} %get-tuple-element.31), channel_id=1, source_target_pairs={{0,3},{1,2},{4,7},{5,6},{3,0},{2,1},{7,4},{6,5},{8,11},{9,10},{12,... | collective-permute-start | bytes 215048 | tf_op jit(solution)/shard_map/ppermute | solution.py:28
  13.1 23.4 %collective-permute-start.6 = (bf16[80,448]{1,0:T(8,128)(2,1)S(1)}, bf16[80,448]{1,0:T(8,128)(2,1)S(1)}, u32[]{:S(2)}, u32[]{:S(2)}) collective-permute-start(bf16[80,448]{1,0:T(8,128)(2,1)S(1)} %get-tuple-element.32), channel_id=1, source_target_pairs={{2,5},{3,4},{5,2},{4,3},{10,13},{11,12},{13,10},{12,11},{18,21},{1... | collective-permute-start | bytes 215048 | tf_op jit(solution)/shard_map/ppermute | solution.py:28
  13.8 7.0 %copy-start.2 = (bf16[316,56,56]{0,2,1:T(8,128)(2,1)S(1)}, bf16[316,56,56]{0,2,1:T(8,128)(2,1)}, u32[]{:S(2)}) copy-start(bf16[316,56,56]{0,2,1:T(8,128)(2,1)} %param.6) | copy-start | bytes 5945860
  13.9 22.6 %collective-permute-start.3 = (bf16[192,448]{1,0:T(8,128)(2,1)S(1)}, bf16[192,448]{1,0:T(8,128)(2,1)S(1)}, u32[]{:S(2)}, u32[]{:S(2)}) collective-permute-start(bf16[192,448]{1,0:T(8,128)(2,1)S(1)} %get-tuple-element.27), channel_id=1, source_target_pairs={{0,2},{4,6},{2,0},{6,4},{1,3},{5,7},{3,1},{7,5},{8,10},{12,14},{10... | collective-permute-start | bytes 516104 | tf_op jit(solution)/shard_map/ppermute | solution.py:28
  18.3 18.2 %collective-permute-start.4 = (bf16[192,448]{1,0:T(8,128)(2,1)S(1)}, bf16[192,448]{1,0:T(8,128)(2,1)S(1)}, u32[]{:S(2)}, u32[]{:S(2)}) collective-permute-start(bf16[192,448]{1,0:T(8,128)(2,1)S(1)} %get-tuple-element.28), channel_id=1, source_target_pairs={{2,4},{4,2},{3,5},{5,3},{10,12},{12,10},{11,13},{13,11},{18,20},{2... | collective-permute-start | bytes 516104 | tf_op jit(solution)/shard_map/ppermute | solution.py:28
  19.2 17.4 %collective-permute-start.2 = (bf16[384,448]{1,0:T(8,128)(2,1)S(1)}, bf16[384,448]{1,0:T(8,128)(2,1)S(1)}, u32[]{:S(2)}, u32[]{:S(2)}) collective-permute-start(bf16[384,448]{1,0:T(8,128)(2,1)S(1)} %get-tuple-element.29), channel_id=1, source_target_pairs={{0,1},{1,0},{2,3},{3,2},{4,5},{5,4},{6,7},{7,6},{8,9},{9,8},{10,11... | collective-permute-start | bytes 1032200 | tf_op jit(solution)/shard_map/ppermute | solution.py:28
  36.4 0.8 %copy-start.1 = (bf16[56,448]{1,0:T(8,128)(2,1)S(1)}, bf16[56,448]{1,0:T(8,128)(2,1)}, u32[]{:S(2)}) copy-start(bf16[56,448]{1,0:T(8,128)(2,1)} %down.1) | copy-start | bytes 150532

commit v5 on v4

--- a/solution.py
+++ b/solution.py
@@ -61,7 +61,7 @@
 def lift_kernel(base, weight, middle, top, low, high):
     size_y, size_z, size_x, width = base.shape
     half, part = size_x // 2, size_x // 4
-    up = weight[...]
+    up = weight[: weight.shape[0] // 2][: width // 8]
 
     def lift(rows):
         product = lax.dot_general(rows, up, (((1,), (1,)), ((), ())), preferred_element_type=F32)
@@ -105,7 +105,7 @@
     high[...] = jnp.concatenate(highs + fill, axis=0).astype(BF)
 
 
-def lifted(base, upward_weight):
+def lifted(base, weights):
     size_y, size_z, size_x, width = base.shape
     count = size_y * size_z + (size_y // 2) * (size_z // 2) + (size_y // 4) * (size_z // 4)
     ends = jax.ShapeDtypeStruct((-(-count // 16) * 16, width), BF)
@@ -121,24 +121,21 @@
         out_specs=(WHOLE,) * 4,
         compiler_params=params(24),
         name="lift",
-    )(base, upward_weight.T)
-
-
-def turn_operators(weight, arriving, blocks):
+    )(base, weights)
+
+
+def turn_operators(weight, blocks, source, at):
     coeffs, _, count = weight.shape
-    lanes, batch = 128, coeffs // len(arriving)
-
-    def turn(source, carry):
-        rows = weight[source].astype(F32)
-        for at in range(0, count, lanes):
-            part = widened(rows[:, at : min(at + lanes, count)])
-            turned = widened(part.T)
-            blocks[pl.ds(at * coeffs + source, lanes, stride=coeffs), :] = turned
-        return carry
-
-    for i, copy in enumerate(arriving):
-        copy.wait()
-        lax.fori_loop(i * batch, (i + 1) * batch, turn, 0, unroll=4)
+    lanes = blocks.shape[1]
+    part = widened(weight[source, :, at : min(at + lanes, count)].astype(F32))
+    blocks[pl.ds(at * coeffs + source, lanes, stride=coeffs), :] = widened(part.T)
+
+
+def number_of(first, second, third):
+    number = 0
+    for i in range(first * 49 + second * 7 + third):
+        number += not all(2 <= j <= 4 for j in (i // 49, i // 7 % 7, i % 7))
+    return number
 
 
 def fill_entry(blocks, table, first, second, third, coeffs):
@@ -146,9 +143,7 @@
         spot = (first, second, at)
         if all(2 <= i <= 4 for i in spot):
             return jnp.zeros((coeffs, blocks.shape[1]), F32)
-        before = 0
-        for i in range(spot[0] * 49 + spot[1] * 7 + at):
-            before += not all(2 <= j <= 4 for j in (i // 49, i // 7 % 7, i % 7))
+        before = number_of(*spot)
         return blocks[before * coeffs : (before + 1) * coeffs]
 
     rows = []
@@ -162,9 +157,9 @@
 SLOTS = 8
 SHIFTS = [
     (dx, dy, dz)
+    for dx in range(3)
+    for dy in (1, 0, 2)
     for dz in (1, 0, 2)
-    for dy in (1, 0, 2)
-    for dx in range(3)
     if (dx, dy, dz) != (1, 1, 1)
 ]
 
@@ -190,11 +185,11 @@
     return rows
 
 
-def store_moved(rows, low, high, copies, y, z, fill=False):
+def store_moved(rows, low, high, copies, y, z, fill=False, wanted=range(3)):
     rows = widened(rows.astype(F32))
     one, two = moved_rows(rows, widened(low), widened(high))
     three = [one, [rows], two]
-    for dx in range(3):
+    for dx in wanted:
         if fill:
             three[dx] = three[dx] + [jnp.zeros_like(rows)]
         copies[dx, y, z] = jnp.concatenate(three[dx], axis=0).astype(BF)
@@ -219,14 +214,68 @@
     return kernels[slot]
 
 
-def add_near(prepare, table, leaf, below, above, leaves, kernels, total):
+def first_kernel(weight, leaf, below, above, _, table, total, blocks, leaves, kernels):
+    coeffs, _, offsets = weight.shape
     size_y, size_z, size_x, width = leaf.shape
+    lanes = blocks.shape[1]
+
     low = below[: size_y * size_z].astype(F32)
     high = above[: size_y * size_z].astype(F32)
-    for y in range(size_y):
-        for z in range(size_z):
-            at = y * size_z + z
-            store_moved(leaf[y, z], low[at : at + 1], high[at : at + 1], leaves, y, z)
+
+    def move(dx):
+        steps = []
+        for y in range(size_y):
+            for z in range(size_z):
+                ends = [rows[y * size_z + z : y * size_z + z + 1] for rows in (low, high)]
+                steps.append(
+                    functools.partial(
+                        store_moved, leaf[y, z], *ends, leaves, y, z, wanted=(dx,)
+                    )
+                )
+        return steps
+
+    for step in move(0):
+        step()
+
+    def turn(source, carry):
+        turn_operators(weight, blocks, source, 0)
+        return carry
+
+    lax.fori_loop(0, coeffs, turn, 0, unroll=8)
+
+    tasks = []
+
+    def due(steps, begin, end):
+        for i, step in enumerate(steps):
+            tasks.append((begin + i * (end - begin) // len(steps), step))
+
+    def needs(shift):
+        dx, dy, dz = shift
+        return number_of(2 * dx + 2, 2 * dy + 2, 2 * dz + 2)
+
+    begin = 0
+    for at in range(lanes, offsets, lanes):
+        end = min(slot for slot, shift in enumerate(SHIFTS) if needs(shift) >= at)
+        begin = min(begin, end - 1)
+        steps = [
+            functools.partial(turn_operators, weight, blocks, source, at)
+            for source in range(coeffs)
+        ]
+        due(steps, begin, end)
+        begin = end
+    for dx in range(1, 3):
+        end = min(slot for slot, shift in enumerate(SHIFTS) if shift[0] == dx)
+        due(move(dx), end - 8, end)
+
+    done = set()
+
+    def prepare(dx, dy, dz):
+        for first in range(2 * dx, 2 * dx + 3):
+            for second in range(2 * dy, 2 * dy + 3):
+                if (dz, first, second) not in done:
+                    done.add((dz, first, second))
+                    fill_entry(blocks, table, first, second, dz, coeffs)
+
     for slot, (dx, dy, dz) in enumerate(SHIFTS):
         prepare(dx, dy, dz)
         kernel = operator(table, (dx, dy, dz), kernels, slot)
@@ -241,30 +290,9 @@
             at = ((first_y + i) * size_z + first_z) * size_x
             piece = product[i * count : (i + 1) * count]
             total[at : at + count] = piece if slot == 0 else total[at : at + count] + piece
-
-
-def first_kernel(
-    given, leaf, below, above, _, table, total, weight, blocks, leaves, kernels, arrived
-):
-    coeffs = given.shape[0]
-    count = arrived.shape[0]
-    batch = coeffs // count
-    arriving = []
-    for i in range(count):
-        part = pl.ds(i * batch, batch)
-        arriving.append(pltpu.make_async_copy(given.at[part], weight.at[part], arrived.at[i]))
-        arriving[i].start()
-    turn_operators(weight, arriving, blocks)
-    done = set()
-
-    def prepare(dx, dy, dz):
-        for first in range(2 * dx, 2 * dx + 3):
-            for second in range(2 * dy, 2 * dy + 3):
-                if (dz, first, second) not in done:
-                    done.add((dz, first, second))
-                    fill_entry(blocks, table, first, second, dz, coeffs)
-
-    add_near(prepare, table, leaf, below, above, leaves, kernels, total)
+        for when, step in tasks:
+            if when == slot:
+                step()
     for dx, dy, dz in [(dx, dy, dz) for dx in range(3) for dy in range(3) for dz in range(3)]:
         prepare(dx, dy, dz)
 
@@ -279,14 +307,12 @@
             jax.ShapeDtypeStruct((3, 7, 7, 2 * coeffs, 2 * coeffs), BF),
             jax.ShapeDtypeStruct((size_y * size_z * size_x, wide), F32),
         ),
-        in_specs=[HBM] + [WHOLE] * 3 + [ANYWHERE],
+        in_specs=[WHOLE] * 4 + [ANYWHERE],
         out_specs=(WHOLE, WHOLE),
         scratch_shapes=[
-            pltpu.VMEM((coeffs, coeffs, count), BF),
             pltpu.VMEM((-(-count // 128) * 128 * coeffs, 128), F32),
             pltpu.VMEM((3, size_y, size_z, size_x, wide), BF),
             pltpu.VMEM((SLOTS, wide, wide), BF),
-            pltpu.SemaphoreType.DMA((7,)),
         ],
         compiler_params=params(32),
         cost_estimate=pl.CostEstimate(flops=2 * 10**10, bytes_accessed=10**7, transcendentals=0),
@@ -359,11 +385,31 @@
             )
 
     copies = (leaves, middles, tops)
-    for level in range(3):
+
+    def move(level, wanted):
+        steps = []
         for (y, z), (rows, low, high) in slabs[level].items():
             if level == 2:
                 rows = rows[: half // 2]
-            store_moved(rows, low, high, copies[level], y, z, level == 2)
+            steps.append(
+                functools.partial(
+                    store_moved, rows, low, high, copies[level], y, z, level == 2, wanted
+                )
+            )
+        return steps
+
+    for step in move(1, (0,)) + move(2, (0,)):
+        step()
+    tasks = []
+
+    def due(steps, begin, end):
+        for i, step in enumerate(steps):
+            tasks.append((begin + i * (end - begin) // len(steps), step))
+
+    for dx in range(1, 3):
+        end = min(slot for slot, shift in enumerate(SHIFTS) if shift[0] == dx)
+        due(move(1, (dx,)) + move(2, (dx,)), end - 8, end)
+    due(move(0, range(3)), 0, len(SHIFTS))
 
     leaf_rows = size_y * size_z * size_x
     wide = kernels.shape[1]
@@ -377,8 +423,11 @@
         rows = jnp.concatenate(rows, axis=0)
         product = jnp.dot(rows, made[slot], preferred_element_type=F32)[:, :width]
         upper[...] = product if slot == 0 else upper[...] + product
-
-    weight = down[...]
+        for when, step in tasks:
+            if when == slot:
+                step()
+
+    weight = down[down.shape[0] // 2 :][:coeffs]
 
     def spread(count_y, count_z, parent, rows):
         pieces = []
@@ -494,9 +543,12 @@
 
 def shards(densities, upward_weight, transfer_weight, downward_weight):
     size_x, size_y, size_z, width = densities.shape
+    fill = ((0, -downward_weight.shape[0] % 16), (0, 0))
+    weights = [jnp.pad(upward_weight.T, fill), jnp.pad(downward_weight, fill)]
+    weights = jnp.concatenate(weights, axis=0)
     base = densities.reshape(size_x // 4, 2, 2, size_y, size_z, width)
     base = base.transpose(3, 4, 2, 1, 0, 5).reshape(size_y, size_z, size_x, width)
-    middle, top, low, high = lifted(base, upward_weight)
+    middle, top, low, high = lifted(base, weights)
     levels = [base, middle, top]
 
     def packed(pieces):
@@ -538,7 +590,7 @@
     table, near = first_part(transfer_weight, base, below_x, above_x, low_z)
     odd = jnp.stack([is_odd("gy"), is_odd("gz")]).astype(jnp.int32)
     halos = (below_x, above_x, got_z, got_y, got_yz)
-    return far(odd, near, table, middle, top, halos, downward_weight)
+    return far(odd, near, table, middle, top, halos, weights)
 
 
 def solution(mesh):

time: 46.5 us -> 43.3 us (0.931)
  Pallas kernels: 25.3 us -> 22.7 us
  local copies, waits for them, and re-layouts: 3.9 us -> 2.52 us
  other arithmetic: 0.8 us -> 1.66 us
    pallas_call x1, Pallas kernels: 15.6 us -> 12.9 us  [first_part(): pl.pallas_call(first_kernel, out_shape=(jax.ShapeDtypeStruct((3, 7, 7, 2...]
    unnamed x14 -> x10, local copies, waits for them, and re-layouts: 1.45 us -> 0.08 us
    concatenate x0 -> x1, other arithmetic: none -> 0.86 us  [shards(): weights = jnp.concatenate(weights, axis=0)]
  transfers between devices with their start and end apart: 7 -> 7, of which waited for: 1 -> 1; matrix products, arithmetic and copies ran while one was open for 1% -> 2% of each run, Pallas kernels for 34% -> 30%
where the time goes in v5:
time: 43.3 us; the launch traced here: 43 us
  Pallas kernels  22.7 us (52%)
  starting transfers between devices  14.9 us (34%)
  local copies, waits for them, and re-layouts  2.52 us (6%)
  other arithmetic  1.66 us (4%)
  between operations  0.64 us (1%)
  waiting for transfers between devices  0.56 us (1%)
    ppermute x7, starting transfers between devices, swapped(): return lax.ppermute(block, axis, both) if pairs else jnp.zeros_like(block)  14.9 us
    pallas_call x1, Pallas kernels, first_part(): pl.pallas_call(first_kernel, out_shape=(jax.ShapeDtypeStruct((3, 7, 7, 2...  12.9 us
    pallas_call x1, Pallas kernels, far(): pl.pallas_call(far_kernel, out_shape=jax.ShapeDtypeStruct((2 * half, size...  8.82 us
    reshape x1, local copies, waits for them, and re-layouts, shards(): base = densities.reshape(size_x // 4, 2, 2, size_y, size_z, width)  1.8 us
    pallas_call x1, Pallas kernels, lifted(): pl.pallas_call(lift_kernel, out_shape=(jax.ShapeDtypeStruct((size_y // 2,...  0.95 us
  transfers between devices with their start and end apart: 7, of which 1 were waited for; matrix products, arithmetic and copies ran while one was open for 2% of the time, Pallas kernels for 30%

profile of v5, /device:TPU:0, one launch (start us, length us, event | category | flops | bytes accessed | tf_op | source)
XLA Modules:
  0.0 43.0 jit_solution(8931898543837818429)
XLA Ops:
  0.0 1.8 %copy.54 = bf16[8,2,2,8,4,448]{5,0,1,2,4,3:T(8,128)(2,1)S(1)} copy(bf16[8,2,2,8,4,448]{5,4,3,2,1,0:T(4,128)(2,1)} %bitcast.95) | data formatting | bytes 1835008 | tf_op jit(solution)/shard_map/reshape | solution.py:549
  1.8 0.9 %fusion.2.weight.down = bf16[128,448]{1,0:T(8,128)(2,1)S(1)} fusion(bf16[56,448]{1,0:T(8,128)(2,1)} %param.7, bf16[56,448]{1,0:T(8,128)(2,1)} %bitcast.109), kind=kLoop, calls=%fused_computation.9 | loop fusion | flops 458752 | bytes 215040 | tf_op jit(solution)/shard_map/concatenate | solution.py:548
  2.7 0.9 %lift.1 = (bf16[4,2,16,448]{3,2,1,0:T(8,128)(2,1)S(1)}, bf16[2,1,16,448]{3,2,1,0:T(8,128)(2,1)S(1)}, bf16[48,448]{1,0:T(8,128)(2,1)S(1)}, bf16[48,448]{1,0:T(8,128)(2,1)S(1)}) custom-call(bf16[8,4,32,448]{3,2,1,0:T(8,128)(2,1)S(1)} %bitcast.87, bf16[128,448]{1,0:T(8,128)(2,1)S(1)} %fusion.2.weight.down), custom_call_target="tpu_custom_call" | custom-call | tf_op jit(solution)/shard_map/lift/pallas_call | solution.py:112
  3.6 0.7 %collective-permute-start.1 = (bf16[48,448]{1,0:T(8,128)(2,1)S(1)}, bf16[48,448]{1,0:T(8,128)(2,1)S(1)}, u32[]{:S(2)}, u32[]{:S(2)}) collective-permute-start(bf16[48,448]{1,0:T(8,128)(2,1)S(1)} %get-tuple-element.50), channel_id=1, source_target_pairs={{8,16},{16,8},{9,17},{17,9},{10,18},{18,10},{11,19},{19,11},{12,20... | collective-permute-start | bytes 129032 | tf_op jit(solution)/shard_map/ppermute | solution.py:28
  4.3 4.4 %collective-permute-start = (bf16[48,448]{1,0:T(8,128)(2,1)S(1)}, bf16[48,448]{1,0:T(8,128)(2,1)S(1)}, u32[]{:S(2)}, u32[]{:S(2)}) collective-permute-start(bf16[48,448]{1,0:T(8,128)(2,1)S(1)} %get-tuple-element.51), channel_id=1, source_target_pairs={{0,8},{16,24},{8,0},{24,16},{1,9},{17,25},{9,1},{25,17},{2,10},{18... | collective-permute-start | bytes 129032 | tf_op jit(solution)/shard_map/ppermute | solution.py:28
  8.9 0.1 add_convert_fusion.odd
  9.0 0.0 collective-permute-done.1
  9.0 0.5 %collective-permute-done = bf16[48,448]{1,0:T(8,128)(2,1)S(1)} collective-permute-done((bf16[48,448]{1,0:T(8,128)(2,1)S(1)}, bf16[48,448]{1,0:T(8,128)(2,1)S(1)}, u32[]{:S(2)}, u32[]{:S(2)}) %collective-permute-start) | collective-permute-done | bytes 43040 | tf_op jit(solution)/shard_map/ppermute | solution.py:28
  10.0 0.1 slice_maximum_fusion
  10.4 0.1 select_select_fusion.1
  10.5 2.6 %collective-permute-start.5 = (bf16[80,448]{1,0:T(8,128)(2,1)S(1)}, bf16[80,448]{1,0:T(8,128)(2,1)S(1)}, u32[]{:S(2)}, u32[]{:S(2)}) collective-permute-start(bf16[80,448]{1,0:T(8,128)(2,1)S(1)} %get-tuple-element.31), channel_id=1, source_target_pairs={{0,3},{1,2},{4,7},{5,6},{3,0},{2,1},{7,4},{6,5},{8,11},{9,10},{12,... | collective-permute-start | bytes 215048 | tf_op jit(solution)/shard_map/ppermute | solution.py:28
  13.1 0.7 %collective-permute-start.6 = (bf16[80,448]{1,0:T(8,128)(2,1)S(1)}, bf16[80,448]{1,0:T(8,128)(2,1)S(1)}, u32[]{:S(2)}, u32[]{:S(2)}) collective-permute-start(bf16[80,448]{1,0:T(8,128)(2,1)S(1)} %get-tuple-element.32), channel_id=1, source_target_pairs={{2,5},{3,4},{5,2},{4,3},{10,13},{11,12},{13,10},{12,11},{18,21},{1... | collective-permute-start | bytes 215048 | tf_op jit(solution)/shard_map/ppermute | solution.py:28
  13.8 0.0 copy-start
  13.8 0.1 broadcast_select_fusion.1
  13.9 4.4 %collective-permute-start.3 = (bf16[192,448]{1,0:T(8,128)(2,1)S(1)}, bf16[192,448]{1,0:T(8,128)(2,1)S(1)}, u32[]{:S(2)}, u32[]{:S(2)}) collective-permute-start(bf16[192,448]{1,0:T(8,128)(2,1)S(1)} %get-tuple-element.27), channel_id=1, source_target_pairs={{0,2},{4,6},{2,0},{6,4},{1,3},{5,7},{3,1},{7,5},{8,10},{12,14},{10... | collective-permute-start | bytes 516104 | tf_op jit(solution)/shard_map/ppermute | solution.py:28
  18.3 0.7 %collective-permute-start.4 = (bf16[192,448]{1,0:T(8,128)(2,1)S(1)}, bf16[192,448]{1,0:T(8,128)(2,1)S(1)}, u32[]{:S(2)}, u32[]{:S(2)}) collective-permute-start(bf16[192,448]{1,0:T(8,128)(2,1)S(1)} %get-tuple-element.28), channel_id=1, source_target_pairs={{2,4},{4,2},{3,5},{5,3},{10,12},{12,10},{11,13},{13,11},{18,20},{2... | collective-permute-start | bytes 516104 | tf_op jit(solution)/shard_map/ppermute | solution.py:28
  19.1 0.2 pad_select_fusion
  19.2 1.6 %collective-permute-start.2 = (bf16[384,448]{1,0:T(8,128)(2,1)S(1)}, bf16[384,448]{1,0:T(8,128)(2,1)S(1)}, u32[]{:S(2)}, u32[]{:S(2)}) collective-permute-start(bf16[384,448]{1,0:T(8,128)(2,1)S(1)} %get-tuple-element.29), channel_id=1, source_target_pairs={{0,1},{1,0},{2,3},{3,2},{4,5},{5,4},{6,7},{7,6},{8,9},{9,8},{10,11... | collective-permute-start | bytes 1032200 | tf_op jit(solution)/shard_map/ppermute | solution.py:28
  20.8 0.0 copy-done
  20.8 12.9 %first.1 = (bf16[3,7,7,112,112]{4,3,2,1,0:T(8,128)(2,1)S(1)}, f32[1024,512]{1,0:T(8,128)S(1)}) custom-call(bf16[56,56,316]{2,1,0:T(8,128)(2,1)S(1)} %bitcast.94, bf16[8,4,32,448]{3,2,1,0:T(8,128)(2,1)S(1)} %bitcast.91, bf16[48,448]{1,0:T(8,128)(2,1)S(1)} %get-tuple-element.49.below.below_x, bf16[48,448]{1,0:T(8,128)(2,1)S(1)} %get-tuple-element.48.above.above_x, ...), custom_call_target="tpu_custom_call" | custom-call | flops 20000000000 | bytes 10000000 | tf_op jit(solution)/shard_map/first/pallas_call | solution.py:304
  33.8 0.0 collective-permute-done.5
  33.8 0.0 collective-permute-done.6
  33.9 0.0 collective-permute-done.3
  33.9 0.0 collective-permute-done.4
  33.9 0.0 collective-permute-done.2
  33.9 0.1 stack.49.got_z
  34.0 8.8 %far.1 = f32[32,8,4,448]{3,2,1,0:T(4,128)} custom-call(s32[2]{0:T(128)S(1)} %add_convert_fusion.odd, f32[1024,512]{1,0:T(8,128)S(1)} %get-tuple-element.15.near, bf16[3,7,7,112,112]{4,3,2,1,0:T(8,128)(2,1)S(1)} %get-tuple-element.16.table, bf16[4,2,16,448]{3,2,1,0:T(8,128)(2,1)S(1)} %get-tuple-element.13.middle, ...), custom_call_target="tpu_custom_call" | custom-call | tf_op jit(solution)/shard_map/far/pallas_call | solution.py:524
  (58 shorter events, 1.0 us)
Async XLA Ops:
  3.6 5.4 %collective-permute-start.1 = (bf16[48,448]{1,0:T(8,128)(2,1)S(1)}, bf16[48,448]{1,0:T(8,128)(2,1)S(1)}, u32[]{:S(2)}, u32[]{:S(2)}) collective-permute-start(bf16[48,448]{1,0:T(8,128)(2,1)S(1)} %get-tuple-element.50), channel_id=1, source_target_pairs={{8,16},{16,8},{9,17},{17,9},{10,18},{18,10},{11,19},{19,11},{12,20... | collective-permute-start | bytes 129032 | tf_op jit(solution)/shard_map/ppermute | solution.py:28
  4.3 5.2 %collective-permute-start = (bf16[48,448]{1,0:T(8,128)(2,1)S(1)}, bf16[48,448]{1,0:T(8,128)(2,1)S(1)}, u32[]{:S(2)}, u32[]{:S(2)}) collective-permute-start(bf16[48,448]{1,0:T(8,128)(2,1)S(1)} %get-tuple-element.51), channel_id=1, source_target_pairs={{0,8},{16,24},{8,0},{24,16},{1,9},{17,25},{9,1},{25,17},{2,10},{18... | collective-permute-start | bytes 129032 | tf_op jit(solution)/shard_map/ppermute | solution.py:28
  10.5 23.3 %collective-permute-start.5 = (bf16[80,448]{1,0:T(8,128)(2,1)S(1)}, bf16[80,448]{1,0:T(8,128)(2,1)S(1)}, u32[]{:S(2)}, u32[]{:S(2)}) collective-permute-start(bf16[80,448]{1,0:T(8,128)(2,1)S(1)} %get-tuple-element.31), channel_id=1, source_target_pairs={{0,3},{1,2},{4,7},{5,6},{3,0},{2,1},{7,4},{6,5},{8,11},{9,10},{12,... | collective-permute-start | bytes 215048 | tf_op jit(solution)/shard_map/ppermute | solution.py:28
  13.1 20.7 %collective-permute-start.6 = (bf16[80,448]{1,0:T(8,128)(2,1)S(1)}, bf16[80,448]{1,0:T(8,128)(2,1)S(1)}, u32[]{:S(2)}, u32[]{:S(2)}) collective-permute-start(bf16[80,448]{1,0:T(8,128)(2,1)S(1)} %get-tuple-element.32), channel_id=1, source_target_pairs={{2,5},{3,4},{5,2},{4,3},{10,13},{11,12},{13,10},{12,11},{18,21},{1... | collective-permute-start | bytes 215048 | tf_op jit(solution)/shard_map/ppermute | solution.py:28
  13.8 7.0 %copy-start = (bf16[316,56,56]{0,2,1:T(8,128)(2,1)S(1)}, bf16[316,56,56]{0,2,1:T(8,128)(2,1)}, u32[]{:S(2)}) copy-start(bf16[316,56,56]{0,2,1:T(8,128)(2,1)} %param.6) | copy-start | bytes 5945860
  13.9 19.9 %collective-permute-start.3 = (bf16[192,448]{1,0:T(8,128)(2,1)S(1)}, bf16[192,448]{1,0:T(8,128)(2,1)S(1)}, u32[]{:S(2)}, u32[]{:S(2)}) collective-permute-start(bf16[192,448]{1,0:T(8,128)(2,1)S(1)} %get-tuple-element.27), channel_id=1, source_target_pairs={{0,2},{4,6},{2,0},{6,4},{1,3},{5,7},{3,1},{7,5},{8,10},{12,14},{10... | collective-permute-start | bytes 516104 | tf_op jit(solution)/shard_map/ppermute | solution.py:28
  18.3 15.5 %collective-permute-start.4 = (bf16[192,448]{1,0:T(8,128)(2,1)S(1)}, bf16[192,448]{1,0:T(8,128)(2,1)S(1)}, u32[]{:S(2)}, u32[]{:S(2)}) collective-permute-start(bf16[192,448]{1,0:T(8,128)(2,1)S(1)} %get-tuple-element.28), channel_id=1, source_target_pairs={{2,4},{4,2},{3,5},{5,3},{10,12},{12,10},{11,13},{13,11},{18,20},{2... | collective-permute-start | bytes 516104 | tf_op jit(solution)/shard_map/ppermute | solution.py:28
  19.2 14.7 %collective-permute-start.2 = (bf16[384,448]{1,0:T(8,128)(2,1)S(1)}, bf16[384,448]{1,0:T(8,128)(2,1)S(1)}, u32[]{:S(2)}, u32[]{:S(2)}) collective-permute-start(bf16[384,448]{1,0:T(8,128)(2,1)S(1)} %get-tuple-element.29), channel_id=1, source_target_pairs={{0,1},{1,0},{2,3},{3,2},{4,5},{5,4},{6,7},{7,6},{8,9},{9,8},{10,11... | collective-permute-start | bytes 1032200 | tf_op jit(solution)/shard_map/ppermute | solution.py:28

commit v6 on v5

--- a/solution.py
+++ b/solution.py
@@ -241,7 +241,7 @@
         turn_operators(weight, blocks, source, 0)
         return carry
 
-    lax.fori_loop(0, coeffs, turn, 0, unroll=8)
+    lax.fori_loop(0, coeffs, turn, 0, unroll=28)
 
     tasks = []
 

time: 43.3 us -> 42.9 us (level)
  transfers between devices with their start and end apart: 7 -> 7, of which waited for: 1 -> 1; matrix products, arithmetic and copies ran while one was open for 2% -> 2% of each run, Pallas kernels for 30% -> 29%
where the time goes in v6:
time: 42.9 us; the launch traced here: 42.7 us
  Pallas kernels  22.3 us (52%)
  starting transfers between devices  14.9 us (35%)
  local copies, waits for them, and re-layouts  2.52 us (6%)
  other arithmetic  1.66 us (4%)
  between operations  0.64 us (1%)
  waiting for transfers between devices  0.56 us (1%)
    ppermute x7, starting transfers between devices, swapped(): return lax.ppermute(block, axis, both) if pairs else jnp.zeros_like(block)  14.9 us
    pallas_call x1, Pallas kernels, first_part(): pl.pallas_call(first_kernel, out_shape=(jax.ShapeDtypeStruct((3, 7, 7, 2...  12.6 us
    pallas_call x1, Pallas kernels, far(): pl.pallas_call(far_kernel, out_shape=jax.ShapeDtypeStruct((2 * half, size...  8.81 us
    reshape x1, local copies, waits for them, and re-layouts, shards(): base = densities.reshape(size_x // 4, 2, 2, size_y, size_z, width)  1.8 us
    pallas_call x1, Pallas kernels, lifted(): pl.pallas_call(lift_kernel, out_shape=(jax.ShapeDtypeStruct((size_y // 2,...  0.95 us
    concatenate x1, other arithmetic, shards(): weights = jnp.concatenate(weights, axis=0)  0.86 us
  transfers between devices with their start and end apart: 7, of which 1 were waited for; matrix products, arithmetic and copies ran while one was open for 2% of the time, Pallas kernels for 29%

profile of v6, /device:TPU:0, one launch (start us, length us, event | category | flops | bytes accessed | tf_op | source)
XLA Modules:
  0.0 42.7 jit_solution(3520592789478848525)
XLA Ops:
  0.0 1.8 %copy.54 = bf16[8,2,2,8,4,448]{5,0,1,2,4,3:T(8,128)(2,1)S(1)} copy(bf16[8,2,2,8,4,448]{5,4,3,2,1,0:T(4,128)(2,1)} %bitcast.95) | data formatting | bytes 1835008 | tf_op jit(solution)/shard_map/reshape | solution.py:549
  1.8 0.9 %fusion.2.weight.down = bf16[128,448]{1,0:T(8,128)(2,1)S(1)} fusion(bf16[56,448]{1,0:T(8,128)(2,1)} %param.7, bf16[56,448]{1,0:T(8,128)(2,1)} %bitcast.109), kind=kLoop, calls=%fused_computation.9 | loop fusion | flops 458752 | bytes 215040 | tf_op jit(solution)/shard_map/concatenate | solution.py:548
  2.7 0.9 %lift.1 = (bf16[4,2,16,448]{3,2,1,0:T(8,128)(2,1)S(1)}, bf16[2,1,16,448]{3,2,1,0:T(8,128)(2,1)S(1)}, bf16[48,448]{1,0:T(8,128)(2,1)S(1)}, bf16[48,448]{1,0:T(8,128)(2,1)S(1)}) custom-call(bf16[8,4,32,448]{3,2,1,0:T(8,128)(2,1)S(1)} %bitcast.87, bf16[128,448]{1,0:T(8,128)(2,1)S(1)} %fusion.2.weight.down), custom_call_target="tpu_custom_call" | custom-call | tf_op jit(solution)/shard_map/lift/pallas_call | solution.py:112
  3.6 0.7 %collective-permute-start.1 = (bf16[48,448]{1,0:T(8,128)(2,1)S(1)}, bf16[48,448]{1,0:T(8,128)(2,1)S(1)}, u32[]{:S(2)}, u32[]{:S(2)}) collective-permute-start(bf16[48,448]{1,0:T(8,128)(2,1)S(1)} %get-tuple-element.50), channel_id=1, source_target_pairs={{8,16},{16,8},{9,17},{17,9},{10,18},{18,10},{11,19},{19,11},{12,20... | collective-permute-start | bytes 129032 | tf_op jit(solution)/shard_map/ppermute | solution.py:28
  4.3 4.4 %collective-permute-start = (bf16[48,448]{1,0:T(8,128)(2,1)S(1)}, bf16[48,448]{1,0:T(8,128)(2,1)S(1)}, u32[]{:S(2)}, u32[]{:S(2)}) collective-permute-start(bf16[48,448]{1,0:T(8,128)(2,1)S(1)} %get-tuple-element.51), channel_id=1, source_target_pairs={{0,8},{16,24},{8,0},{24,16},{1,9},{17,25},{9,1},{25,17},{2,10},{18... | collective-permute-start | bytes 129032 | tf_op jit(solution)/shard_map/ppermute | solution.py:28
  8.9 0.1 add_convert_fusion.odd
  9.0 0.0 collective-permute-done.1
  9.0 0.5 %collective-permute-done = bf16[48,448]{1,0:T(8,128)(2,1)S(1)} collective-permute-done((bf16[48,448]{1,0:T(8,128)(2,1)S(1)}, bf16[48,448]{1,0:T(8,128)(2,1)S(1)}, u32[]{:S(2)}, u32[]{:S(2)}) %collective-permute-start) | collective-permute-done | bytes 43040 | tf_op jit(solution)/shard_map/ppermute | solution.py:28
  10.0 0.1 slice_maximum_fusion
  10.4 0.1 select_select_fusion.1
  10.5 2.6 %collective-permute-start.5 = (bf16[80,448]{1,0:T(8,128)(2,1)S(1)}, bf16[80,448]{1,0:T(8,128)(2,1)S(1)}, u32[]{:S(2)}, u32[]{:S(2)}) collective-permute-start(bf16[80,448]{1,0:T(8,128)(2,1)S(1)} %get-tuple-element.31), channel_id=1, source_target_pairs={{0,3},{1,2},{4,7},{5,6},{3,0},{2,1},{7,4},{6,5},{8,11},{9,10},{12,... | collective-permute-start | bytes 215048 | tf_op jit(solution)/shard_map/ppermute | solution.py:28
  13.1 0.7 %collective-permute-start.6 = (bf16[80,448]{1,0:T(8,128)(2,1)S(1)}, bf16[80,448]{1,0:T(8,128)(2,1)S(1)}, u32[]{:S(2)}, u32[]{:S(2)}) collective-permute-start(bf16[80,448]{1,0:T(8,128)(2,1)S(1)} %get-tuple-element.32), channel_id=1, source_target_pairs={{2,5},{3,4},{5,2},{4,3},{10,13},{11,12},{13,10},{12,11},{18,21},{1... | collective-permute-start | bytes 215048 | tf_op jit(solution)/shard_map/ppermute | solution.py:28
  13.8 0.0 copy-start
  13.8 0.1 broadcast_select_fusion.1
  13.9 4.4 %collective-permute-start.3 = (bf16[192,448]{1,0:T(8,128)(2,1)S(1)}, bf16[192,448]{1,0:T(8,128)(2,1)S(1)}, u32[]{:S(2)}, u32[]{:S(2)}) collective-permute-start(bf16[192,448]{1,0:T(8,128)(2,1)S(1)} %get-tuple-element.27), channel_id=1, source_target_pairs={{0,2},{4,6},{2,0},{6,4},{1,3},{5,7},{3,1},{7,5},{8,10},{12,14},{10... | collective-permute-start | bytes 516104 | tf_op jit(solution)/shard_map/ppermute | solution.py:28
  18.3 0.7 %collective-permute-start.4 = (bf16[192,448]{1,0:T(8,128)(2,1)S(1)}, bf16[192,448]{1,0:T(8,128)(2,1)S(1)}, u32[]{:S(2)}, u32[]{:S(2)}) collective-permute-start(bf16[192,448]{1,0:T(8,128)(2,1)S(1)} %get-tuple-element.28), channel_id=1, source_target_pairs={{2,4},{4,2},{3,5},{5,3},{10,12},{12,10},{11,13},{13,11},{18,20},{2... | collective-permute-start | bytes 516104 | tf_op jit(solution)/shard_map/ppermute | solution.py:28
  19.1 0.2 pad_select_fusion
  19.2 1.6 %collective-permute-start.2 = (bf16[384,448]{1,0:T(8,128)(2,1)S(1)}, bf16[384,448]{1,0:T(8,128)(2,1)S(1)}, u32[]{:S(2)}, u32[]{:S(2)}) collective-permute-start(bf16[384,448]{1,0:T(8,128)(2,1)S(1)} %get-tuple-element.29), channel_id=1, source_target_pairs={{0,1},{1,0},{2,3},{3,2},{4,5},{5,4},{6,7},{7,6},{8,9},{9,8},{10,11... | collective-permute-start | bytes 1032200 | tf_op jit(solution)/shard_map/ppermute | solution.py:28
  20.8 0.0 copy-done
  20.8 12.6 %first.1 = (bf16[3,7,7,112,112]{4,3,2,1,0:T(8,128)(2,1)S(1)}, f32[1024,512]{1,0:T(8,128)S(1)}) custom-call(bf16[56,56,316]{2,1,0:T(8,128)(2,1)S(1)} %bitcast.94, bf16[8,4,32,448]{3,2,1,0:T(8,128)(2,1)S(1)} %bitcast.91, bf16[48,448]{1,0:T(8,128)(2,1)S(1)} %get-tuple-element.49.below.below_x, bf16[48,448]{1,0:T(8,128)(2,1)S(1)} %get-tuple-element.48.above.above_x, ...), custom_call_target="tpu_custom_call" | custom-call | flops 20000000000 | bytes 10000000 | tf_op jit(solution)/shard_map/first/pallas_call | solution.py:304
  33.4 0.0 collective-permute-done.5
  33.4 0.0 collective-permute-done.6
  33.5 0.0 collective-permute-done.3
  33.5 0.0 collective-permute-done.4
  33.6 0.0 collective-permute-done.2
  33.6 0.1 stack.49.got_z
  33.7 8.8 %far.1 = f32[32,8,4,448]{3,2,1,0:T(4,128)} custom-call(s32[2]{0:T(128)S(1)} %add_convert_fusion.odd, f32[1024,512]{1,0:T(8,128)S(1)} %get-tuple-element.15.near, bf16[3,7,7,112,112]{4,3,2,1,0:T(8,128)(2,1)S(1)} %get-tuple-element.16.table, bf16[4,2,16,448]{3,2,1,0:T(8,128)(2,1)S(1)} %get-tuple-element.13.middle, ...), custom_call_target="tpu_custom_call" | custom-call | tf_op jit(solution)/shard_map/far/pallas_call | solution.py:524
  (58 shorter events, 1.0 us)
Async XLA Ops:
  3.6 5.4 %collective-permute-start.1 = (bf16[48,448]{1,0:T(8,128)(2,1)S(1)}, bf16[48,448]{1,0:T(8,128)(2,1)S(1)}, u32[]{:S(2)}, u32[]{:S(2)}) collective-permute-start(bf16[48,448]{1,0:T(8,128)(2,1)S(1)} %get-tuple-element.50), channel_id=1, source_target_pairs={{8,16},{16,8},{9,17},{17,9},{10,18},{18,10},{11,19},{19,11},{12,20... | collective-permute-start | bytes 129032 | tf_op jit(solution)/shard_map/ppermute | solution.py:28
  4.3 5.2 %collective-permute-start = (bf16[48,448]{1,0:T(8,128)(2,1)S(1)}, bf16[48,448]{1,0:T(8,128)(2,1)S(1)}, u32[]{:S(2)}, u32[]{:S(2)}) collective-permute-start(bf16[48,448]{1,0:T(8,128)(2,1)S(1)} %get-tuple-element.51), channel_id=1, source_target_pairs={{0,8},{16,24},{8,0},{24,16},{1,9},{17,25},{9,1},{25,17},{2,10},{18... | collective-permute-start | bytes 129032 | tf_op jit(solution)/shard_map/ppermute | solution.py:28
  10.5 22.9 %collective-permute-start.5 = (bf16[80,448]{1,0:T(8,128)(2,1)S(1)}, bf16[80,448]{1,0:T(8,128)(2,1)S(1)}, u32[]{:S(2)}, u32[]{:S(2)}) collective-permute-start(bf16[80,448]{1,0:T(8,128)(2,1)S(1)} %get-tuple-element.31), channel_id=1, source_target_pairs={{0,3},{1,2},{4,7},{5,6},{3,0},{2,1},{7,4},{6,5},{8,11},{9,10},{12,... | collective-permute-start | bytes 215048 | tf_op jit(solution)/shard_map/ppermute | solution.py:28
  13.1 20.3 %collective-permute-start.6 = (bf16[80,448]{1,0:T(8,128)(2,1)S(1)}, bf16[80,448]{1,0:T(8,128)(2,1)S(1)}, u32[]{:S(2)}, u32[]{:S(2)}) collective-permute-start(bf16[80,448]{1,0:T(8,128)(2,1)S(1)} %get-tuple-element.32), channel_id=1, source_target_pairs={{2,5},{3,4},{5,2},{4,3},{10,13},{11,12},{13,10},{12,11},{18,21},{1... | collective-permute-start | bytes 215048 | tf_op jit(solution)/shard_map/ppermute | solution.py:28
  13.8 7.0 %copy-start = (bf16[316,56,56]{0,2,1:T(8,128)(2,1)S(1)}, bf16[316,56,56]{0,2,1:T(8,128)(2,1)}, u32[]{:S(2)}) copy-start(bf16[316,56,56]{0,2,1:T(8,128)(2,1)} %param.6) | copy-start | bytes 5945860
  13.9 19.6 %collective-permute-start.3 = (bf16[192,448]{1,0:T(8,128)(2,1)S(1)}, bf16[192,448]{1,0:T(8,128)(2,1)S(1)}, u32[]{:S(2)}, u32[]{:S(2)}) collective-permute-start(bf16[192,448]{1,0:T(8,128)(2,1)S(1)} %get-tuple-element.27), channel_id=1, source_target_pairs={{0,2},{4,6},{2,0},{6,4},{1,3},{5,7},{3,1},{7,5},{8,10},{12,14},{10... | collective-permute-start | bytes 516104 | tf_op jit(solution)/shard_map/ppermute | solution.py:28
  18.3 15.2 %collective-permute-start.4 = (bf16[192,448]{1,0:T(8,128)(2,1)S(1)}, bf16[192,448]{1,0:T(8,128)(2,1)S(1)}, u32[]{:S(2)}, u32[]{:S(2)}) collective-permute-start(bf16[192,448]{1,0:T(8,128)(2,1)S(1)} %get-tuple-element.28), channel_id=1, source_target_pairs={{2,4},{4,2},{3,5},{5,3},{10,12},{12,10},{11,13},{13,11},{18,20},{2... | collective-permute-start | bytes 516104 | tf_op jit(solution)/shard_map/ppermute | solution.py:28
  19.2 14.4 %collective-permute-start.2 = (bf16[384,448]{1,0:T(8,128)(2,1)S(1)}, bf16[384,448]{1,0:T(8,128)(2,1)S(1)}, u32[]{:S(2)}, u32[]{:S(2)}) collective-permute-start(bf16[384,448]{1,0:T(8,128)(2,1)S(1)} %get-tuple-element.29), channel_id=1, source_target_pairs={{0,1},{1,0},{2,3},{3,2},{4,5},{5,4},{6,7},{7,6},{8,9},{9,8},{10,11... | collective-permute-start | bytes 1032200 | tf_op jit(solution)/shard_map/ppermute | solution.py:28

commit v7 on v6

--- a/solution.py
+++ b/solution.py
@@ -74,11 +74,12 @@
         highs.append(rows[rows.shape[0] - 1 :])
 
     boxes = {}
+    lifted_rows = lift(base[...].reshape(-1, width))
     for y in range(size_y):
         for z in range(size_z):
-            rows = base[y, z]
-            boxes[y, z] = lift(rows)
-            ends(rows.astype(F32))
+            at = (y * size_z + z) * size_x
+            boxes[y, z] = lifted_rows[at : at + size_x]
+            ends(base[y, z].astype(F32))
 
     def grouped(boxes, y, z, rows):
         pieces = []
@@ -88,13 +89,18 @@
                     pieces.append(boxes[2 * y + v, 2 * z + w][u * rows : (u + 1) * rows])
         return jnp.concatenate(pieces, axis=1)
 
-    coarse = {}
+    coarse, groups = {}, []
     for y in range(size_y // 2):
         for z in range(size_z // 2):
             group = grouped(boxes, y, z, half)
             ends(group)
             middle[y, z] = group.astype(BF)
-            coarse[y, z] = lift(group.astype(BF))
+            groups.append(group.astype(BF))
+    lifted_rows = lift(jnp.concatenate(groups, axis=0))
+    for y in range(size_y // 2):
+        for z in range(size_z // 2):
+            at = (y * (size_z // 2) + z) * half
+            coarse[y, z] = lifted_rows[at : at + half]
     for y in range(size_y // 4):
         for z in range(size_z // 4):
             group = grouped(coarse, y, z, part)

time: 42.9 us -> 42.8 us (level)
  transfers between devices with their start and end apart: 7 -> 7, of which waited for: 1 -> 1; matrix products, arithmetic and copies ran while one was open for 2% -> 2% of each run, Pallas kernels for 29% -> 30%
where the time goes in v7:
time: 42.8 us; the launch traced here: 42.5 us
  Pallas kernels  22.2 us (52%)
  starting transfers between devices  14.9 us (35%)
  local copies, waits for them, and re-layouts  2.52 us (6%)
  other arithmetic  1.66 us (4%)
  between operations  0.64 us (1%)
  waiting for transfers between devices  0.56 us (1%)
    ppermute x7, starting transfers between devices, swapped(): return lax.ppermute(block, axis, both) if pairs else jnp.zeros_like(block)  14.9 us
    pallas_call x1, Pallas kernels, first_part(): pl.pallas_call(first_kernel, out_shape=(jax.ShapeDtypeStruct((3, 7, 7, 2...  12.6 us
    pallas_call x1, Pallas kernels, far(): pl.pallas_call(far_kernel, out_shape=jax.ShapeDtypeStruct((2 * half, size...  8.82 us
    reshape x1, local copies, waits for them, and re-layouts, shards(): base = densities.reshape(size_x // 4, 2, 2, size_y, size_z, width)  1.8 us
    concatenate x1, other arithmetic, shards(): weights = jnp.concatenate(weights, axis=0)  0.86 us
  transfers between devices with their start and end apart: 7, of which 1 were waited for; matrix products, arithmetic and copies ran while one was open for 2% of the time, Pallas kernels for 30%

profile of v7, /device:TPU:0, one launch (start us, length us, event | category | flops | bytes accessed | tf_op | source)
XLA Modules:
  0.0 42.5 jit_solution(12363937840252163986)
XLA Ops:
  0.0 1.8 %copy.54 = bf16[8,2,2,8,4,448]{5,0,1,2,4,3:T(8,128)(2,1)S(1)} copy(bf16[8,2,2,8,4,448]{5,4,3,2,1,0:T(4,128)(2,1)} %bitcast.95) | data formatting | bytes 1835008 | tf_op jit(solution)/shard_map/reshape | solution.py:555
  1.8 0.9 %fusion.2.weight.down = bf16[128,448]{1,0:T(8,128)(2,1)S(1)} fusion(bf16[56,448]{1,0:T(8,128)(2,1)} %param.7, bf16[56,448]{1,0:T(8,128)(2,1)} %bitcast.109), kind=kLoop, calls=%fused_computation.9 | loop fusion | flops 458752 | bytes 215040 | tf_op jit(solution)/shard_map/concatenate | solution.py:554
  2.7 0.8 %lift.1 = (bf16[4,2,16,448]{3,2,1,0:T(8,128)(2,1)S(1)}, bf16[2,1,16,448]{3,2,1,0:T(8,128)(2,1)S(1)}, bf16[48,448]{1,0:T(8,128)(2,1)S(1)}, bf16[48,448]{1,0:T(8,128)(2,1)S(1)}) custom-call(bf16[8,4,32,448]{3,2,1,0:T(8,128)(2,1)S(1)} %bitcast.87, bf16[128,448]{1,0:T(8,128)(2,1)S(1)} %fusion.2.weight.down), custom_call_target="tpu_custom_call" | custom-call | tf_op jit(solution)/shard_map/lift/pallas_call | solution.py:118
  3.5 0.7 %collective-permute-start.1 = (bf16[48,448]{1,0:T(8,128)(2,1)S(1)}, bf16[48,448]{1,0:T(8,128)(2,1)S(1)}, u32[]{:S(2)}, u32[]{:S(2)}) collective-permute-start(bf16[48,448]{1,0:T(8,128)(2,1)S(1)} %get-tuple-element.50), channel_id=1, source_target_pairs={{8,16},{16,8},{9,17},{17,9},{10,18},{18,10},{11,19},{19,11},{12,20... | collective-permute-start | bytes 129032 | tf_op jit(solution)/shard_map/ppermute | solution.py:28
  4.2 4.4 %collective-permute-start = (bf16[48,448]{1,0:T(8,128)(2,1)S(1)}, bf16[48,448]{1,0:T(8,128)(2,1)S(1)}, u32[]{:S(2)}, u32[]{:S(2)}) collective-permute-start(bf16[48,448]{1,0:T(8,128)(2,1)S(1)} %get-tuple-element.51), channel_id=1, source_target_pairs={{0,8},{16,24},{8,0},{24,16},{1,9},{17,25},{9,1},{25,17},{2,10},{18... | collective-permute-start | bytes 129032 | tf_op jit(solution)/shard_map/ppermute | solution.py:28
  8.8 0.1 add_convert_fusion.odd
  8.9 0.0 collective-permute-done.1
  8.9 0.5 %collective-permute-done = bf16[48,448]{1,0:T(8,128)(2,1)S(1)} collective-permute-done((bf16[48,448]{1,0:T(8,128)(2,1)S(1)}, bf16[48,448]{1,0:T(8,128)(2,1)S(1)}, u32[]{:S(2)}, u32[]{:S(2)}) %collective-permute-start) | collective-permute-done | bytes 43040 | tf_op jit(solution)/shard_map/ppermute | solution.py:28
  9.9 0.1 slice_maximum_fusion
  10.3 0.1 select_select_fusion.1
  10.4 2.6 %collective-permute-start.5 = (bf16[80,448]{1,0:T(8,128)(2,1)S(1)}, bf16[80,448]{1,0:T(8,128)(2,1)S(1)}, u32[]{:S(2)}, u32[]{:S(2)}) collective-permute-start(bf16[80,448]{1,0:T(8,128)(2,1)S(1)} %get-tuple-element.31), channel_id=1, source_target_pairs={{0,3},{1,2},{4,7},{5,6},{3,0},{2,1},{7,4},{6,5},{8,11},{9,10},{12,... | collective-permute-start | bytes 215048 | tf_op jit(solution)/shard_map/ppermute | solution.py:28
  13.0 0.7 %collective-permute-start.6 = (bf16[80,448]{1,0:T(8,128)(2,1)S(1)}, bf16[80,448]{1,0:T(8,128)(2,1)S(1)}, u32[]{:S(2)}, u32[]{:S(2)}) collective-permute-start(bf16[80,448]{1,0:T(8,128)(2,1)S(1)} %get-tuple-element.32), channel_id=1, source_target_pairs={{2,5},{3,4},{5,2},{4,3},{10,13},{11,12},{13,10},{12,11},{18,21},{1... | collective-permute-start | bytes 215048 | tf_op jit(solution)/shard_map/ppermute | solution.py:28
  13.7 0.0 copy-start
  13.7 0.1 broadcast_select_fusion.1
  13.8 4.4 %collective-permute-start.3 = (bf16[192,448]{1,0:T(8,128)(2,1)S(1)}, bf16[192,448]{1,0:T(8,128)(2,1)S(1)}, u32[]{:S(2)}, u32[]{:S(2)}) collective-permute-start(bf16[192,448]{1,0:T(8,128)(2,1)S(1)} %get-tuple-element.27), channel_id=1, source_target_pairs={{0,2},{4,6},{2,0},{6,4},{1,3},{5,7},{3,1},{7,5},{8,10},{12,14},{10... | collective-permute-start | bytes 516104 | tf_op jit(solution)/shard_map/ppermute | solution.py:28
  18.2 0.7 %collective-permute-start.4 = (bf16[192,448]{1,0:T(8,128)(2,1)S(1)}, bf16[192,448]{1,0:T(8,128)(2,1)S(1)}, u32[]{:S(2)}, u32[]{:S(2)}) collective-permute-start(bf16[192,448]{1,0:T(8,128)(2,1)S(1)} %get-tuple-element.28), channel_id=1, source_target_pairs={{2,4},{4,2},{3,5},{5,3},{10,12},{12,10},{11,13},{13,11},{18,20},{2... | collective-permute-start | bytes 516104 | tf_op jit(solution)/shard_map/ppermute | solution.py:28
  18.9 0.2 pad_select_fusion
  19.1 1.6 %collective-permute-start.2 = (bf16[384,448]{1,0:T(8,128)(2,1)S(1)}, bf16[384,448]{1,0:T(8,128)(2,1)S(1)}, u32[]{:S(2)}, u32[]{:S(2)}) collective-permute-start(bf16[384,448]{1,0:T(8,128)(2,1)S(1)} %get-tuple-element.29), channel_id=1, source_target_pairs={{0,1},{1,0},{2,3},{3,2},{4,5},{5,4},{6,7},{7,6},{8,9},{9,8},{10,11... | collective-permute-start | bytes 1032200 | tf_op jit(solution)/shard_map/ppermute | solution.py:28
  20.7 0.0 copy-done
  20.7 12.6 %first.1 = (bf16[3,7,7,112,112]{4,3,2,1,0:T(8,128)(2,1)S(1)}, f32[1024,512]{1,0:T(8,128)S(1)}) custom-call(bf16[56,56,316]{2,1,0:T(8,128)(2,1)S(1)} %bitcast.94, bf16[8,4,32,448]{3,2,1,0:T(8,128)(2,1)S(1)} %bitcast.91, bf16[48,448]{1,0:T(8,128)(2,1)S(1)} %get-tuple-element.49.below.below_x, bf16[48,448]{1,0:T(8,128)(2,1)S(1)} %get-tuple-element.48.above.above_x, ...), custom_call_target="tpu_custom_call" | custom-call | flops 20000000000 | bytes 10000000 | tf_op jit(solution)/shard_map/first/pallas_call | solution.py:310
  33.3 0.0 collective-permute-done.5
  33.3 0.0 collective-permute-done.6
  33.4 0.0 collective-permute-done.3
  33.4 0.0 collective-permute-done.4
  33.5 0.0 collective-permute-done.2
  33.5 0.1 stack.49.got_z
  33.5 8.8 %far.1 = f32[32,8,4,448]{3,2,1,0:T(4,128)} custom-call(s32[2]{0:T(128)S(1)} %add_convert_fusion.odd, f32[1024,512]{1,0:T(8,128)S(1)} %get-tuple-element.15.near, bf16[3,7,7,112,112]{4,3,2,1,0:T(8,128)(2,1)S(1)} %get-tuple-element.16.table, bf16[4,2,16,448]{3,2,1,0:T(8,128)(2,1)S(1)} %get-tuple-element.13.middle, ...), custom_call_target="tpu_custom_call" | custom-call | tf_op jit(solution)/shard_map/far/pallas_call | solution.py:530
  (58 shorter events, 1.0 us)
Async XLA Ops:
  3.5 5.4 %collective-permute-start.1 = (bf16[48,448]{1,0:T(8,128)(2,1)S(1)}, bf16[48,448]{1,0:T(8,128)(2,1)S(1)}, u32[]{:S(2)}, u32[]{:S(2)}) collective-permute-start(bf16[48,448]{1,0:T(8,128)(2,1)S(1)} %get-tuple-element.50), channel_id=1, source_target_pairs={{8,16},{16,8},{9,17},{17,9},{10,18},{18,10},{11,19},{19,11},{12,20... | collective-permute-start | bytes 129032 | tf_op jit(solution)/shard_map/ppermute | solution.py:28
  4.2 5.2 %collective-permute-start = (bf16[48,448]{1,0:T(8,128)(2,1)S(1)}, bf16[48,448]{1,0:T(8,128)(2,1)S(1)}, u32[]{:S(2)}, u32[]{:S(2)}) collective-permute-start(bf16[48,448]{1,0:T(8,128)(2,1)S(1)} %get-tuple-element.51), channel_id=1, source_target_pairs={{0,8},{16,24},{8,0},{24,16},{1,9},{17,25},{9,1},{25,17},{2,10},{18... | collective-permute-start | bytes 129032 | tf_op jit(solution)/shard_map/ppermute | solution.py:28
  10.4 22.9 %collective-permute-start.5 = (bf16[80,448]{1,0:T(8,128)(2,1)S(1)}, bf16[80,448]{1,0:T(8,128)(2,1)S(1)}, u32[]{:S(2)}, u32[]{:S(2)}) collective-permute-start(bf16[80,448]{1,0:T(8,128)(2,1)S(1)} %get-tuple-element.31), channel_id=1, source_target_pairs={{0,3},{1,2},{4,7},{5,6},{3,0},{2,1},{7,4},{6,5},{8,11},{9,10},{12,... | collective-permute-start | bytes 215048 | tf_op jit(solution)/shard_map/ppermute | solution.py:28
  13.0 20.3 %collective-permute-start.6 = (bf16[80,448]{1,0:T(8,128)(2,1)S(1)}, bf16[80,448]{1,0:T(8,128)(2,1)S(1)}, u32[]{:S(2)}, u32[]{:S(2)}) collective-permute-start(bf16[80,448]{1,0:T(8,128)(2,1)S(1)} %get-tuple-element.32), channel_id=1, source_target_pairs={{2,5},{3,4},{5,2},{4,3},{10,13},{11,12},{13,10},{12,11},{18,21},{1... | collective-permute-start | bytes 215048 | tf_op jit(solution)/shard_map/ppermute | solution.py:28
  13.7 7.0 %copy-start = (bf16[316,56,56]{0,2,1:T(8,128)(2,1)S(1)}, bf16[316,56,56]{0,2,1:T(8,128)(2,1)}, u32[]{:S(2)}) copy-start(bf16[316,56,56]{0,2,1:T(8,128)(2,1)} %param.6) | copy-start | bytes 5945860
  13.8 19.6 %collective-permute-start.3 = (bf16[192,448]{1,0:T(8,128)(2,1)S(1)}, bf16[192,448]{1,0:T(8,128)(2,1)S(1)}, u32[]{:S(2)}, u32[]{:S(2)}) collective-permute-start(bf16[192,448]{1,0:T(8,128)(2,1)S(1)} %get-tuple-element.27), channel_id=1, source_target_pairs={{0,2},{4,6},{2,0},{6,4},{1,3},{5,7},{3,1},{7,5},{8,10},{12,14},{10... | collective-permute-start | bytes 516104 | tf_op jit(solution)/shard_map/ppermute | solution.py:28
  18.2 15.2 %collective-permute-start.4 = (bf16[192,448]{1,0:T(8,128)(2,1)S(1)}, bf16[192,448]{1,0:T(8,128)(2,1)S(1)}, u32[]{:S(2)}, u32[]{:S(2)}) collective-permute-start(bf16[192,448]{1,0:T(8,128)(2,1)S(1)} %get-tuple-element.28), channel_id=1, source_target_pairs={{2,4},{4,2},{3,5},{5,3},{10,12},{12,10},{11,13},{13,11},{18,20},{2... | collective-permute-start | bytes 516104 | tf_op jit(solution)/shard_map/ppermute | solution.py:28
  19.1 14.4 %collective-permute-start.2 = (bf16[384,448]{1,0:T(8,128)(2,1)S(1)}, bf16[384,448]{1,0:T(8,128)(2,1)S(1)}, u32[]{:S(2)}, u32[]{:S(2)}) collective-permute-start(bf16[384,448]{1,0:T(8,128)(2,1)S(1)} %get-tuple-element.29), channel_id=1, source_target_pairs={{0,1},{1,0},{2,3},{3,2},{4,5},{5,4},{6,7},{7,6},{8,9},{9,8},{10,11... | collective-permute-start | bytes 1032200 | tf_op jit(solution)/shard_map/ppermute | solution.py:28
